TPU v7x, 32 devices: a whole 2x2x4 slice. The times are simulated.
32 devices in a mesh: section: 2 (over core), dp: 4 (over z), seq: 4 (over y, x).
Axes of the slice: x: 2, y: 2, z: 4, core: 2. Of those that a mesh axis runs over, the one named last changes fastest.
Arguments:
- inputs: bfloat16 [4, 4, 1024, 1280], P(None, 'dp', 'seq'), may hold values from -6 to 6
- lengths: int32 [4, 4], P(None, 'dp'), may hold values from 256 to 1024, as said below
- mlm_mask: int32 [4, 4, 1024], P(None, 'dp', 'seq'), may hold values 0 or 1
- true_types: int32 [4, 4, 1024], P(None, 'dp', 'seq'), may hold values from 0 to 29
- gain_in: bfloat16 [2, 1280], P('section'), may hold values from 0.25 to 1.75
- bias_in: bfloat16 [2, 1280], P('section'), may hold values from -3 to 3
- gain_mid: bfloat16 [2, 2, 640], P('section'), may hold values from 0.25 to 1.75
- bias_mid: bfloat16 [2, 2, 640], P('section'), may hold values from -3 to 3
- w_in: bfloat16 [2, 1280, 640], P('section'), may hold values from -0.15625 to 0.15625
- conv_w: bfloat16 [2, 5, 640, 640], P('section'), may hold values from -0.109375 to 0.109375
- w_out: bfloat16 [2, 640, 1280], P('section'), may hold values from -0.25 to 0.25
- decoder: bfloat16 [1280, 30], replicated, may hold values from -0.15625 to 0.15625
- cotangent: bfloat16 [4, 4, 1024, 1280], P(None, 'dp', 'seq'), may hold values from -6 to 6
Outputs:
- activations: bfloat16 [2, 4, 4, 1024, 1280], P('section', None, 'dp', 'seq')
- input_grads: bfloat16 [2, 4, 4, 1024, 1280], P('section', None, 'dp', 'seq')
- grad_gain_in: float32 [2, 1280], P('section')
- grad_bias_in: float32 [2, 1280], P('section')
- grad_gain_mid: float32 [2, 2, 640], P('section')
- grad_bias_mid: float32 [2, 2, 640], P('section')
- grad_w_in: float32 [2, 1280, 640], P('section')
- grad_conv_w: float32 [2, 5, 640, 640], P('section')
- grad_w_out: float32 [2, 640, 1280], P('section')
- counts: float32 [30], replicated
Inputs may be any that keep to these rules, and one draw needn't show every extreme that they name: `lengths`: in every column one of the 4 sequences, drawn from the seed, has the full length 1024.
All inputs are finite; a program needn't handle non-finite values. No bound on the sum of `mlm_mask` on one device may be relied on, other than what follows from the above.
Results may differ from a plain program's by a relative error of at most 0.011.
Values may be sent and summed in bfloat16 or wider, within the bound.
A program may use at most 128 MiB of HBM per device.

v0:
```python
import jax
import jax.numpy as jnp
from jax import lax
from jax.sharding import PartitionSpec as P

DILATION_ONE = 2
DILATION_SECOND = 128


EPS = 1e-05


def extended(shard, sides, width):
    for axis, dim in sides:
        count, length = (lax.axis_size(axis), shard.shape[dim])
        up = [(i, (i + 1) % count) for i in range(count - 1)]
        down = [(j, i) for i, j in up]
        last = lax.slice_in_dim(shard, length - width, length, axis=dim)
        first = lax.slice_in_dim(shard, 0, width, axis=dim)
        before = lax.ppermute(last, axis, up)
        after = lax.ppermute(first, axis, down)
        shard = jnp.concatenate([before, shard, after], axis=dim)
    return shard


def from_behind(shard, axis, by):
    count = lax.axis_size(axis)
    pairs = [(i, i + by) for i in range(count) if 0 <= i + by < count]
    return lax.ppermute(shard, axis, pairs)


def layer_norm(value_entries, gain, shift):
    middle_position = value_entries - jnp.mean(value_entries, axis=-1, keepdims=True)
    spread = jnp.mean(middle_position * middle_position, axis=-1, keepdims=True)
    return middle_position * lax.rsqrt(spread + EPS) * gain + shift


def front_part(value_entries, gain, shift):
    return jax.nn.gelu(layer_norm(value_entries, gain, shift))


def middle_part(value_entries, gain, shift, keep_flags):
    return jax.nn.gelu(layer_norm(value_entries, gain, shift)) * keep_flags


def row_products(left, right):
    return jnp.einsum("ti,tj->ij", left, right, preferred_element_type=jnp.float32)


def back_products(grad, weight):
    return jnp.einsum("tj,ij->ti", grad, weight, preferred_element_type=jnp.float32)


def pick(stacked, slot):
    return lax.dynamic_index_in_dim(stacked, slot, 0, keepdims=False)


def store(stacked, value, slot, valid):
    kept_value = jnp.where(valid, value, pick(stacked, slot))
    return lax.dynamic_update_index_in_dim(stacked, kept_value, slot, 0)


def body(
    inputs,
    lengths,
    mlm_mask,
    true_types,
    gain_in,
    bias_in,
    gain_mid,
    bias_mid,
    w_in,
    conv_w,
    w_out,
    decoder,
    cotangent,
):
    section_number = lax.axis_index("section")
    on_last = section_number == 1
    micro = inputs.shape[0]
    seg_rows = inputs.shape[2]
    width = inputs.shape[3]
    hidden_width = w_in.shape[2]
    taps = conv_w.shape[1]
    middle_position = taps // 2
    classes = decoder.shape[1]
    receptive_reach = middle_position * DILATION_SECOND
    dilation_rate = jnp.where(section_number == 0, DILATION_ONE, DILATION_SECOND).astype(jnp.int32)
    offsets = [receptive_reach + (tap - middle_position) * dilation_rate for tap in range(taps)]
    gain_first = gain_in[0].astype(jnp.float32)
    shift_first = bias_in[0].astype(jnp.float32)
    gains_mid = gain_mid[0].astype(jnp.float32)
    shifts_mid = bias_mid[0].astype(jnp.float32)
    weight_first = w_in[0]
    kernel = conv_w[0]
    weight_last = w_out[0]
    positions = lax.axis_index("seq") * seg_rows + jnp.arange(seg_rows, dtype=jnp.int32)
    keeps = (positions[None, :] < lengths).astype(jnp.float32)
    own_inputs = inputs[:, 0]
    own_cot = cotangent[:, 0]
    own_mask = mlm_mask[:, 0].astype(jnp.float32)
    own_types = true_types[:, 0]
    labels = jnp.arange(classes, dtype=jnp.int32)

    def forward_parts(layer_in, keep_flags):
        first = front_part(layer_in.astype(jnp.float32), gain_first, shift_first).astype(
            jnp.bfloat16
        )
        hidden = jnp.dot(first, weight_first, preferred_element_type=jnp.float32)
        second = middle_part(hidden, gains_mid[0], shifts_mid[0], keep_flags).astype(jnp.bfloat16)
        padded = extended(second, (("seq", 0),), receptive_reach)
        mixed = jnp.zeros((seg_rows, hidden_width), jnp.float32)
        for tap in range(taps):
            window = lax.dynamic_slice_in_dim(padded, offsets[tap], seg_rows, 0)
            mixed = mixed + jnp.dot(window, kernel[tap], preferred_element_type=jnp.float32)
        third = front_part(mixed, gains_mid[1], shifts_mid[1]).astype(jnp.bfloat16)
        branch = jnp.dot(third, weight_last, preferred_element_type=jnp.float32)
        return (first, hidden, padded, mixed, third, branch)

    def forward_tick(tick, carry):
        incoming, results, kept_in, counts = carry
        index = tick - section_number
        valid = (index >= 0) & (index < micro)
        slot = jnp.clip(index, 0, micro - 1)
        layer_in = jnp.where(on_last, incoming, pick(own_inputs, slot))
        keep_flags = pick(keeps, slot)[:, None]
        branch = forward_parts(layer_in, keep_flags)[-1]
        result = (layer_in.astype(jnp.float32) + branch).astype(jnp.bfloat16)
        outgoing = from_behind(result, "section", 1)
        results = store(results, result, slot, valid)
        kept_in = store(kept_in, layer_in, slot, valid)
        probs = jax.nn.softmax(
            jnp.dot(result, decoder, preferred_element_type=jnp.float32), axis=-1
        )
        onehot = (pick(own_types, slot)[:, None] == labels[None, :]).astype(jnp.float32)
        chance = jnp.sum(probs * onehot, axis=-1)
        weight = (
            chance * pick(own_mask, slot) * keep_flags[:, 0] * (valid & on_last).astype(jnp.float32)
        )
        counts = counts + jnp.sum(onehot * weight[:, None], axis=0)
        return (outgoing, results, kept_in, counts)

    blank = jnp.zeros((seg_rows, width), jnp.bfloat16)
    stacked_blank = jnp.zeros((micro, seg_rows, width), jnp.bfloat16)
    start = (blank, stacked_blank, stacked_blank, jnp.zeros((classes,), jnp.float32))
    _, results, kept_in, counts = lax.fori_loop(0, micro + 1, forward_tick, start)

    def backward_tick(tick, carry):
        incoming, grads_in, grads = carry
        index = micro - 1 - tick + (1 - section_number)
        valid = (index >= 0) & (index < micro)
        slot = jnp.clip(index, 0, micro - 1)
        out_grad = jnp.where(on_last, pick(own_cot, slot), incoming)
        layer_in = pick(kept_in, slot)
        keep_flags = pick(keeps, slot)[:, None]
        first, hidden, padded, mixed, third, branch = forward_parts(layer_in, keep_flags)
        grad_last = row_products(third, out_grad)
        grad_third = back_products(out_grad, weight_last)
        _, third_back = jax.vjp(front_part, mixed, gains_mid[1], shifts_mid[1])
        grad_mixed, grad_gain_third, grad_shift_third = third_back(grad_third)
        grad_mixed = grad_mixed.astype(jnp.bfloat16)
        grad_padded = extended(grad_mixed, (("seq", 0),), receptive_reach)
        grad_second = jnp.zeros((seg_rows, hidden_width), jnp.float32)
        kernel_terms = []
        for tap in range(taps):
            window = lax.dynamic_slice_in_dim(padded, offsets[tap], seg_rows, 0)
            kernel_terms.append(row_products(window, grad_mixed))
            back_window = lax.dynamic_slice_in_dim(
                grad_padded, 2 * receptive_reach - offsets[tap], seg_rows, 0
            )
            grad_second = grad_second + back_products(back_window, kernel[tap])
        grad_kernel = jnp.stack(kernel_terms)

        def second_piece(value_entries, gain, shift):
            return middle_part(value_entries, gain, shift, keep_flags)

        _, second_back = jax.vjp(second_piece, hidden, gains_mid[0], shifts_mid[0])
        grad_hidden, grad_gain_second, grad_shift_second = second_back(grad_second)
        grad_hidden = grad_hidden.astype(jnp.bfloat16)
        grad_first_weight = row_products(first, grad_hidden)
        grad_first = back_products(grad_hidden, weight_first)
        _, first_back = jax.vjp(front_part, layer_in.astype(jnp.float32), gain_first, shift_first)
        grad_values, grad_gain_first, grad_shift_first = first_back(grad_first)
        grad_input = (out_grad.astype(jnp.float32) + grad_values).astype(jnp.bfloat16)
        outgoing = from_behind(grad_input, "section", -1)
        grads_in = store(grads_in, grad_input, slot, valid)
        flag = valid.astype(jnp.float32)
        terms = (
            grad_gain_first,
            grad_shift_first,
            jnp.stack([grad_gain_second, grad_gain_third]),
            jnp.stack([grad_shift_second, grad_shift_third]),
            grad_first_weight,
            grad_kernel,
            grad_last,
        )
        grads = tuple((acc + flag * term for acc, term in zip(grads, terms)))
        return (outgoing, grads_in, grads)

    zero_grads = (
        jnp.zeros((width,), jnp.float32),
        jnp.zeros((width,), jnp.float32),
        jnp.zeros((2, hidden_width), jnp.float32),
        jnp.zeros((2, hidden_width), jnp.float32),
        jnp.zeros((width, hidden_width), jnp.float32),
        jnp.zeros((taps, hidden_width, hidden_width), jnp.float32),
        jnp.zeros((hidden_width, width), jnp.float32),
    )
    _, grads_in, grads = lax.fori_loop(
        0, micro + 1, backward_tick, (blank, stacked_blank, zero_grads)
    )
    (
        sum_gain_first,
        sum_shift_first,
        sum_gain_mid,
        sum_shift_mid,
        sum_first,
        sum_kernel,
        sum_last,
    ) = grads
    summed = lax.psum(
        (
            sum_gain_first,
            sum_shift_first,
            sum_gain_mid,
            sum_shift_mid,
            sum_first,
            sum_kernel,
            sum_last,
        ),
        ("dp", "seq"),
    )
    total_counts = lax.psum(counts, ("section", "dp", "seq"))
    activations = results[None, :, None]
    input_grads = grads_in[None, :, None]
    return (
        activations,
        input_grads,
        summed[0][None],
        summed[1][None],
        summed[2][None],
        summed[3][None],
        summed[4][None],
        summed[5][None],
        summed[6][None],
        total_counts,
    )


def solution(mesh):
    return jax.shard_map(
        body,
        mesh=mesh,
        in_specs=(
            P(None, "dp", "seq", None),
            P(None, "dp"),
            P(None, "dp", "seq"),
            P(None, "dp", "seq"),
            P("section", None),
            P("section", None),
            P("section", None, None),
            P("section", None, None),
            P("section", None, None),
            P("section", None, None, None),
            P("section", None, None),
            P(),
            P(None, "dp", "seq", None),
        ),
        out_specs=(
            P("section", None, "dp", "seq", None),
            P("section", None, "dp", "seq", None),
            P("section", None),
            P("section", None),
            P("section", None, None),
            P("section", None, None),
            P("section", None, None),
            P("section", None, None, None),
            P("section", None, None),
            P(),
        ),
        check_vma=False,
    )
```

profile of v0, /device:TPU:0, one launch (start us, length us, event | category | flops | bytes accessed | tf_op | source)
XLA Modules:
  0.0 975.3 jit_solution(10392598391493733717)
XLA Ops:
  12.9 183.3 %while.55 = (s32[]{:T(128)}, bf16[256,1280]{1,0:T(8,128)(2,1)}, bf16[4,256,1280]{2,1,0:T(8,128)(2,1)}, bf16[4,256,1280]{2,1,0:T(8,128)(2,1)S(1)}, f32[30]{0:T(12...) while((s32[]{:T(128)}, bf16[256,1280]{1,0:T(8,128)(2,1)}, ...), condition=%wide.region_11.12_spmd.clone, body=%wide.region_0.11_spmd.clone.sunk | while | flops 1925041408 | bytes 71857736 | solution.py:146
  13.8 2.7 bitcast_dynamic-update-slice_fusion.16
  19.6 5.6 collective-permute-start.1
  28.3 3.5 collective-permute-done.1
  31.9 8.9 collective-permute-done
  52.8 2.7 bitcast_dynamic-update-slice_fusion.16
  58.6 4.1 collective-permute-start.1
  65.9 4.1 collective-permute-done.1
  70.0 7.8 collective-permute-done
  90.4 2.7 bitcast_dynamic-update-slice_fusion.16
  96.1 2.2 collective-permute-start.1
  101.5 4.2 collective-permute-done.1
  105.7 7.7 collective-permute-done
  126.0 2.7 bitcast_dynamic-update-slice_fusion.16
  131.7 2.2 collective-permute-start.1
  137.1 4.2 collective-permute-done.1
  141.3 7.7 collective-permute-done
  161.6 2.7 bitcast_dynamic-update-slice_fusion.16
  167.3 2.2 collective-permute-start.1
  172.7 4.2 collective-permute-done.1
  176.9 7.7 collective-permute-done
  198.8 341.1 %while.56 = (s32[]{:T(128)}, bf16[256,1280]{1,0:T(8,128)(2,1)}, bf16[4,256,1280]{2,1,0:T(8,128)(2,1)}, f32[1280]{0:T(1024)S(1)}, f32[1280]{0:T(1024)S(1)}, /*ind...) while((s32[]{:T(128)}, bf16[256,1280]{1,0:T(8,128)(2,1)}, ...), condition=%wide.region_31.32_spmd.clone, body=%wide.region_12.31_spmd.clone.sunk | while | flops 5305403392 | bytes 234888640 | solution.py:209
  200.4 2.8 fusion.368
  212.9 7.6 collective-permute-done.3
  231.4 3.1 copy-done.2
  234.6 7.5 select_add_fusion.6
  242.0 2.6 fusion.386
  249.2 3.0 fusion.382
  256.0 2.2 fusion.385
  261.7 2.8 fusion.368
  265.2 4.6 collective-permute-start.4
  277.6 8.4 collective-permute-done.3
  297.1 3.1 copy-done.2
  300.3 9.8 %select_add_fusion.6 = f32[5,640,640]{2,1,0:T(8,128)} fusion(f32[5,640,640]{2,1,0:T(8,128)} %get-tuple-element.2212, f32[5,640,640]{2,1,0:T(8,128)} %copy-done.2, f32[]{:T(128)S(6)} %convert_element_type.403, pred[]{:T(512)S(6)} %compare.7), kind=kLoop, calls=%fused_computation.121.clone.1 | loop fusion | flops 6144000 | bytes 24576004 | tf_op jit(solution)/shard_map/while/body/eval_jaxpr/add | solution.py:197
  310.1 4.5 fusion.386
  319.2 3.0 fusion.382
  331.7 2.8 fusion.368
  335.1 4.6 collective-permute-start.4
  347.6 8.4 collective-permute-done.3
  367.1 3.1 copy-done.2
  370.2 9.8 %select_add_fusion.6 = f32[5,640,640]{2,1,0:T(8,128)} fusion(f32[5,640,640]{2,1,0:T(8,128)} %get-tuple-element.2212, f32[5,640,640]{2,1,0:T(8,128)} %copy-done.2, f32[]{:T(128)S(6)} %convert_element_type.403, pred[]{:T(512)S(6)} %compare.7), kind=kLoop, calls=%fused_computation.121.clone.1 | loop fusion | flops 6144000 | bytes 24576004 | tf_op jit(solution)/shard_map/while/body/eval_jaxpr/add | solution.py:197
  380.0 4.5 fusion.386
  389.1 3.0 fusion.382
  395.9 2.2 fusion.385
  401.6 2.8 fusion.368
  405.1 4.6 collective-permute-start.4
  417.5 8.4 collective-permute-done.3
  437.1 3.1 copy-done.2
  440.2 9.8 %select_add_fusion.6 = f32[5,640,640]{2,1,0:T(8,128)} fusion(f32[5,640,640]{2,1,0:T(8,128)} %get-tuple-element.2212, f32[5,640,640]{2,1,0:T(8,128)} %copy-done.2, f32[]{:T(128)S(6)} %convert_element_type.403, pred[]{:T(512)S(6)} %compare.7), kind=kLoop, calls=%fused_computation.121.clone.1 | loop fusion | flops 6144000 | bytes 24576004 | tf_op jit(solution)/shard_map/while/body/eval_jaxpr/add | solution.py:197
  450.0 4.5 fusion.386
  459.1 3.0 fusion.382
  465.9 2.2 fusion.385
  471.6 2.8 fusion.368
  475.0 4.6 collective-permute-start.4
  487.5 8.4 collective-permute-done.3
  507.0 3.1 copy-done.2
  510.1 9.8 %select_add_fusion.6 = f32[5,640,640]{2,1,0:T(8,128)} fusion(f32[5,640,640]{2,1,0:T(8,128)} %get-tuple-element.2212, f32[5,640,640]{2,1,0:T(8,128)} %copy-done.2, f32[]{:T(128)S(6)} %convert_element_type.403, pred[]{:T(512)S(6)} %compare.7), kind=kLoop, calls=%fused_computation.121.clone.1 | loop fusion | flops 6144000 | bytes 24576004 | tf_op jit(solution)/shard_map/while/body/eval_jaxpr/add | solution.py:197
  519.9 4.5 fusion.386
  529.0 3.0 fusion.382
  540.6 45.8 %psum.63 = f32[30]{0:T(128)} all-reduce(f32[30]{0:T(128)S(1)} %copy-done.15), channel_id=1, replica_groups=mesh['section'=2,'dp'=4,'seq'=4] {'section','dp','seq'}, use_global_device_ids=true, to_apply=%region_39.40 | all-reduce | flops 30 | bytes 240 | tf_op jit(solution)/shard_map/psum | solution.py:233
  586.4 78.5 %all-reduce = (f32[1,1280]{1,0:T(1,128)}, f32[1,1280]{1,0:T(1,128)}, f32[1,2,640]{2,1,0:T(2,128)}, f32[1,2,640]{2,1,0:T(2,128)}) all-reduce(f32[1,1280]{1,0:T(1,128)S(1)} %broadcast_in_dim.223, f32[1,1280]{1,0:T(1,128)S(1)} %broadcast_in_dim.224, ...), channel_id=1, replica_groups=mesh['section'=2,'dp'=4,'seq'=4] {'dp','seq'}, use_global_device_ids=true, to_apply=%region_32.33 | all-reduce | flops 5120 | bytes 40960 | tf_op jit(solution)/shard_map/psum | solution.py:221
  665.0 290.6 %all-reduce.4.cloned.1.call-done = (f32[1,1280,640]{2,1,0:T(8,128)}, f32[1,5,640,640]{3,2,1,0:T(8,128)}, f32[1,640,1280]{2,1,0:T(8,128)}) async-done(((f32[1,1280,640]{2,1,0:T(8,128)}, f32[1,5,640,640]{3,2,1,0:T(8,128)}, f32[1,640,1280]{2,1,0:T(8,128)}), (f32[1,1280,640]{2,1,0:T(8,128)}, f32[1,5,640,640]{3,2,1,0:T(8,128)}, f32[1,640,1280]{2,1,0:T(8,128)})) %all-reduce.4.cloned.1.call-update) | async-done | bytes 14745616 | tf_op jit(solution)/shard_map/psum | solution.py:221
  955.6 3.8 copy.84
  959.4 7.3 copy.85
  (649 shorter events, 264.9 us)
Async XLA Ops:
  7.2 948.4 %all-reduce.4.cloned.1.call-start = ((), (), s32[]{:S(2)}) async-start(), calls=%async_computation | async-start | bytes 29491200 | tf_op jit(solution)/shard_map/psum | solution.py:221
  13.8 3.2 copy-start.16
  19.6 12.3 %collective-permute-start.1 = (bf16[256,640]{1,0:T(8,128)(2,1)}, bf16[256,640]{1,0:T(8,128)(2,1)}, u32[]{:S(2)}, u32[]{:S(2)}) collective-permute-start(bf16[256,640]{1,0:T(8,128)(2,1)} %fusion.323), channel_id=1, source_target_pairs={{0,1},{1,2},{2,3},{4,5},{5,6},{6,7},{8,9},{9,10},{10,11},{12,13},{... | collective-permute-start | bytes 983048 | tf_op jit(solution)/shard_map/while/body/eval_jaxpr/ppermute | solution.py:20
  25.1 15.7 %collective-permute-start = (bf16[256,640]{1,0:T(8,128)(2,1)}, bf16[256,640]{1,0:T(8,128)(2,1)}, u32[]{:S(2)}, u32[]{:S(2)}) collective-permute-start(bf16[256,640]{1,0:T(8,128)(2,1)} %fusion.323), channel_id=1, source_target_pairs={{1,0},{2,1},{3,2},{5,4},{6,5},{7,6},{9,8},{10,9},{11,10},{13,12},{... | collective-permute-start | bytes 983048 | tf_op jit(solution)/shard_map/while/body/eval_jaxpr/ppermute | solution.py:21
  26.5 17.2 %copy-start = (bf16[5,640,640]{2,1,0:T(8,128)(2,1)S(1)}, bf16[5,640,640]{2,1,0:T(8,128)(2,1)}, u32[]{:S(2)}) copy-start(bf16[5,640,640]{2,1,0:T(8,128)(2,1)} %get-tuple-element.2158) | copy-start | bytes 12288004 | tf_op jit(solution)/shard_map/while
  48.1 3.0 collective-permute-start.2
  52.8 3.2 copy-start.16
  58.6 11.4 %collective-permute-start.1 = (bf16[256,640]{1,0:T(8,128)(2,1)}, bf16[256,640]{1,0:T(8,128)(2,1)}, u32[]{:S(2)}, u32[]{:S(2)}) collective-permute-start(bf16[256,640]{1,0:T(8,128)(2,1)} %fusion.323), channel_id=1, source_target_pairs={{0,1},{1,2},{2,3},{4,5},{5,6},{6,7},{8,9},{9,10},{10,11},{12,13},{... | collective-permute-start | bytes 983048 | tf_op jit(solution)/shard_map/while/body/eval_jaxpr/ppermute | solution.py:20
  62.7 15.1 %collective-permute-start = (bf16[256,640]{1,0:T(8,128)(2,1)}, bf16[256,640]{1,0:T(8,128)(2,1)}, u32[]{:S(2)}, u32[]{:S(2)}) collective-permute-start(bf16[256,640]{1,0:T(8,128)(2,1)} %fusion.323), channel_id=1, source_target_pairs={{1,0},{2,1},{3,2},{5,4},{6,5},{7,6},{9,8},{10,9},{11,10},{13,12},{... | collective-permute-start | bytes 983048 | tf_op jit(solution)/shard_map/while/body/eval_jaxpr/ppermute | solution.py:21
  64.0 16.6 %copy-start = (bf16[5,640,640]{2,1,0:T(8,128)(2,1)S(1)}, bf16[5,640,640]{2,1,0:T(8,128)(2,1)}, u32[]{:S(2)}) copy-start(bf16[5,640,640]{2,1,0:T(8,128)(2,1)} %get-tuple-element.2158) | copy-start | bytes 12288004 | tf_op jit(solution)/shard_map/while
  85.1 3.6 collective-permute-start.2
  90.4 3.2 copy-start.16
  96.1 9.6 collective-permute-start.1
  98.3 15.0 %collective-permute-start = (bf16[256,640]{1,0:T(8,128)(2,1)}, bf16[256,640]{1,0:T(8,128)(2,1)}, u32[]{:S(2)}, u32[]{:S(2)}) collective-permute-start(bf16[256,640]{1,0:T(8,128)(2,1)} %fusion.323), channel_id=1, source_target_pairs={{1,0},{2,1},{3,2},{5,4},{6,5},{7,6},{9,8},{10,9},{11,10},{13,12},{... | collective-permute-start | bytes 983048 | tf_op jit(solution)/shard_map/while/body/eval_jaxpr/ppermute | solution.py:21
  99.7 16.6 %copy-start = (bf16[5,640,640]{2,1,0:T(8,128)(2,1)S(1)}, bf16[5,640,640]{2,1,0:T(8,128)(2,1)}, u32[]{:S(2)}) copy-start(bf16[5,640,640]{2,1,0:T(8,128)(2,1)} %get-tuple-element.2158) | copy-start | bytes 12288004 | tf_op jit(solution)/shard_map/while
  120.7 3.6 collective-permute-start.2
  126.0 3.2 copy-start.16
  131.7 9.6 collective-permute-start.1
  133.9 15.0 %collective-permute-start = (bf16[256,640]{1,0:T(8,128)(2,1)}, bf16[256,640]{1,0:T(8,128)(2,1)}, u32[]{:S(2)}, u32[]{:S(2)}) collective-permute-start(bf16[256,640]{1,0:T(8,128)(2,1)} %fusion.323), channel_id=1, source_target_pairs={{1,0},{2,1},{3,2},{5,4},{6,5},{7,6},{9,8},{10,9},{11,10},{13,12},{... | collective-permute-start | bytes 983048 | tf_op jit(solution)/shard_map/while/body/eval_jaxpr/ppermute | solution.py:21
  135.2 16.6 %copy-start = (bf16[5,640,640]{2,1,0:T(8,128)(2,1)S(1)}, bf16[5,640,640]{2,1,0:T(8,128)(2,1)}, u32[]{:S(2)}) copy-start(bf16[5,640,640]{2,1,0:T(8,128)(2,1)} %get-tuple-element.2158) | copy-start | bytes 12288004 | tf_op jit(solution)/shard_map/while
  156.3 3.6 collective-permute-start.2
  161.6 3.2 copy-start.16
  167.3 9.6 collective-permute-start.1
  169.5 15.0 %collective-permute-start = (bf16[256,640]{1,0:T(8,128)(2,1)}, bf16[256,640]{1,0:T(8,128)(2,1)}, u32[]{:S(2)}, u32[]{:S(2)}) collective-permute-start(bf16[256,640]{1,0:T(8,128)(2,1)} %fusion.323), channel_id=1, source_target_pairs={{1,0},{2,1},{3,2},{5,4},{6,5},{7,6},{9,8},{10,9},{11,10},{13,12},{... | collective-permute-start | bytes 983048 | tf_op jit(solution)/shard_map/while/body/eval_jaxpr/ppermute | solution.py:21
  170.8 16.6 %copy-start = (bf16[5,640,640]{2,1,0:T(8,128)(2,1)S(1)}, bf16[5,640,640]{2,1,0:T(8,128)(2,1)}, u32[]{:S(2)}) copy-start(bf16[5,640,640]{2,1,0:T(8,128)(2,1)} %get-tuple-element.2158) | copy-start | bytes 12288004 | tf_op jit(solution)/shard_map/while
  191.8 3.6 collective-permute-start.2
  203.2 3.5 copy-start.6
  203.8 9.1 collective-permute-start.4
  205.3 15.2 %collective-permute-start.3 = (bf16[256,640]{1,0:T(8,128)(2,1)S(1)}, bf16[256,640]{1,0:T(8,128)(2,1)S(1)}, u32[]{:S(2)}, u32[]{:S(2)}) collective-permute-start(bf16[256,640]{1,0:T(8,128)(2,1)S(1)} %multiply_convert_fusion.6), channel_id=1, source_target_pairs={{1,0},{2,1},{3,2},{5,4},{6,5},{7,6},{9,8},{10,9},{11,10},{13,12},{... | collective-permute-start | bytes 983048 | tf_op jit(solution)/shard_map/while/body/eval_jaxpr/ppermute | solution.py:21
  209.8 12.5 %copy-start.1 = (bf16[5,640,640]{2,1,0:T(8,128)(2,1)S(1)}, bf16[5,640,640]{2,1,0:T(8,128)(2,1)}, u32[]{:S(2)}) copy-start(bf16[5,640,640]{2,1,0:T(8,128)(2,1)} %get-tuple-element.2260) | copy-start | bytes 12288004 | tf_op jit(solution)/shard_map/while
  226.2 18.9 %collective-permute-start.6 = (bf16[256,640]{1,0:T(8,128)(2,1)S(1)}, bf16[256,640]{1,0:T(8,128)(2,1)S(1)}, u32[]{:S(2)}, u32[]{:S(2)}) collective-permute-start(bf16[256,640]{1,0:T(8,128)(2,1)S(1)} %add_convert_fusion.11), channel_id=1, source_target_pairs={{0,1},{1,2},{2,3},{4,5},{5,6},{6,7},{8,9},{9,10},{10,11},{12,13},{... | collective-permute-start | bytes 983048 | tf_op jit(solution)/shard_map/while/body/eval_jaxpr/ppermute | solution.py:20
  227.7 17.4 %collective-permute-start.5 = (bf16[256,640]{1,0:T(8,128)(2,1)S(1)}, bf16[256,640]{1,0:T(8,128)(2,1)S(1)}, u32[]{:S(2)}, u32[]{:S(2)}) collective-permute-start(bf16[256,640]{1,0:T(8,128)(2,1)S(1)} %add_convert_fusion.11), channel_id=1, source_target_pairs={{1,0},{2,1},{3,2},{5,4},{6,5},{7,6},{9,8},{10,9},{11,10},{13,12},{... | collective-permute-start | bytes 983048 | tf_op jit(solution)/shard_map/while/body/eval_jaxpr/ppermute | solution.py:21
  254.6 4.1 collective-permute-start.7
  264.5 6.6 copy-start.6
  265.2 12.4 %collective-permute-start.4 = (bf16[256,640]{1,0:T(8,128)(2,1)S(1)}, bf16[256,640]{1,0:T(8,128)(2,1)S(1)}, u32[]{:S(2)}, u32[]{:S(2)}) collective-permute-start(bf16[256,640]{1,0:T(8,128)(2,1)S(1)} %multiply_convert_fusion.6), channel_id=1, source_target_pairs={{0,1},{1,2},{2,3},{4,5},{5,6},{6,7},{8,9},{9,10},{10,11},{12,13},{... | collective-permute-start | bytes 983048 | tf_op jit(solution)/shard_map/while/body/eval_jaxpr/ppermute | solution.py:20
  269.7 16.2 %collective-permute-start.3 = (bf16[256,640]{1,0:T(8,128)(2,1)S(1)}, bf16[256,640]{1,0:T(8,128)(2,1)S(1)}, u32[]{:S(2)}, u32[]{:S(2)}) collective-permute-start(bf16[256,640]{1,0:T(8,128)(2,1)S(1)} %multiply_convert_fusion.6), channel_id=1, source_target_pairs={{1,0},{2,1},{3,2},{5,4},{6,5},{7,6},{9,8},{10,9},{11,10},{13,12},{... | collective-permute-start | bytes 983048 | tf_op jit(solution)/shard_map/while/body/eval_jaxpr/ppermute | solution.py:21
  274.2 13.5 %copy-start.1 = (bf16[5,640,640]{2,1,0:T(8,128)(2,1)S(1)}, bf16[5,640,640]{2,1,0:T(8,128)(2,1)}, u32[]{:S(2)}) copy-start(bf16[5,640,640]{2,1,0:T(8,128)(2,1)} %get-tuple-element.2260) | copy-start | bytes 12288004 | tf_op jit(solution)/shard_map/while
  291.7 23.4 %collective-permute-start.6 = (bf16[256,640]{1,0:T(8,128)(2,1)S(1)}, bf16[256,640]{1,0:T(8,128)(2,1)S(1)}, u32[]{:S(2)}, u32[]{:S(2)}) collective-permute-start(bf16[256,640]{1,0:T(8,128)(2,1)S(1)} %add_convert_fusion.11), channel_id=1, source_target_pairs={{0,1},{1,2},{2,3},{4,5},{5,6},{6,7},{8,9},{9,10},{10,11},{12,13},{... | collective-permute-start | bytes 983048 | tf_op jit(solution)/shard_map/while/body/eval_jaxpr/ppermute | solution.py:20
  293.4 21.7 %collective-permute-start.5 = (bf16[256,640]{1,0:T(8,128)(2,1)S(1)}, bf16[256,640]{1,0:T(8,128)(2,1)S(1)}, u32[]{:S(2)}, u32[]{:S(2)}) collective-permute-start(bf16[256,640]{1,0:T(8,128)(2,1)S(1)} %add_convert_fusion.11), channel_id=1, source_target_pairs={{1,0},{2,1},{3,2},{5,4},{6,5},{7,6},{9,8},{10,9},{11,10},{13,12},{... | collective-permute-start | bytes 983048 | tf_op jit(solution)/shard_map/while/body/eval_jaxpr/ppermute | solution.py:21
  324.5 4.1 collective-permute-start.7
  334.4 6.6 copy-start.6
  335.1 12.4 %collective-permute-start.4 = (bf16[256,640]{1,0:T(8,128)(2,1)S(1)}, bf16[256,640]{1,0:T(8,128)(2,1)S(1)}, u32[]{:S(2)}, u32[]{:S(2)}) collective-permute-start(bf16[256,640]{1,0:T(8,128)(2,1)S(1)} %multiply_convert_fusion.6), channel_id=1, source_target_pairs={{0,1},{1,2},{2,3},{4,5},{5,6},{6,7},{8,9},{9,10},{10,11},{12,13},{... | collective-permute-start | bytes 983048 | tf_op jit(solution)/shard_map/while/body/eval_jaxpr/ppermute | solution.py:20
  339.7 16.2 %collective-permute-start.3 = (bf16[256,640]{1,0:T(8,128)(2,1)S(1)}, bf16[256,640]{1,0:T(8,128)(2,1)S(1)}, u32[]{:S(2)}, u32[]{:S(2)}) collective-permute-start(bf16[256,640]{1,0:T(8,128)(2,1)S(1)} %multiply_convert_fusion.6), channel_id=1, source_target_pairs={{1,0},{2,1},{3,2},{5,4},{6,5},{7,6},{9,8},{10,9},{11,10},{13,12},{... | collective-permute-start | bytes 983048 | tf_op jit(solution)/shard_map/while/body/eval_jaxpr/ppermute | solution.py:21
  344.2 13.5 %copy-start.1 = (bf16[5,640,640]{2,1,0:T(8,128)(2,1)S(1)}, bf16[5,640,640]{2,1,0:T(8,128)(2,1)}, u32[]{:S(2)}) copy-start(bf16[5,640,640]{2,1,0:T(8,128)(2,1)} %get-tuple-element.2260) | copy-start | bytes 12288004 | tf_op jit(solution)/shard_map/while
  361.6 23.4 %collective-permute-start.6 = (bf16[256,640]{1,0:T(8,128)(2,1)S(1)}, bf16[256,640]{1,0:T(8,128)(2,1)S(1)}, u32[]{:S(2)}, u32[]{:S(2)}) collective-permute-start(bf16[256,640]{1,0:T(8,128)(2,1)S(1)} %add_convert_fusion.11), channel_id=1, source_target_pairs={{0,1},{1,2},{2,3},{4,5},{5,6},{6,7},{8,9},{9,10},{10,11},{12,13},{... | collective-permute-start | bytes 983048 | tf_op jit(solution)/shard_map/while/body/eval_jaxpr/ppermute | solution.py:20
  363.4 21.7 %collective-permute-start.5 = (bf16[256,640]{1,0:T(8,128)(2,1)S(1)}, bf16[256,640]{1,0:T(8,128)(2,1)S(1)}, u32[]{:S(2)}, u32[]{:S(2)}) collective-permute-start(bf16[256,640]{1,0:T(8,128)(2,1)S(1)} %add_convert_fusion.11), channel_id=1, source_target_pairs={{1,0},{2,1},{3,2},{5,4},{6,5},{7,6},{9,8},{10,9},{11,10},{13,12},{... | collective-permute-start | bytes 983048 | tf_op jit(solution)/shard_map/while/body/eval_jaxpr/ppermute | solution.py:21
  394.5 4.1 collective-permute-start.7
  404.4 6.6 copy-start.6
  405.1 12.4 %collective-permute-start.4 = (bf16[256,640]{1,0:T(8,128)(2,1)S(1)}, bf16[256,640]{1,0:T(8,128)(2,1)S(1)}, u32[]{:S(2)}, u32[]{:S(2)}) collective-permute-start(bf16[256,640]{1,0:T(8,128)(2,1)S(1)} %multiply_convert_fusion.6), channel_id=1, source_target_pairs={{0,1},{1,2},{2,3},{4,5},{5,6},{6,7},{8,9},{9,10},{10,11},{12,13},{... | collective-permute-start | bytes 983048 | tf_op jit(solution)/shard_map/while/body/eval_jaxpr/ppermute | solution.py:20
  409.7 16.2 %collective-permute-start.3 = (bf16[256,640]{1,0:T(8,128)(2,1)S(1)}, bf16[256,640]{1,0:T(8,128)(2,1)S(1)}, u32[]{:S(2)}, u32[]{:S(2)}) collective-permute-start(bf16[256,640]{1,0:T(8,128)(2,1)S(1)} %multiply_convert_fusion.6), channel_id=1, source_target_pairs={{1,0},{2,1},{3,2},{5,4},{6,5},{7,6},{9,8},{10,9},{11,10},{13,12},{... | collective-permute-start | bytes 983048 | tf_op jit(solution)/shard_map/while/body/eval_jaxpr/ppermute | solution.py:21
  414.1 13.5 %copy-start.1 = (bf16[5,640,640]{2,1,0:T(8,128)(2,1)S(1)}, bf16[5,640,640]{2,1,0:T(8,128)(2,1)}, u32[]{:S(2)}) copy-start(bf16[5,640,640]{2,1,0:T(8,128)(2,1)} %get-tuple-element.2260) | copy-start | bytes 12288004 | tf_op jit(solution)/shard_map/while
  431.6 23.4 %collective-permute-start.6 = (bf16[256,640]{1,0:T(8,128)(2,1)S(1)}, bf16[256,640]{1,0:T(8,128)(2,1)S(1)}, u32[]{:S(2)}, u32[]{:S(2)}) collective-permute-start(bf16[256,640]{1,0:T(8,128)(2,1)S(1)} %add_convert_fusion.11), channel_id=1, source_target_pairs={{0,1},{1,2},{2,3},{4,5},{5,6},{6,7},{8,9},{9,10},{10,11},{12,13},{... | collective-permute-start | bytes 983048 | tf_op jit(solution)/shard_map/while/body/eval_jaxpr/ppermute | solution.py:20
  433.3 21.7 %collective-permute-start.5 = (bf16[256,640]{1,0:T(8,128)(2,1)S(1)}, bf16[256,640]{1,0:T(8,128)(2,1)S(1)}, u32[]{:S(2)}, u32[]{:S(2)}) collective-permute-start(bf16[256,640]{1,0:T(8,128)(2,1)S(1)} %add_convert_fusion.11), channel_id=1, source_target_pairs={{1,0},{2,1},{3,2},{5,4},{6,5},{7,6},{9,8},{10,9},{11,10},{13,12},{... | collective-permute-start | bytes 983048 | tf_op jit(solution)/shard_map/while/body/eval_jaxpr/ppermute | solution.py:21
  437.0 3.2 copy-start.2
  464.4 4.1 collective-permute-start.7
  474.4 6.6 copy-start.6
  475.0 12.4 %collective-permute-start.4 = (bf16[256,640]{1,0:T(8,128)(2,1)S(1)}, bf16[256,640]{1,0:T(8,128)(2,1)S(1)}, u32[]{:S(2)}, u32[]{:S(2)}) collective-permute-start(bf16[256,640]{1,0:T(8,128)(2,1)S(1)} %multiply_convert_fusion.6), channel_id=1, source_target_pairs={{0,1},{1,2},{2,3},{4,5},{5,6},{6,7},{8,9},{9,10},{10,11},{12,13},{... | collective-permute-start | bytes 983048 | tf_op jit(solution)/shard_map/while/body/eval_jaxpr/ppermute | solution.py:20
  479.6 16.2 %collective-permute-start.3 = (bf16[256,640]{1,0:T(8,128)(2,1)S(1)}, bf16[256,640]{1,0:T(8,128)(2,1)S(1)}, u32[]{:S(2)}, u32[]{:S(2)}) collective-permute-start(bf16[256,640]{1,0:T(8,128)(2,1)S(1)} %multiply_convert_fusion.6), channel_id=1, source_target_pairs={{1,0},{2,1},{3,2},{5,4},{6,5},{7,6},{9,8},{10,9},{11,10},{13,12},{... | collective-permute-start | bytes 983048 | tf_op jit(solution)/shard_map/while/body/eval_jaxpr/ppermute | solution.py:21
  484.1 13.5 %copy-start.1 = (bf16[5,640,640]{2,1,0:T(8,128)(2,1)S(1)}, bf16[5,640,640]{2,1,0:T(8,128)(2,1)}, u32[]{:S(2)}) copy-start(bf16[5,640,640]{2,1,0:T(8,128)(2,1)} %get-tuple-element.2260) | copy-start | bytes 12288004 | tf_op jit(solution)/shard_map/while
  501.5 23.4 %collective-permute-start.6 = (bf16[256,640]{1,0:T(8,128)(2,1)S(1)}, bf16[256,640]{1,0:T(8,128)(2,1)S(1)}, u32[]{:S(2)}, u32[]{:S(2)}) collective-permute-start(bf16[256,640]{1,0:T(8,128)(2,1)S(1)} %add_convert_fusion.11), channel_id=1, source_target_pairs={{0,1},{1,2},{2,3},{4,5},{5,6},{6,7},{8,9},{9,10},{10,11},{12,13},{... | collective-permute-start | bytes 983048 | tf_op jit(solution)/shard_map/while/body/eval_jaxpr/ppermute | solution.py:20
  503.3 21.7 %collective-permute-start.5 = (bf16[256,640]{1,0:T(8,128)(2,1)S(1)}, bf16[256,640]{1,0:T(8,128)(2,1)S(1)}, u32[]{:S(2)}, u32[]{:S(2)}) collective-permute-start(bf16[256,640]{1,0:T(8,128)(2,1)S(1)} %add_convert_fusion.11), channel_id=1, source_target_pairs={{1,0},{2,1},{3,2},{5,4},{6,5},{7,6},{9,8},{10,9},{11,10},{13,12},{... | collective-permute-start | bytes 983048 | tf_op jit(solution)/shard_map/while/body/eval_jaxpr/ppermute | solution.py:21
  507.0 3.2 copy-start.2
  534.4 4.1 collective-permute-start.7
  959.4 7.3 copy-start.12
  (61 other events, 104.2 us)
Sparse Core Ops, SparseCore 0:
  540.1 415.4 all-reduce.3
where the time goes:
time: 979 us; the launch traced here: 975 us
  waiting for transfers between devices  407 us (42%)
  matrix products  159 us (16%)
  blocking collectives  124 us (13%)
  other arithmetic  106 us (11%)
  local copies, waits for them, and re-layouts  81.7 us (8%)
  starting transfers between devices  79.9 us (8%)
  between operations  14.2 us (1%)
    psum x1, waiting for transfers between devices, body(): lax.psum((sum_gain_first, sum_shift_first, sum_gain_mid, sum_shift_mid, s...  291 us
    ppermute x15, waiting for transfers between devices, extended(): after = lax.ppermute(first, axis, down)  80.8 us
    psum x1, blocking collectives, body(): lax.psum((sum_gain_first, sum_shift_first, sum_gain_mid, sum_shift_mid, s...  78.5 us
    dot_general x50, matrix products, forward_parts(): jnp.dot(window, kernel[tap], preferred_element_type=jnp.float32)  48.9 us
    while x160, local copies, waits for them, and re-layouts  48 us
    add x15, other arithmetic, backward_tick(): grads = tuple((acc + flag * term for acc, term in zip(grads, terms)))  46.8 us
    psum x1, blocking collectives, body(): total_counts = lax.psum(counts, ('section', 'dp', 'seq'))  45.8 us
    ppermute x15, starting transfers between devices, extended(): before = lax.ppermute(last, axis, up)  44.4 us
  transfers between devices with their start and end apart: 41, of which 31 were waited for; matrix products, arithmetic and copies ran while one was open for 13% of the time, Pallas kernels for 0%

commit v1 on v0

v1 whole, which is shorter than its diff:
```python
import functools

import jax
import jax.numpy as jnp
from jax import lax
from jax.experimental import pallas as pl
from jax.experimental.pallas import tpu as pltpu
from jax.sharding import PartitionSpec as P

EPS = 1e-05
BF, F32 = jnp.bfloat16, jnp.float32
MESH = pl.DeviceIdType.MESH
G0 = 0.7978845608028654
G1 = 0.044715
DIL = 2
HALO = 16
CH = 16


def dot(a, b):
    return lax.dot_general(a, b, (((1,), (0,)), ((), ())), preferred_element_type=F32)


def dot_nt(a, b):
    return lax.dot_general(a, b, (((1,), (1,)), ((), ())), preferred_element_type=F32)


def dot_tn(a, b):
    return lax.dot_general(a, b, (((0,), (0,)), ((), ())), preferred_element_type=F32)


def chunks(rows, fn, size=CH):
    def one(i, _):
        fn(pl.multiple_of(i * size, size))
        return 0

    lax.fori_loop(0, rows // size, one, 0)


def normed(v):
    centre = v - jnp.mean(v, axis=-1, keepdims=True)
    var = jnp.mean(centre * centre, axis=-1, keepdims=True)
    rstd = lax.rsqrt(var + EPS)
    return centre * rstd, rstd


def gelu(u):
    t = jnp.tanh(u * (G0 + (G0 * G1) * (u * u)))
    h = 0.5 * u
    return h + h * t


def gelu_slope(u):
    w = u * u
    t = jnp.tanh(u * (G0 + (G0 * G1) * w))
    return 0.5 * (1.0 + t) + (0.5 * u) * (1.0 - t * t) * (G0 + (3.0 * G0 * G1) * w)


def fold(v):
    rows, width = v.shape
    return jnp.sum(v.reshape(rows // 8, 8, width), axis=0)


def norm_gelu_back(v, dy, gain, shift, dgain, dshift):
    hat, rstd = normed(v)
    du = dy * gelu_slope(hat * gain + shift)
    dhat_raw = du * hat
    if dgain is not None:
        dgain[...] += fold(dhat_raw)
        dshift[...] += fold(du)
    dh = du * gain
    m1 = jnp.mean(dh, axis=-1, keepdims=True)
    m2 = jnp.mean(dh * hat, axis=-1, keepdims=True)
    return rstd * (dh - m1 - hat * m2)


def put_grad(g_ref, unit, value, col0=0):
    m, n = value.shape
    per = m // 32
    value = value.astype(BF)
    for j in range(n // 128):
        block = value[:, j * 128 : (j + 1) * 128].reshape(m // 16, 16, 128)
        for h in range(2):
            g_ref[h, pl.ds(unit + (col0 + j) * per, per)] = block[h * per : (h + 1) * per]


CONV0, OUT0, IN0, EXTRA0, UNITS = 0, 500, 700, 900, 912


def k1(xe, cot, scal, w_in1, conv1, w_out1, w_in2, w_out2, gi1, bi1, gm1, bm1, gi2, bi2, gm2, bm2,
       out1, first1, hidden1, sec1, mixed1, third1, first2, hidden2, sec2, dthird2, fe, he, me):
    base = scal[0]
    rows, seg = xe.shape[1], out1.shape[1]
    for m in range(2):
        def a(i):
            hat, _ = normed(xe[m, pl.ds(i, CH)].astype(F32))
            fe[pl.ds(i, CH)] = gelu(hat * gi1[...] + bi1[...]).astype(BF)

        chunks(rows, a)
        first1[m] = fe[pl.ds(HALO, seg)]
        he[...] = dot(fe[...], w_in1[0])
        hidden1[m] = he[pl.ds(HALO, seg)]
        sec1[m, pl.ds(0, 8)] = jnp.zeros((8, sec1.shape[2]), F32)
        sec1[m, pl.ds(rows + 8, 8)] = jnp.zeros((8, sec1.shape[2]), F32)
        length = scal[1 + m]

        def b(i):
            hat, _ = normed(he[pl.ds(i, CH)])
            pos = base - HALO + i + lax.broadcasted_iota(jnp.int32, (CH, 1), 0)
            keep = jnp.logical_and(pos >= 0, pos < length)
            val = gelu(hat * gm1[pl.ds(0, 1)] + bm1[pl.ds(0, 1)])
            sec1[m, pl.ds(i + 8, CH)] = jnp.where(keep, val, 0.0).astype(BF).astype(F32)

        chunks(rows, b)
        acc = None
        for k in range(5):
            term = dot(sec1[m, pl.ds(8 + DIL * (k - 2), rows)].astype(BF), conv1[0, k])
            acc = term if acc is None else acc + term
        mixed1[m] = acc

        def c(i):
            hat, _ = normed(mixed1[m, pl.ds(i + HALO, CH)])
            third1[m, pl.ds(i, CH)] = gelu(hat * gm1[pl.ds(1, 1)] + bm1[pl.ds(1, 1)]).astype(BF)

        chunks(seg, c)
        he[pl.ds(0, seg)] = dot(third1[m], w_out1[0, :, :640])
        me[...] = dot(third1[m], w_out1[0, :, 640:])

        def d(i):
            br = jnp.concatenate([he[pl.ds(i, CH)], me[pl.ds(i, CH)]], axis=1)
            res = (xe[m, pl.ds(i + HALO, CH)].astype(F32) + br).astype(BF)
            out1[m, pl.ds(i, CH)] = res
            hat, _ = normed(res.astype(F32))
            first2[m, pl.ds(i, CH)] = gelu(hat * gi2[...] + bi2[...]).astype(BF)

        chunks(seg, d)
        hidden2[m] = dot(first2[m], w_in2[0])

        def e(i):
            hat, _ = normed(hidden2[m, pl.ds(i, CH)])
            pos = base + i + lax.broadcasted_iota(jnp.int32, (CH, 1), 0)
            val = gelu(hat * gm2[pl.ds(0, 1)] + bm2[pl.ds(0, 1)])
            sec2[m, pl.ds(i, CH)] = jnp.where(pos < length, val, 0.0).astype(BF)

        chunks(seg, e)
        dthird2[m] = dot_nt(cot[m], w_out2[0]).astype(BF)


def k2(sec, dthird, conv2, gm2, bm2, third, dsec, dgb, g_ref, sp, dp, mx, acc_ref):
    rows, w = sec.shape
    pad = 128
    z = jnp.zeros((pad, w), BF)
    for ref in (sp, dp):
        ref[pl.ds(0, pad)] = z
        ref[pl.ds(pad + rows, pad)] = z
    sp[pl.ds(pad, rows)] = sec[...]
    for r in range(0, rows, 256):
        acc = None
        for k in range(5):
            term = dot(sp[pl.ds(64 * k + r, 256)], conv2[0, k])
            acc = term if acc is None else acc + term
        mx[pl.ds(r, 256)] = acc
    dgb[...] = jnp.zeros_like(dgb)

    def a(i):
        v = mx[pl.ds(i, CH)]
        hat, rstd = normed(v)
        gain, shift = gm2[pl.ds(1, 1)], bm2[pl.ds(1, 1)]
        third[pl.ds(i, CH)] = gelu(hat * gain + shift).astype(BF)
        dm = norm_gelu_back(v, dthird[pl.ds(i, CH)].astype(F32), gain, shift, dgb.at[0], dgb.at[1])
        dp[pl.ds(pad + i, CH)] = dm.astype(BF)

    chunks(rows, a)
    dm = dp[pl.ds(pad, rows)]
    for k in range(5):
        put_grad(g_ref, CONV0 + k * 100, dot_tn(sp[pl.ds(64 * k, rows)], dm))
    for r in range(0, rows, 256):
        acc = None
        for k in range(5):
            term = dot_nt(dp[pl.ds(64 * (4 - k) + r, 256)], conv2[0, k])
            acc = term if acc is None else acc + term
        dsec[pl.ds(r, 256)] = acc.astype(BF)


def k3(out1, third2, dsec2, cot, first2, hidden2, w_in2, w_out2, dec, gi2, bi2, gm2, bm2, scal, mask, types,
       out2, grad2, dgbi, dgbm, counts, g_ref, he, me, dh):
    base = scal[0]
    seg = out1.shape[1]
    rows = 2 * seg
    classes = dec.shape[1]
    for ref in (dgbi, dgbm, counts):
        ref[...] = jnp.zeros_like(ref)
    labels = lax.broadcasted_iota(jnp.int32, (1, 128), 1)
    for m in range(2):
        length = scal[1 + m]
        he[...] = dot(third2[m], w_out2[0, :, :640])
        me[...] = dot(third2[m], w_out2[0, :, 640:])

        def a(i):
            br = jnp.concatenate([he[pl.ds(i, CH)], me[pl.ds(i, CH)]], axis=1)
            out2[m, pl.ds(i, CH)] = (out1[m, pl.ds(i, CH)].astype(F32) + br).astype(BF)

        chunks(seg, a)
        logits = dot(out2[m], dec[...])
        logits = jnp.where(labels < 30, logits, -1e30)
        top = jnp.max(logits, axis=-1, keepdims=True)
        ex = jnp.exp(logits - top)
        probs = ex / jnp.sum(ex, axis=-1, keepdims=True)
        pos = base + lax.broadcasted_iota(jnp.int32, (seg, 1), 0)
        weight = jnp.where(pos < length, mask[m].astype(F32), 0.0)
        hit = types[m] == labels
        counts[...] += fold(jnp.where(hit, probs * weight, 0.0))

        def b(i):
            pos = base + i + lax.broadcasted_iota(jnp.int32, (CH, 1), 0)
            ds = jnp.where(pos < length, dsec2[m, pl.ds(i, CH)].astype(F32), 0.0)
            dv = norm_gelu_back(hidden2[m, pl.ds(i, CH)], ds, gm2[pl.ds(0, 1)], bm2[pl.ds(0, 1)], dgbm.at[0], dgbm.at[1])
            dh[m, pl.ds(i, CH)] = dv.astype(BF)

        chunks(seg, b)
        he[...] = dot_nt(dh[m], w_in2[0, :640])
        me[...] = dot_nt(dh[m], w_in2[0, 640:])

        def c(i):
            df = jnp.concatenate([he[pl.ds(i, CH)], me[pl.ds(i, CH)]], axis=1)
            dv = norm_gelu_back(out1[m, pl.ds(i, CH)].astype(F32), df, gi2[...], bi2[...], dgbi.at[0], dgbi.at[1])
            grad2[m, pl.ds(i, CH)] = (cot[m, pl.ds(i, CH)].astype(F32) + dv).astype(BF)

        chunks(seg, c)
    flat = lambda ref: ref[...].reshape(rows, ref.shape[2])
    t2, g2 = flat(third2), flat(cot)
    for j in range(2):
        put_grad(g_ref, 0, dot_tn(t2, g2[:, j * 640 : (j + 1) * 640]), 5 * j)
    f2, d2 = flat(first2), flat(dh)
    put_grad(g_ref, 200, dot_tn(f2, d2))


def k4(xe, ge, scal, first1, hidden1, sec1, mixed1, third1, w_in1, conv1, w_out1, gi1, bi1, gm1, bm1,
       grad1, dgbi, dgbm, g_ref, he, me, dme, dh, dm, swin):
    base = scal[0]
    rows, seg = xe.shape[1], grad1.shape[1]
    for ref in (dgbi, dgbm):
        ref[...] = jnp.zeros_like(ref)
    for m in range(2):
        length = scal[1 + m]
        he[...] = dot_nt(ge[m], w_out1[0])
        gain, shift = gm1[pl.ds(1, 1)], bm1[pl.ds(1, 1)]

        def a(i):
            dv = norm_gelu_back(mixed1[m, pl.ds(i + HALO, CH)], he[pl.ds(i + HALO, CH)], gain, shift, dgbm.at[2], dgbm.at[3])
            dme[pl.ds(i + HALO, CH)] = dv.astype(BF).astype(F32)
            dm[m, pl.ds(i, CH)] = dv.astype(BF)

        chunks(seg, a)
        for edge in (0, rows - HALO):
            dv = norm_gelu_back(mixed1[m, pl.ds(edge, HALO)], he[pl.ds(edge, HALO)], gain, shift, None, None)
            pos = base - HALO + edge + lax.broadcasted_iota(jnp.int32, (HALO, 1), 0)
            inside = jnp.logical_and(pos >= 0, pos < 1024)
            dme[pl.ds(edge, HALO)] = jnp.where(inside, dv, 0.0).astype(BF).astype(F32)
        acc = None
        for k in range(5):
            term = dot_nt(dme[pl.ds(HALO - DIL * (k - 2), seg)].astype(BF), conv1[0, k])
            acc = term if acc is None else acc + term
        he[pl.ds(0, seg)] = acc

        def b(i):
            pos = base + i + lax.broadcasted_iota(jnp.int32, (CH, 1), 0)
            ds = jnp.where(pos < length, he[pl.ds(i, CH)], 0.0)
            dv = norm_gelu_back(hidden1[m, pl.ds(i, CH)], ds, gm1[pl.ds(0, 1)], bm1[pl.ds(0, 1)], dgbm.at[0], dgbm.at[1])
            dh[m, pl.ds(i, CH)] = dv.astype(BF)

        chunks(seg, b)
        he[pl.ds(0, seg)] = dot_nt(dh[m], w_in1[0, :640])
        me[...] = dot_nt(dh[m], w_in1[0, 640:])

        def c(i):
            df = jnp.concatenate([he[pl.ds(i, CH)], me[pl.ds(i, CH)]], axis=1)
            dv = norm_gelu_back(xe[m, pl.ds(i + HALO, CH)].astype(F32), df, gi1[...], bi1[...], dgbi.at[0], dgbi.at[1])
            grad1[m, pl.ds(i, CH)] = (ge[m, pl.ds(i + HALO, CH)].astype(F32) + dv).astype(BF)

        chunks(seg, c)
    flat = lambda v: v.reshape(2 * seg, v.shape[-1])
    t1 = flat(third1[...])
    for j in range(2):
        g1 = flat(ge[:, pl.ds(HALO, seg), pl.ds(j * 640, 640)])
        put_grad(g_ref, OUT0, dot_tn(t1, g1), 5 * j)
    d1 = flat(dm[...])
    for k in range(5):
        for m in range(2):
            swin[pl.ds(m * seg, seg)] = sec1[m, pl.ds(8 + HALO + DIL * (k - 2), seg)].astype(BF)
        put_grad(g_ref, CONV0 + k * 100, dot_tn(swin[...], d1))
    put_grad(g_ref, IN0, dot_tn(flat(first1[...]), flat(dh[...])))


class Ring:
    def __init__(self, N, PU, QU):
        self.N, self.PU, self.QU, self.U = N, PU, QU, PU + QU
        self.kinds = ["D","P1","P2","PZ1","PZ2","PT1","PT2","PT3","G1","G2","Q1","Q2","X1","X2","X3","X4","QT1","QT2","QT3","F"]
    def scratch(self):
        N2, PU, QU, U = 2*self.N, self.PU, self.QU, self.U
        b = lambda u: pltpu.VMEM((N2, u, 16, 128), BF)
        nk = len(self.kinds)
        return [b(U), b(PU//2), b(PU//4), b(PU//4), b(PU//8), b(QU), b(QU//2), b(QU//4), b(QU//8), b(U),
                pltpu.SemaphoreType.DMA((nk, N2)), pltpu.SemaphoreType.DMA((nk, N2))]
    def bind(self, G, two, one, out, D, RP1, RP2, RZ1, RZ2, RQ1, RQ2, RX1, RX2, R, ss, rs):
        N, PU, QU, U = self.N, self.PU, self.QU, self.U
        c, z, q = lax.axis_index("section"), lax.axis_index("dp"), lax.axis_index("seq")
        xb, yb = lax.rem(q, 2), lax.div(q, 2)
        f = jnp.where(c == 0, xb, yb); s = jnp.where(c == 0, yb, xb)
        qx = xb ^ 1;
        nx = (c, z, yb*2 + 1 - xb); ny = (c, z, (1-yb)*2 + xb)
        n1 = (c, z, jnp.where(c == 0, nx[2], ny[2])); n2 = (c, z, jnp.where(c == 0, ny[2], nx[2]))
        side = lax.div(z, 2)
        zp = (c, side*2 + 1 - lax.rem(z, 2), q)
        far = (c, 3 - z, q)
        peer = (1 - c, z, q)
        inner = jnp.logical_or(z == 1, z == 2)
        outer = jnp.logical_not(inner)
        K = {k: i for i, k in enumerate(self.kinds)}
        def cp(k, i, src, dst, dev):
            return pltpu.make_async_remote_copy(src_ref=src, dst_ref=dst, send_sem=ss.at[K[k], i], recv_sem=rs.at[K[k], i], device_id=dev, device_id_type=MESH)
        ds = pl.ds
        H, Q4, E8 = PU//2, PU//4, PU//8
        h, q4, e8 = QU//2, QU//8, QU//8
        def add(dst, a, *bs):
            acc = a[...].astype(F32)
            for b in bs: acc = acc + b[...].astype(F32)
            dst[...] = acc.astype(BF)
        pq = lambda ff, s2: ds((2*ff + s2)*Q4, Q4)
        pch = lambda k: ds((2*f + s)*Q4 + k*E8, E8)
        def qn(k): return ds(PU + k*h, h)
        def qhalf(k, ff): return ds(PU + k*h + ff*(h//2), h//2)
        def qquart(k, ff, s2): return ds(PU + k*h + (2*ff+s2)*(h//4), h//4)
        near, farc = side, 1 - side
        C = dict(
          D=lambda i: cp("D", i, two.at[1-c, i], D.at[i], peer),
          E=lambda i: cp("D", i, one.at[1-c, i-N], D.at[i], peer),
          W=lambda i: cp("D", i, G.at[i], D.at[i], peer),
          P1=lambda i: cp("P1", i, D.at[i, ds((1-f)*H, H)], RP1.at[i], n1),
          P2=lambda i: cp("P2", i, D.at[i, pq(f, 1-s)], RP2.at[i], n2),
          PZ1=lambda i: cp("PZ1", i, D.at[i, pq(f, s)], RZ1.at[i], zp),
          PZ2=lambda i: cp("PZ2", i, D.at[i, pch(farc)], RZ2.at[i], far),
          PT1=lambda i: cp("PT1", i, R.at[i, pch(near)], R.at[i, pch(near)], far),
          PT2=lambda i: cp("PT2", i, R.at[i, pch(near)], R.at[i, pch(near)], zp),
          PT3=lambda i: cp("PT3", i, R.at[i, pch(farc)], R.at[i, pch(farc)], zp),
          G1=lambda i: cp("G1", i, R.at[i, pq(f, s)], R.at[i, pq(f, s)], n2),
          G2=lambda i: cp("G2", i, R.at[i, ds(f*H, H)], R.at[i, ds(f*H, H)], n1),
          Q1=lambda i: cp("Q1", i, D.at[i, ds(PU, QU)], RQ1.at[i], zp),
          Q2=lambda i: cp("Q2", i, D.at[i, qn(farc)], RQ2.at[i], far),
          X1=lambda i: cp("X1", i, D.at[i, qhalf(near, 1-f)], RX1.at[i], n1),
          X2=lambda i: cp("X2", i, D.at[i, qquart(near, f, 1-s)], RX2.at[i], n2),
          X3=lambda i: cp("X3", i, R.at[i, qquart(near, f, s)], R.at[i, qquart(near, f, s)], n2),
          X4=lambda i: cp("X4", i, R.at[i, qhalf(near, f)], R.at[i, qhalf(near, f)], n1),
          QT1=lambda i: cp("QT1", i, R.at[i, qn(near)], R.at[i, qn(near)], far),
          QT2=lambda i: cp("QT2", i, R.at[i, qn(near)], R.at[i, qn(near)], zp),
          QT3=lambda i: cp("QT3", i, R.at[i, qn(farc)], R.at[i, qn(farc)], zp),
        )
        def mine(i): return jnp.where(i < N, 1, 0) == c
        def slot(i): return jnp.where(i < N, i, i - N)
        Fr = lambda i: cp("F", i, R.at[i], out.at[c, slot(i)], peer)
        Fl = lambda i: pltpu.make_async_copy(R.at[i], out.at[c, slot(i)], ss.at[K["F"], i])
        def S0(i):
            @pl.when(i < N)
            def _(): C["D"](i).start()
            @pl.when(i >= N)
            def _(): C["E"](i).start()
        def S1(i):
            C["W"](i).wait()
            add(D.at[i], D.at[i], G.at[i])
            C["P1"](i).start()
            @pl.when(outer)
            def _(): C["Q1"](i).start()
        def S2(i):
            @pl.when(inner)
            def _():
                C["Q1"](i).wait_recv()
                add(D.at[i, qn(farc)], D.at[i, qn(farc)], RQ1.at[i, ds(farc*h, h)])
                C["Q2"](i).start()
            C["P1"](i).wait()
            add(D.at[i, ds(f*H, H)], D.at[i, ds(f*H, H)], RP1.at[i])
            C["P2"](i).start()
            @pl.when(outer)
            def _(): C["Q1"](i).wait_send()
        def S3(i):
            C["P2"](i).wait()
            add(D.at[i, pq(f, s)], D.at[i, pq(f, s)], RP2.at[i])
            @pl.when(outer)
            def _(): C["PZ1"](i).start()
            @pl.when(inner)
            def _():
                C["Q2"](i).wait()
                add(D.at[i, qn(near)], D.at[i, qn(near)], RQ1.at[i, ds(near*h, h)], RQ2.at[i])
                C["X1"](i).start()
        def S4(i):
            @pl.when(inner)
            def _():
                C["PZ1"](i).wait_recv()
                add(D.at[i, pch(farc)], D.at[i, pch(farc)], RZ1.at[i, ds(farc*E8, E8)])
                C["PZ2"](i).start()
                C["X1"](i).wait()
                add(D.at[i, qhalf(near, f)], D.at[i, qhalf(near, f)], RX1.at[i])
                C["X2"](i).start()
            @pl.when(outer)
            def _(): C["PZ1"](i).wait_send()
        def S5(i):
            @pl.when(inner)
            def _():
                C["PZ2"](i).wait()
                add(R.at[i, pch(near)], D.at[i, pch(near)], RZ1.at[i, ds(near*E8, E8)], RZ2.at[i])
                C["PT1"](i).start(); C["PT2"](i).start()
                C["X2"](i).wait()
                add(R.at[i, qquart(near, f, s)], D.at[i, qquart(near, f, s)], RX2.at[i])
                C["X3"](i).start()
        def S6(i):
            @pl.when(inner)
            def _():
                C["PT1"](i).wait()
                C["PT3"](i).start()
                C["X3"](i).wait()
                C["X4"](i).start()
        def S7(i):
            @pl.when(outer)
            def _():
                C["PT2"](i).wait_recv(); C["PT3"](i).wait_recv()
            @pl.when(inner)
            def _():
                C["PT2"](i).wait_send(); C["PT3"](i).wait_send()
            C["G1"](i).start()
            @pl.when(inner)
            def _():
                C["X4"](i).wait()
                C["QT1"](i).start(); C["QT2"](i).start()
        def S8(i):
            C["G1"](i).wait()
            C["G2"](i).start()
            @pl.when(inner)
            def _():
                C["QT1"](i).wait()
                C["QT3"](i).start()
        def S9(i):
            C["G2"](i).wait()
            @pl.when(outer)
            def _():
                C["QT2"](i).wait_recv(); C["QT3"](i).wait_recv()
            @pl.when(inner)
            def _():
                C["QT2"](i).wait_send(); C["QT3"](i).wait_send()
            m = mine(i)
            @pl.when(m)
            def _(): Fl(i).start()
            @pl.when(jnp.logical_not(m))
            def _(): Fr(i).start()
        def S10(i):
            m = mine(i)
            @pl.when(m)
            def _(): Fl(i).wait()
            @pl.when(jnp.logical_not(m))
            def _(): Fr(i).wait_send()
        stages = [S0,S1,S2,S3,S4,S5,S6,S7,S8,S9,S10]
        def step(t):
            for si in range(len(stages)):
                i = t - si
                @pl.when(jnp.logical_and(i >= 0, i < 2*N))
                def _(): stages[si](i)
        def recv_final():
            def body(j, _):
                i = jnp.where(c == 1, j, j + N)
                Fr(i).wait_recv()
                return 0
            lax.fori_loop(0, N, body, 0)
        def barrier():
            b = pltpu.get_barrier_semaphore()
            for d in (peer, n1, n2, zp):
                pl.semaphore_signal(b, inc=1, device_id=d, device_id_type=MESH)
            @pl.when(inner)
            def _():
                pl.semaphore_signal(b, inc=1, device_id=far, device_id_type=MESH)
                pl.semaphore_wait(b, 5)
            @pl.when(outer)
            def _(): pl.semaphore_wait(b, 4)
        self.R = R
        self.barrier, self.step, self.recv_final, self.iters = barrier, step, recv_final, 2*N + len(stages) - 1


def ar_kernel(ring, one, two, out, cnt, G, gsem, *scr):
    N = ring.N
    c = lax.axis_index("section")
    loads = [pltpu.make_async_copy(two.at[c], G.at[pl.ds(0, N)], gsem.at[0]), pltpu.make_async_copy(one.at[c], G.at[pl.ds(N, N)], gsem.at[1])]
    for cp in loads:
        cp.start()
    ring.bind(G, two, one, out, *scr)
    ring.barrier()
    for cp in loads:
        cp.wait()

    def body(t, _):
        ring.step(t)
        return 0

    lax.fori_loop(0, ring.iters, body, 0)
    ring.recv_final()
    cnt[...] = ring.R[N - 1, pl.ds(ring.U - 12, 12)]


def allreduce(one, two, N, PU, QU):
    ring = Ring(N, PU, QU)
    U = PU + QU
    any_ = pl.BlockSpec(memory_space=pl.ANY)
    split = lambda g: g.reshape(2, N, U, 16, 128)
    return pl.pallas_call(
        functools.partial(ar_kernel, ring),
        out_shape=[jax.ShapeDtypeStruct((2, N, U, 16, 128), BF), jax.ShapeDtypeStruct((12, 16, 128), BF)],
        in_specs=[any_, any_],
        out_specs=[any_, pl.BlockSpec(memory_space=pltpu.VMEM)],
        scratch_shapes=[pltpu.VMEM((2 * N, U, 16, 128), BF), pltpu.SemaphoreType.DMA((2,))] + ring.scratch(),
        compiler_params=pltpu.CompilerParams(collective_id=0, has_side_effects=True, vmem_limit_bytes=60 * 2**20),
    )(split(one), split(two))


def plane(c, z, q):
    out = []
    for i in range(1, 8):
        n = lax.rem(c * 4 + q + i, 8)
        out.append((lax.div(n, 4), z, lax.rem(n, 4)))
    return out


def greet(ids):
    barrier = pltpu.get_barrier_semaphore()
    for d in ids:
        pl.semaphore_signal(barrier, inc=1, device_id=d, device_id_type=MESH)
    pl.semaphore_wait(barrier, len(ids))


def spread_kernel(n, *refs):
    srcs, dsts, ss, rs, ls = refs[:n], refs[n : 2 * n], refs[-3], refs[-2], refs[-1]
    c, z, q = lax.axis_index("section"), lax.axis_index("dp"), lax.axis_index("seq")
    greet(plane(c, z, q))
    from_core = lax.div(q, 2)
    for phase in (0, 1):
        for a in range(n):
            for ml in range(2):
                for h in range(2):
                    local = jnp.logical_and(h == c, 2 * c + ml == q)
                    src, dst = srcs[a].at[ml, :, h], dsts[a].at[q]
                    j = 2 * ml + h
                    far = pltpu.make_async_remote_copy(src_ref=src, dst_ref=dst, send_sem=ss.at[a, j], recv_sem=rs.at[a, q],
                                                       device_id=(h, z, 2 * c + ml), device_id_type=MESH)
                    near = pltpu.make_async_copy(src, dst, ls.at[a])

                    @pl.when(local)
                    def _():
                        near.start() if phase == 0 else near.wait()

                    @pl.when(jnp.logical_not(local))
                    def _():
                        far.start() if phase == 0 else far.wait_send()
            if phase == 1:
                for p in range(4):
                    @pl.when(jnp.logical_not(jnp.logical_and(c == from_core, p == q)))
                    def _():
                        pltpu.make_async_remote_copy(src_ref=srcs[a].at[0, :, 0], dst_ref=dsts[a].at[p], send_sem=ss.at[a, 0],
                                                     recv_sem=rs.at[a, p], device_id=(from_core, z, p), device_id_type=MESH).wait_recv()


def gather_kernel(n, *refs):
    srcs, dsts, ss, rs, ls = refs[:n], refs[n : 2 * n], refs[-3], refs[-2], refs[-1]
    c, z, q = lax.axis_index("section"), lax.axis_index("dp"), lax.axis_index("seq")
    greet(plane(c, z, q))
    to_core, slot = lax.div(q, 2), lax.rem(q, 2)
    for phase in (0, 1):
        for a in range(n):
            for p in range(4):
                local = jnp.logical_and(to_core == c, p == q)
                src, dst = srcs[a].at[p], dsts[a].at[slot, :, c]
                far = pltpu.make_async_remote_copy(src_ref=src, dst_ref=dst, send_sem=ss.at[a, p], recv_sem=rs.at[a, 2 * slot + c],
                                                   device_id=(to_core, z, p), device_id_type=MESH)
                near = pltpu.make_async_copy(src, dst, ls.at[a])

                @pl.when(local)
                def _():
                    near.start() if phase == 0 else near.wait()

                @pl.when(jnp.logical_not(local))
                def _():
                    far.start() if phase == 0 else far.wait_send()
            if phase == 1:
                for ml in range(2):
                    for h in range(2):
                        @pl.when(jnp.logical_not(jnp.logical_and(h == c, 2 * c + ml == q)))
                        def _():
                            pltpu.make_async_remote_copy(src_ref=srcs[a].at[0], dst_ref=dsts[a].at[ml, :, h], send_sem=ss.at[a, 0],
                                                         recv_sem=rs.at[a, 2 * ml + h], device_id=(h, z, 2 * c + ml), device_id_type=MESH).wait_recv()


def exchange(kernel, arrays, shape, cid):
    n = len(arrays)
    any_ = pl.BlockSpec(memory_space=pl.ANY)
    return pl.pallas_call(
        functools.partial(kernel, n),
        out_shape=[jax.ShapeDtypeStruct(shape, BF)] * n,
        in_specs=[any_] * n,
        out_specs=[any_] * n,
        scratch_shapes=[pltpu.SemaphoreType.DMA((n, 4)), pltpu.SemaphoreType.DMA((n, 4)), pltpu.SemaphoreType.DMA((n,))],
        compiler_params=pltpu.CompilerParams(collective_id=cid, has_side_effects=True),
    )(*arrays)


def call(fn, outs, scratch, args, scal_at=(), layer={}):
    vm = pl.BlockSpec(memory_space=pltpu.VMEM)
    whole, place = [], []
    for a in args:
        if not any(a is w for w in whole):
            whole.append(a)
        place.append(next(i for i, w in enumerate(whole) if w is a))
    specs = [pl.BlockSpec(memory_space=pltpu.SMEM) if place.index(i) in scal_at else vm for i in range(len(whole))]

    def kernel(*refs):
        ins = [refs[p].at[pl.ds(layer[i], 1)] if i in layer else refs[p] for i, p in enumerate(place)]
        fn(*ins, *refs[len(whole):])

    return pl.pallas_call(
        kernel,
        out_shape=[jax.ShapeDtypeStruct(s, d) for s, d in outs],
        in_specs=specs,
        out_specs=[vm] * len(outs),
        scratch_shapes=[pltpu.VMEM(s, d) for s, d in scratch],
        compiler_params=pltpu.CompilerParams(vmem_limit_bytes=60 * 2**20),
    )(*whole)


def body(inputs, lengths, mlm_mask, true_types, gain_in, bias_in, gain_mid, bias_mid, w_in, conv_w, w_out, decoder, cotangent, fast):
    c, q = lax.axis_index("section"), lax.axis_index("seq")
    seg, D, H = inputs.shape[2], inputs.shape[3], w_in.shape[2]
    rows = seg + 2 * HALO
    both = lambda w: lax.all_gather(w, "section", axis=0, tiled=True)
    w_in, conv_w, w_out = both(w_in), both(conv_w), both(w_out)
    gi, bi, gm, bm = (both(v.astype(F32)) for v in (gain_in, bias_in, gain_mid, bias_mid))
    mine = lambda v: lax.dynamic_slice_in_dim(v[:, 0], 2 * c, 2, 0)
    x, cot = mine(inputs), mine(cotangent)
    mask, types = mine(mlm_mask)[..., None], mine(true_types)[..., None]
    scal = jnp.concatenate([jnp.reshape(q * seg, (1,)), lax.dynamic_slice_in_dim(lengths[:, 0], 2 * c, 2, 0)]).astype(jnp.int32)
    n = lax.axis_size("seq")
    up = [(i, i + 1) for i in range(n - 1)]
    down = [(j, i) for i, j in up]

    def haloed(v):
        before = lax.ppermute(v[:, seg - HALO :], "seq", up)
        after = lax.ppermute(v[:, :HALO], "seq", down)
        return jnp.concatenate([before, v, after], axis=1)

    g1_, b1_, g2_, b2_ = gi[0:1], bi[0:1], gi[1:2], bi[1:2]
    xe = haloed(x)
    out1, first1, hidden1, sec1, mixed1, third1, first2, hidden2, sec2, dthird2 = call(
        k1,
        [((2, seg, D), BF), ((2, seg, D), BF), ((2, seg, H), F32), ((2, rows + 16, H), F32), ((2, rows, H), F32), ((2, seg, H), BF),
         ((2, seg, D), BF), ((2, seg, H), F32), ((2, seg, H), BF), ((2, seg, H), BF)],
        [((rows, D), BF), ((rows, H), F32), ((seg, H), F32)],
        (xe, cot, scal, w_in, conv_w, w_out, w_in, w_out, g1_, b1_, gm[0], bm[0], g2_, b2_, gm[1], bm[1]),
        (2,), {3: 0, 4: 0, 5: 0, 6: 1, 7: 1})
    split = lambda v: v.reshape(2, 2, 2, 64, H)
    sec_r, dthird_r = exchange(spread_kernel, [split(sec2), split(dthird2)], (4, 2, 64, H), 1)
    line = lambda v: v.reshape(8 * 64, H)
    units = lambda u: ((2, u, 16, 128), BF)
    third_r, dsec_r, dgb2, g_conv = call(
        k2,
        [((512, H), BF), ((512, H), BF), ((2, 8, H), F32), units(500)],
        [((768, H), BF), ((768, H), BF), ((512, H), F32), ((8, H), F32)],
        (line(sec_r), line(dthird_r), conv_w, gm[1], bm[1]), (), {2: 1})
    block = lambda v: v.reshape(4, 2, 64, H)
    third2, dsec2 = exchange(gather_kernel, [block(third_r), block(dsec_r)], (2, 2, 2, 64, H), 2)
    join = lambda v: v.reshape(2, seg, H)
    dec = jnp.pad(decoder, ((0, 0), (0, 128 - decoder.shape[1])))
    out2, grad2, dgbi2, dgbm2, counts, g_rest = call(
        k3,
        [((2, seg, D), BF), ((2, seg, D), BF), ((2, 8, D), F32), ((2, 8, H), F32), ((8, 128), F32), units(400)],
        [((seg, H), F32), ((seg, H), F32), ((2, seg, H), BF)],
        (out1, join(third2), join(dsec2), cot, first2, hidden2, w_in, w_out, dec, g2_, b2_, gm[1], bm[1], scal, mask, types),
        (13,), {6: 1, 7: 1})
    ge = haloed(grad2)
    grad1, dgbi1, dgbm1, g_one = call(
        k4,
        [((2, seg, D), BF), ((2, 8, D), F32), ((4, 8, H), F32), units(900)],
        [((rows, H), F32), ((seg, H), F32), ((rows, H), F32), ((2, seg, H), BF), ((2, seg, H), BF), ((2 * seg, H), BF)],
        (xe, ge, scal, first1, hidden1, sec1, mixed1, third1, w_in, conv_w, w_out, g1_, b1_, gm[0], bm[0]),
        (2,), {8: 0, 9: 0, 10: 0})

    def extra(dgbi, dgbm, cnt):
        flat = jnp.concatenate([dgbi.sum(1).reshape(-1), dgbm.sum(1).reshape(-1), cnt.sum(0)])
        flat = jnp.pad(flat, (0, 12 * 2048 - flat.shape[0])).astype(BF).reshape(1, 12, 16, 128)
        return jnp.concatenate([flat, flat], 0)

    g_two = jnp.concatenate([g_conv, g_rest, extra(dgbi2, jnp.concatenate([dgbm2, dgb2]), counts)], 1)
    g_one = jnp.concatenate([g_one, extra(dgbi1, dgbm1, jnp.zeros_like(counts))], 1)
    if fast:
        N, PU, QU = 6, 88, 64
        total, cnt = allreduce(g_one, g_two, N, PU, QU)
        total = total.reshape(2, UNITS, 16, 128)
    else:
        own, other = jnp.where(c == 0, g_one, g_two), jnp.where(c == 0, g_two, g_one)
        got = lax.ppermute(other, "section", [(0, 1), (1, 0)])
        total = lax.psum(own.astype(F32) + got.astype(F32), ("dp", "seq"))
        cnt = lax.psum(g_two[0, EXTRA0:].astype(F32), ("section", "dp", "seq"))
    total = total.astype(F32)
    s_conv = total[:, :OUT0].reshape(2, 5, 5, H // 2, 128).transpose(1, 0, 3, 2, 4).reshape(1, 5, H, H)
    s_out = total[:, OUT0:IN0].reshape(2, D // 128, H // 2, 128).transpose(0, 2, 1, 3).reshape(1, H, D)
    s_in = total[:, IN0:EXTRA0].reshape(2, H // 128, D // 2, 128).transpose(0, 2, 1, 3).reshape(1, D, H)
    small = total[0, EXTRA0 : EXTRA0 + 3].reshape(-1)
    s_bi = small[: 2 * D].reshape(2, D)
    s_bm = small[2 * D : 2 * D + 4 * H].reshape(2, 2, H)
    s_cnt = cnt[:3].astype(F32).reshape(-1)[2 * D + 4 * H : 2 * D + 4 * H + decoder.shape[1]]

    def placed(one, two):
        own, other = jnp.where(c == 0, one, two), jnp.where(c == 0, two, one)
        got = lax.ppermute(other, "section", [(0, 1), (1, 0)])
        return jnp.where(c == 0, jnp.concatenate([own, got]), jnp.concatenate([got, own]))[None, :, None]

    return (placed(out1, out2), placed(grad1, grad2), s_bi[0:1], s_bi[1:2], s_bm[None, :, 0], s_bm[None, :, 1],
            s_in, s_conv, s_out, s_cnt)


def solution(mesh):
    fast = mesh.shape["dp"] == 4 and mesh.shape["seq"] == 4
    return jax.shard_map(
        functools.partial(body, fast=fast),
        mesh=mesh,
        in_specs=(P(None, "dp", "seq", None), P(None, "dp"), P(None, "dp", "seq"), P(None, "dp", "seq"), P("section", None),
                  P("section", None), P("section", None, None), P("section", None, None), P("section", None, None),
                  P("section", None, None, None), P("section", None, None), P(), P(None, "dp", "seq", None)),
        out_specs=(P("section", None, "dp", "seq", None), P("section", None, "dp", "seq", None), P("section", None), P("section", None),
                   P("section", None, None), P("section", None, None), P("section", None, None), P("section", None, None, None),
                   P("section", None, None), P()),
        check_vma=False,
    )
```

time: 979 us -> 536 us (0.55)
  waiting for transfers between devices: 407 us -> 30.3 us
  Pallas kernels: 0 us -> 352 us
  matrix products: 159 us -> 0 us
  blocking collectives: 124 us -> 7.17 us
  starting transfers between devices: 79.9 us -> 11.7 us
  other arithmetic: 106 us -> 46.8 us
  local copies, waits for them, and re-layouts: 81.7 us -> 62.9 us
    pallas_call x0 -> x7, Pallas kernels: none -> 352 us  [the longest x4 168 us: call(): pl.pallas_call(kernel, out_shape=[jax.ShapeDtypeStruct(s, d) for s, d in...]
    psum x1 -> x0, waiting for transfers between devices: 291 us -> none  [body(): lax.psum((sum_gain_first, sum_shift_first, sum_gain_mid, sum_shift_mid, s...]
    dot_general x140 -> x0, matrix products: 159 us -> none  [the longest x50 48.9 us: forward_parts(): jnp.dot(window, kernel[tap], preferred_element_type=jnp.float32)]
    psum x2 -> x0, blocking collectives: 124 us -> none  [the longest x1 78.5 us: body(): lax.psum((sum_gain_first, sum_shift_first, sum_gain_mid, sum_shift_mid, s...]
    ppermute x40 -> x6, waiting for transfers between devices: 117 us -> 0.02 us  [the longest x2 0.01 us: haloed(): before = lax.ppermute(v[:, seg - HALO:], 'seq', up)]
    ppermute x40 -> x6, starting transfers between devices: 79.8 us -> 11.6 us  [the longest x2 8.02 us: haloed(): before = lax.ppermute(v[:, seg - HALO:], 'seq', up)]
    while x160 -> x0, local copies, waits for them, and re-layouts: 48 us -> none
    add x21 -> x0, other arithmetic: 46.8 us -> none  [the longest x15 46.8 us: backward_tick(): grads = tuple((acc + flag * term for acc, term in zip(grads, terms)))]
  transfers between devices with their start and end apart: 41 -> 9, of which waited for: 31 -> 2; matrix products, arithmetic and copies ran while one was open for 13% -> 19% of each run, Pallas kernels for 0% -> 39%
where the time goes in v1:
time: 536 us; the launch traced here: 525 us
  Pallas kernels  352 us (66%)
  local copies, waits for them, and re-layouts  62.9 us (12%)
  other arithmetic  46.8 us (9%)
  waiting for transfers between devices  30.3 us (6%)
  between operations  14.4 us (3%)
  starting transfers between devices  11.7 us (2%)
  blocking collectives  7.17 us (1%)
    pallas_call x4, Pallas kernels, call(): pl.pallas_call(kernel, out_shape=[jax.ShapeDtypeStruct(s, d) for s, d in...  168 us
    pallas_call x1, Pallas kernels, allreduce(): pl.pallas_call(functools.partial(ar_kernel, ring), out_shape=[jax.ShapeDt...  149 us
    unnamed x45, local copies, waits for them, and re-layouts  46.3 us
    pallas_call x2, Pallas kernels, exchange(): pl.pallas_call(functools.partial(kernel, n), out_shape=[jax.ShapeDtypeStr...  35 us
    all_gather x3, waiting for transfers between devices, body(): both = lambda w: lax.all_gather(w, 'section', axis=0, tiled=True)  28.3 us
    concatenate x1, other arithmetic, body(): jnp.concatenate([g_conv, g_rest, extra(dgbi2, jnp.concatenate([dgbm2, dgb...  18.6 us
  transfers between devices with their start and end apart: 9, of which 2 were waited for; matrix products, arithmetic and copies ran while one was open for 19% of the time, Pallas kernels for 39%

profile of v1, /device:TPU:0, one launch (start us, length us, event | category | flops | bytes accessed | tf_op | source)
XLA Modules:
  0.0 525.3 jit_solution(11104457333552482423)
XLA Ops:
  7.2 0.7 all-gather.10.cloned.1.call-update
  7.9 0.0 all-gather.6.cloned.1.call-start
  8.0 0.7 all-gather.6.cloned.1.call-update
  8.7 0.0 all-gather.8.cloned.1.call-start
  8.8 0.7 all-gather.8.cloned.1.call-update
  9.5 0.1 dynamic-slice_bitcast_fusion.1
  9.6 1.0 copy-done.3
  10.7 5.0 collective-permute-start
  15.7 1.3 collective-permute-start.1
  17.1 0.8 broadcast_in_dim.11.refs_14_
  17.9 0.9 broadcast_in_dim.12.refs_15_
  18.8 0.2 copy.52
  19.0 0.8 pad.13.refs_8_
  19.8 1.8 all_gather.27
  21.6 1.8 all_gather.26
  23.4 1.8 all-gather.1
  25.2 1.8 all-gather
  27.0 0.1 fusion.12
  27.1 0.6 slice_bitcast_fusion.2
  27.7 0.6 slice_bitcast_fusion.3
  28.3 2.5 dynamic-slice_bitcast_fusion.refs_1_.refs_3_
  30.8 0.6 slice_bitcast_fusion.4
  31.4 0.6 slice_bitcast_fusion.5
  32.0 0.6 pad_add_fusion.refs_2_.refs_13_
  32.5 1.2 pad_maximum_fusion.refs_0_
  33.8 5.9 %all-gather.6.cloned.1.call-done.refs_3_.refs_6_.refs_8_ = bf16[2,1280,640]{2,1,0:T(8,128)(2,1)} async-done(((bf16[1,1280,640]{2,1,0:T(8,128)(2,1)}), bf16[2,1280,640]{2,1,0:T(8,128)(2,1)}) %all-gather.6.cloned.1.call-update) | async-done | bytes 3276816 | tf_op jit(solution)/shard_map/all_gather | solution.py:636
  39.7 22.3 %all-gather.8.cloned.1.call-done.refs_4_.refs_2_.refs_9_ = bf16[2,5,640,640]{3,2,1,0:T(8,128)(2,1)} async-done(((bf16[1,5,640,640]{3,2,1,0:T(8,128)(2,1)}), bf16[2,5,640,640]{3,2,1,0:T(8,128)(2,1)}) %all-gather.8.cloned.1.call-update) | async-done | bytes 8192016 | tf_op jit(solution)/shard_map/all_gather | solution.py:636
  62.0 55.4 %shard_map.204 = (bf16[2,256,1280]{2,1,0:T(8,128)(2,1)}, bf16[2,256,1280]{2,1,0:T(8,128)(2,1)}, f32[2,256,640]{2,1,0:T(8,128)}, f32[2,304,640]{2,1,0:T(8,128)}, ...) custom-call(bf16[2,288,1280]{2,1,0:T(8,128)(2,1)} %pad_maximum_fusio, ...), custom_call_target="tpu_custom_call" | custom-call | tf_op jit(solution)/shard_map/pallas_call | solution.py:622
  117.4 17.7 %shard_map.205 = (bf16[4,2,64,640]{3,2,1,0:T(8,128)(2,1)}, bf16[4,2,64,640]{3,2,1,0:T(8,128)(2,1)}) custom-call(bf16[2,2,2,64,640]{4,3,2,1,0:T(8,128)(2,1)} %bitcast.80, bf16[2,2,2,64,640]{4,3,2,1,0:T(8,128)(2,1)} %bitcast.81), custom_call_target="tpu_custom_call" | custom-call | tf_op jit(solution)/shard_map/pallas_call | solution.py:599
  135.1 23.2 %shard_map.206 = (bf16[512,640]{1,0:T(8,128)(2,1)}, bf16[512,640]{1,0:T(8,128)(2,1)}, f32[2,8,640]{2,1,0:T(8,128)}, bf16[2,500,16,128]{3,2,1,0:T(8,128)(2,1)}) custom-call(bf16[512,640]{1,0:T(8,128)(2,1)} %bitcast.78, bf16[512,640]{1,0:T(8,128)(2,1)} %bitcast.79, bf16[2,5,640,640]{3,2,1,0:T(8,128)(2,1)} %all-gather.8.cloned.1.call-done.refs_4_.refs_2_.refs_9_, ...), custom_call_target="tpu_custom_call" | custom-call | tf_op jit(solution)/shard_map/pallas_call | solution.py:622
  158.3 17.4 %shard_map.207 = (bf16[2,2,2,64,640]{4,3,2,1,0:T(8,128)(2,1)}, bf16[2,2,2,64,640]{4,3,2,1,0:T(8,128)(2,1)}) custom-call(bf16[4,2,64,640]{3,2,1,0:T(8,128)(2,1)} %bitcast.82, bf16[4,2,64,640]{3,2,1,0:T(8,128)(2,1)} %bitcast.83), custom_call_target="tpu_custom_call" | custom-call | tf_op jit(solution)/shard_map/pallas_call | solution.py:599
  175.7 34.3 %shard_map.208 = (bf16[2,256,1280]{2,1,0:T(8,128)(2,1)}, bf16[2,256,1280]{2,1,0:T(8,128)(2,1)}, f32[2,8,1280]{2,1,0:T(8,128)}, f32[2,8,640]{2,1,0:T(8,128)}, f32...) custom-call(bf16[2,256,1280]{2,1,0:T(8,128)(2,1)} %get-tuple-element.40.refs_0_, bf16[2,256,640]{2,1,0:T(8,128)(2,1)} %bitcast.76, ...), custom_call_target="tpu_custom_call" | custom-call | tf_op jit(solution)/shard_map/pallas_call | solution.py:622
  210.0 0.8 maximum_reduce_fusion
  210.8 0.9 reduce_sum.54
  211.7 0.7 reduce_sum.56
  212.4 0.9 fusion.14
  213.4 3.0 collective-permute-start.3
  216.4 1.3 collective-permute-start.4
  217.7 2.7 select_bitcast_fusion.1
  220.5 1.0 collective-permute-start.2
  221.5 18.6 %maximum_maximum_fusion.1 = bf16[2,912,16,128]{3,2,1,0:T(8,128)(2,1)} fusion(bf16[1,12,16,128]{3,2,1,0:T(8,128)(2,1)S(1)} %bitcast.84, bf16[2,400,16,128]{3,2,1,0:T(8,128)(2,1)} %get-tuple-element.63, bf16[2,500,16,128]{3,2,1,0:T(8,128)(2,1)S(1)} %copy-done.8), kind=kLoop, calls=%fused_computation.1 | loop fusion | flops 11206656 | bytes 14893056 | tf_op jit(solution)/shard_map/concatenate | solution.py:693
  240.1 1.2 pad_maximum_fusion.1.refs_1_
  241.3 55.5 %shard_map.209 = (bf16[2,256,1280]{2,1,0:T(8,128)(2,1)}, f32[2,8,1280]{2,1,0:T(8,128)}, f32[4,8,640]{2,1,0:T(8,128)}, bf16[2,900,16,128]{3,2,1,0:T(8,128)(2,1)}) custom-call(bf16[2,288,1280]{2,1,0:T(8,128)(2,1)} %pad_maximum_fusion.refs_0_, bf16[2,288,1280]{2,1,0:T(8,128)(2,1)} %pad_maximum_fusion.1.refs_1_, s32[3]{0:T(128)} %pad_add_fusion.refs_2_.refs_13_, ...), custom_call_target="tpu_custom_call" | custom-call | tf_op jit(solution)/shard_map/pallas_call | solution.py:622
  296.8 0.9 reduce_sum.51
  297.7 0.9 reduce_sum.52
  298.6 3.0 select_bitcast_fusion
  301.6 8.5 %maximum_maximum_fusion = bf16[2,912,16,128]{3,2,1,0:T(8,128)(2,1)} fusion(bf16[1,12,16,128]{3,2,1,0:T(8,128)(2,1)S(1)} %bitcast.85, bf16[2,900,16,128]{3,2,1,0:T(8,128)(2,1)} %get-tuple-element.59), kind=kLoop, calls=%fused_computation | loop fusion | flops 7471104 | bytes 14893056 | tf_op jit(solution)/shard_map/concatenate | solution.py:694
  310.1 148.6 %shard_map.210 = (bf16[2,6,152,16,128]{4,3,2,1,0:T(8,128)(2,1)}, bf16[12,16,128]{2,1,0:T(8,128)(2,1)}) custom-call(bf16[2,6,152,16,128]{4,3,2,1,0:T(8,128)(2,1)} %bitcast.70, bf16[2,6,152,16,128]{4,3,2,1,0:T(8,128)(2,1)} %bitcast.69), custom_call_target="tpu_custom_call" | custom-call | tf_op jit(solution)/shard_map/pallas_call | solution.py:510
  458.7 5.4 %fusion.13 = (f32[2,200,16,128]{3,2,1,0:T(8,128)}, f32[2,200,16,128]{3,2,1,0:T(8,128)}) fusion(bf16[2,912,16,128]{3,2,1,0:T(8,128)(2,1)} %bitcast.71), kind=kLoop, calls=%fused_computation.44 | loop fusion | bytes 13107200 | tf_op jit(solution)/shard_map/slice | solution.py:706
  464.2 0.6 slice.134
  464.9 9.5 %copy.66 = f32[5,2,320,5,128]{4,3,2,1,0:T(8,128)} copy(f32[5,2,320,5,128]{4,2,3,0,1:T(8,128)S(1)} %bitcast.68) | data formatting | bytes 16384000
  474.4 11.6 %reshape.258 = f32[1,5,640,640]{3,2,1,0:T(8,128)} reshape(f32[5,2,320,5,128]{4,3,2,1,0:T(8,128)} %copy.66) | data formatting | bytes 16384000
  486.0 6.3 %copy.65 = f32[2,640,5,128]{3,2,1,0:T(8,128)} copy(f32[2,640,5,128]{3,1,2,0:T(8,128)} %bitcast.75) | data formatting | bytes 6553600
  492.2 5.2 reshape.257
  497.5 6.3 %copy.67 = f32[2,320,10,128]{3,2,1,0:T(8,128)} copy(f32[2,320,10,128]{3,1,2,0:T(8,128)} %bitcast.74) | data formatting | bytes 6553600
  503.7 4.9 reshape.259
  508.6 0.6 copy.60
  509.2 0.6 copy.61
  509.8 0.6 slice.101
  510.4 0.6 slice.103
  511.0 0.7 slice.110
  511.7 0.5 slice_convert_fusion
  512.3 3.1 fusion
  515.4 3.1 fusion.1
  (62 shorter events, 0.4 us)
Async XLA Ops:
  7.2 2.3 copy-start
  7.2 26.6 %all-gather.10.cloned.1.call-start = ((), (), s32[]{:S(2)}) async-start(), calls=%async_computation.2 | async-start | bytes 4915200 | tf_op jit(solution)/shard_map/all_gather | solution.py:636
  7.9 31.8 %all-gather.6.cloned.1.call-start = ((), (), s32[]{:S(2)}) async-start(), calls=%async_computation | async-start | bytes 4915200 | tf_op jit(solution)/shard_map/all_gather | solution.py:636
  8.7 8.3 %copy-start.13 = (bf16[1,2,640]{2,1,0:T(2,128)(2,1)S(1)}, bf16[1,2,640]{2,1,0:T(2,128)(2,1)}, u32[]{:S(2)}) copy-start(bf16[1,2,640]{2,1,0:T(2,128)(2,1)} %param.20) | copy-start | bytes 7684
  8.7 8.3 %copy-start.14 = (bf16[1,2,640]{2,1,0:T(2,128)(2,1)S(1)}, bf16[1,2,640]{2,1,0:T(2,128)(2,1)}, u32[]{:S(2)}) copy-start(bf16[1,2,640]{2,1,0:T(2,128)(2,1)} %param.19) | copy-start | bytes 7684
  8.7 8.3 %copy-start.15 = (s32[4,1,256]{2,1,0:T(1,128)S(1)}, s32[4,1,256]{2,1,0:T(1,128)}, u32[]{:S(2)}) copy-start(s32[4,1,256]{2,1,0:T(1,128)} %param.16) | copy-start | bytes 12292
  8.7 8.3 %copy-start.16 = (s32[4,1,256]{2,1,0:T(1,128)S(1)}, s32[4,1,256]{2,1,0:T(1,128)}, u32[]{:S(2)}) copy-start(s32[4,1,256]{2,1,0:T(1,128)} %param.15) | copy-start | bytes 12292
  8.7 53.3 %all-gather.8.cloned.1.call-start = ((), (), s32[]{:S(2)}) async-start(), calls=%async_computation.1 | async-start | bytes 12288000 | tf_op jit(solution)/shard_map/all_gather | solution.py:636
  9.5 9.3 %copy-start.9 = (bf16[1280,30]{0,1:T(8,128)(2,1)S(1)}, bf16[1280,30]{0,1:T(8,128)(2,1)}, u32[]{:S(2)}) copy-start(bf16[1280,30]{0,1:T(8,128)(2,1)} %param.24) | copy-start | bytes 230404
  9.5 13.9 %copy-start.11 = (bf16[1,1280]{1,0:T(2,128)(2,1)S(1)}, bf16[1,1280]{1,0:T(2,128)(2,1)}, u32[]{:S(2)}) copy-start(bf16[1,1280]{1,0:T(2,128)(2,1)} %param.18) | copy-start | bytes 7684
  9.5 15.7 %copy-start.12 = (bf16[1,1280]{1,0:T(2,128)(2,1)S(1)}, bf16[1,1280]{1,0:T(2,128)(2,1)}, u32[]{:S(2)}) copy-start(bf16[1,1280]{1,0:T(2,128)(2,1)} %param.17) | copy-start | bytes 7684
  9.5 17.5 %copy-start.17 = (s32[4,1]{0,1:T(1,128)S(1)}, s32[4,1]{0,1:T(1,128)}, u32[]{:S(2)}) copy-start(s32[4,1]{0,1:T(1,128)} %param.14) | copy-start | bytes 52
  9.6 1.1 copy-start.3
  10.7 21.9 %copy-start.4 = (bf16[2,256,1280]{2,1,0:T(8,128)(2,1)S(1)}, bf16[2,256,1280]{2,1,0:T(8,128)(2,1)}, u32[]{:S(2)}) copy-start(bf16[2,256,1280]{2,1,0:T(8,128)(2,1)} %copy-done.3) | copy-start | bytes 3932164
  10.7 21.8 %collective-permute-start = (bf16[2,16,1280]{2,1,0:T(8,128)(2,1)S(1)}, bf16[2,16,1280]{2,1,0:T(8,128)(2,1)S(1)}, u32[]{:S(2)}, u32[]{:S(2)}) collective-permute-start(bf16[2,16,1280]{2,1,0:T(8,128)(2,1)S(1)} %get-tuple-element.118), channel_id=1, source_target_pairs={{0,1},{1,2},{2,3},{4,5},{5,6},{6,7},{8,9},{9,10},{10,11},{12,13},{... | collective-permute-start | bytes 245768 | tf_op jit(solution)/shard_map/ppermute | solution.py:648
  15.7 16.9 %collective-permute-start.1 = (bf16[2,16,1280]{2,1,0:T(8,128)(2,1)S(1)}, bf16[2,16,1280]{2,1,0:T(8,128)(2,1)S(1)}, u32[]{:S(2)}, u32[]{:S(2)}) collective-permute-start(bf16[2,16,1280]{2,1,0:T(8,128)(2,1)S(1)} %get-tuple-element.119), channel_id=1, source_target_pairs={{1,0},{2,1},{3,2},{5,4},{6,5},{7,6},{9,8},{10,9},{11,10},{13,12},{... | collective-permute-start | bytes 245768 | tf_op jit(solution)/shard_map/ppermute | solution.py:649
  175.6 34.3 %copy-start.10 = (f32[2,8,640]{2,1,0:T(8,128)S(1)}, f32[2,8,640]{2,1,0:T(8,128)}, u32[]{:S(2)}) copy-start(f32[2,8,640]{2,1,0:T(8,128)} %get-tuple-element.66) | copy-start | bytes 122884
  175.6 42.1 %copy-start.6 = (bf16[2,256,1280]{2,1,0:T(8,128)(2,1)S(1)}, bf16[2,256,1280]{2,1,0:T(8,128)(2,1)}, u32[]{:S(2)}) copy-start(bf16[2,256,1280]{2,1,0:T(8,128)(2,1)} %get-tuple-element.40.refs_0_) | copy-start | bytes 3932164
  213.4 26.7 %collective-permute-start.3 = (bf16[2,16,1280]{2,1,0:T(8,128)(2,1)S(1)}, bf16[2,16,1280]{2,1,0:T(8,128)(2,1)S(1)}, u32[]{:S(2)}, u32[]{:S(2)}) collective-permute-start(bf16[2,16,1280]{2,1,0:T(8,128)(2,1)S(1)} %get-tuple-element.116), channel_id=1, source_target_pairs={{0,1},{1,2},{2,3},{4,5},{5,6},{6,7},{8,9},{9,10},{10,11},{12,13},{... | collective-permute-start | bytes 245768 | tf_op jit(solution)/shard_map/ppermute | solution.py:648
  216.4 23.7 %collective-permute-start.4 = (bf16[2,16,1280]{2,1,0:T(8,128)(2,1)S(1)}, bf16[2,16,1280]{2,1,0:T(8,128)(2,1)S(1)}, u32[]{:S(2)}, u32[]{:S(2)}) collective-permute-start(bf16[2,16,1280]{2,1,0:T(8,128)(2,1)S(1)} %get-tuple-element.117), channel_id=1, source_target_pairs={{1,0},{2,1},{3,2},{5,4},{6,5},{7,6},{9,8},{10,9},{11,10},{13,12},{... | collective-permute-start | bytes 245768 | tf_op jit(solution)/shard_map/ppermute | solution.py:649
  217.7 3.8 copy-start.8
  220.5 291.8 %collective-permute-start.2 = (bf16[2,256,1280]{2,1,0:T(8,128)(2,1)}, bf16[2,256,1280]{2,1,0:T(8,128)(2,1)}, u32[]{:S(2)}, u32[]{:S(2)}) collective-permute-start(bf16[2,256,1280]{2,1,0:T(8,128)(2,1)} %get-tuple-element.115), channel_id=1, source_target_pairs={{0,16},{16,0},{1,17},{17,1},{2,18},{18,2},{3,19},{19,3},{4,20},{20... | collective-permute-start | bytes 3932168 | tf_op jit(solution)/shard_map/ppermute | solution.py:715
  221.5 18.6 %copy-start.5 = (bf16[2,256,1280]{2,1,0:T(8,128)(2,1)S(1)}, bf16[2,256,1280]{2,1,0:T(8,128)(2,1)}, u32[]{:S(2)}) copy-start(bf16[2,256,1280]{2,1,0:T(8,128)(2,1)} %get-tuple-element.52) | copy-start | bytes 3932164
  301.6 213.7 %collective-permute-start.5 = (bf16[2,256,1280]{2,1,0:T(8,128)(2,1)}, bf16[2,256,1280]{2,1,0:T(8,128)(2,1)}, u32[]{:S(2)}, u32[]{:S(2)}) collective-permute-start(bf16[2,256,1280]{2,1,0:T(8,128)(2,1)} %get-tuple-element.113), channel_id=1, source_target_pairs={{0,16},{16,0},{1,17},{17,1},{2,18},{18,2},{3,19},{19,3},{4,20},{20... | collective-permute-start | bytes 3932168 | tf_op jit(solution)/shard_map/ppermute | solution.py:715
  458.7 5.5 %copy-start.2 = (bf16[2,6,152,16,128]{4,3,2,1,0:T(8,128)(2,1)S(1)}, bf16[2,6,152,16,128]{4,3,2,1,0:T(8,128)(2,1)}, u32[]{:S(2)}) copy-start(bf16[2,6,152,16,128]{4,3,2,1,0:T(8,128)(2,1)} %get-tuple-element.68) | copy-start | bytes 22413316
  512.3 3.1 copy-start.7
  515.3 3.2 copy-start.1
Sparse Core Ops, SparseCore 0:
  9.6 15.0 all-gather.9
  26.2 13.4 all-gather.5
  41.2 20.7 all-gather.7

commit v2 on v1

v2 whole, which is shorter than its diff:
```python
import functools

import jax
import jax.numpy as jnp
from jax import lax
from jax.experimental import pallas as pl
from jax.experimental.pallas import tpu as pltpu
from jax.sharding import PartitionSpec as P

EPS = 1e-05
BF, F32 = jnp.bfloat16, jnp.float32
MESH = pl.DeviceIdType.MESH
G0 = 0.7978845608028654
G1 = 0.044715
DIL = 2
HALO = 16
CH = 16


def dot(a, b):
    return lax.dot_general(a, b, (((1,), (0,)), ((), ())), preferred_element_type=F32)


def dot_nt(a, b):
    return lax.dot_general(a, b, (((1,), (1,)), ((), ())), preferred_element_type=F32)


def dot_tn(a, b):
    return lax.dot_general(a, b, (((0,), (0,)), ((), ())), preferred_element_type=F32)


def chunks(rows, fn, size=None):
    size = size or (96 if rows % 96 == 0 else 64)

    def one(i, _):
        fn(pl.multiple_of(i * size, size), size)
        return 0

    lax.fori_loop(0, rows // size, one, 0)


def cols(j):
    return pl.ds(j * 128, 128)


def stats(load, n):
    total = load(0)
    for j in range(1, n):
        total = total + load(j)
    mean = jnp.sum(total, axis=-1, keepdims=True) * (1.0 / (128 * n))
    square = None
    for j in range(n):
        d = load(j) - mean
        square = d * d if square is None else square + d * d
    var = jnp.sum(square, axis=-1, keepdims=True) * (1.0 / (128 * n))
    return mean, lax.rsqrt(var + EPS)


def norm_gelu(load, n, gain, shift, store):
    mean, rstd = stats(load, n)
    for j in range(n):
        u = (load(j) - mean) * rstd * gain(j) + shift(j)
        t = jnp.tanh(u * (G0 + (G0 * G1) * (u * u)))
        h = 0.5 * u
        store(j, h + h * t)


def fold(v):
    rows, width = v.shape
    return jnp.sum(v.reshape(rows // 8, 8, width), axis=0)


def norm_gelu_back(load, dy, n, gain, shift, dgain, dshift, hold, store):
    mean, rstd = stats(load, n)
    s1 = s2 = None
    for j in range(n):
        g = gain(j)
        hat = (load(j) - mean) * rstd
        u = hat * g + shift(j)
        w = u * u
        t = jnp.tanh(u * (G0 + (G0 * G1) * w))
        slope = 0.5 + 0.5 * t + u * (1.0 - t * t) * (0.5 * G0 + (1.5 * G0 * G1) * w)
        du = dy(j) * slope
        if dgain is not None:
            dgain[:, cols(j)] += fold(du * hat)
            dshift[:, cols(j)] += fold(du)
        dh = du * g
        hold[0, :, cols(j)] = hat
        hold[1, :, cols(j)] = dh
        p = dh * hat
        s1 = dh if s1 is None else s1 + dh
        s2 = p if s2 is None else s2 + p
    m1 = jnp.sum(s1, axis=-1, keepdims=True) * (1.0 / (128 * n))
    m2 = jnp.sum(s2, axis=-1, keepdims=True) * (1.0 / (128 * n))
    for j in range(n):
        store(j, rstd * (hold[1, :, cols(j)] - m1 - hold[0, :, cols(j)] * m2))


def row(ref, k):
    return lambda j: ref[pl.ds(k, 1), cols(j)]


def view(ref, *at):
    return lambda j: ref[(*at, cols(j))].astype(F32)


def put_grad(g_ref, unit, value, col0=0):
    m, n = value.shape
    per = m // 32
    value = value.astype(BF)
    for j in range(n // 128):
        block = value[:, j * 128 : (j + 1) * 128].reshape(m // 16, 16, 128)
        for h in range(2):
            g_ref[h, pl.ds(unit + (col0 + j) * per, per)] = block[h * per : (h + 1) * per]


OUT0, IN0, CONV0, EXTRA0, UNITS = 0, 200, 400, 900, 912


def put(ref, *at):
    def store(j, v):
        ref[(*at, cols(j))] = v.astype(ref.dtype)

    return store


def positions(first, i, size):
    return first + i + lax.broadcasted_iota(jnp.int32, (size, 1), 0)


def k4(xe, ge, scal, first1, hidden1, sec1, mixed1, third1, w_in1, conv1, w_out1, gi1, bi1, gm1, bm1,
       grad1, dgbi, dgbm, g_ref, he, me, dme, dh, dm, swin, hold):
    base = scal[0]
    rows, D = xe.shape[1:]
    seg, H = grad1.shape[1], hidden1.shape[2]
    nd, nh = D // 128, H // 128
    for ref in (dgbi, dgbm):
        ref[...] = jnp.zeros_like(ref)

    def micro(m, _):
        length = scal[1 + m]
        he[...] = dot_nt(ge[m], w_out1[0])

        def a(i, size):
            r = pl.ds(i + HALO, size)

            def store(j, v):
                v = v.astype(BF)
                dme[r, cols(j)] = v.astype(F32)
                dm[m, pl.ds(i, size), cols(j)] = v

            norm_gelu_back(view(mixed1, m, r), view(he, r), nh, row(gm1, 1), row(bm1, 1), dgbm.at[2], dgbm.at[3], hold, store)

        chunks(seg, a)
        for edge in (0, rows - HALO):
            r = pl.ds(edge, HALO)
            pos = positions(base - HALO, edge, HALO)
            inside = jnp.logical_and(pos >= 0, pos < 1024)

            def store(j, v):
                dme[r, cols(j)] = jnp.where(inside, v, 0.0).astype(BF).astype(F32)

            norm_gelu_back(view(mixed1, m, r), view(he, r), nh, row(gm1, 1), row(bm1, 1), None, None, hold.at[:, pl.ds(0, HALO)], store)
        acc = None
        for k in range(5):
            term = dot_nt(dme[pl.ds(HALO - DIL * (k - 2), seg)].astype(BF), conv1[0, k])
            acc = term if acc is None else acc + term
        he[pl.ds(0, seg)] = acc

        def b(i, size):
            r = pl.ds(i, size)
            pos = positions(base, i, size)
            ds = lambda j: jnp.where(pos < length, he[r, cols(j)], 0.0)
            norm_gelu_back(view(hidden1, m, r), ds, nh, row(gm1, 0), row(bm1, 0), dgbm.at[0], dgbm.at[1], hold, put(dh, m, r))

        chunks(seg, b)
        he[pl.ds(0, seg)] = dot_nt(dh[m], w_in1[0, :H])
        me[...] = dot_nt(dh[m], w_in1[0, H:])

        def c(i, size):
            r, e = pl.ds(i, size), pl.ds(i + HALO, size)
            df = lambda j: he[r, cols(j)] if j < nh else me[r, cols(j - nh)]

            def store(j, v):
                grad1[m, r, cols(j)] = (ge[m, e, cols(j)].astype(F32) + v).astype(BF)

            norm_gelu_back(view(xe, m, e), df, nd, row(gi1, 0), row(bi1, 0), dgbi.at[0], dgbi.at[1], hold, store)

        chunks(seg, c)
        return 0

    lax.fori_loop(0, 2, micro, 0)
    flat = lambda v: v.reshape(2 * seg, v.shape[-1])
    t1 = flat(third1[...])
    for j in range(2):
        g1 = flat(ge[:, pl.ds(HALO, seg), pl.ds(j * H, H)])
        put_grad(g_ref, OUT0, dot_tn(t1, g1), nh * j)
    d1 = flat(dm[...])
    for k in range(5):
        for m in range(2):
            swin[pl.ds(m * seg, seg)] = sec1[m, pl.ds(8 + HALO + DIL * (k - 2), seg)].astype(BF)
        put_grad(g_ref, CONV0 + k * 100, dot_tn(swin[...], d1))
    put_grad(g_ref, IN0, dot_tn(flat(first1[...]), flat(dh[...])))


class Ring:
    def __init__(self, N, PU, QU):
        self.N, self.PU, self.QU, self.U = N, PU, QU, PU + QU
        self.kinds = ["D","P1","P2","PZ1","PZ2","PT1","PT2","PT3","G1","G2","Q1","Q2","X1","X2","X3","X4","QT1","QT2","QT3","F"]
    def scratch(self):
        N2, PU, QU, U = 2*self.N, self.PU, self.QU, self.U
        b = lambda u: pltpu.VMEM((N2, u, 16, 128), BF)
        nk = len(self.kinds)
        return [b(U), b(PU//2), b(PU//4), b(PU//4), b(PU//8), b(QU), b(QU//2), b(QU//4), b(QU//8), b(U),
                pltpu.SemaphoreType.DMA((nk, N2)), pltpu.SemaphoreType.DMA((nk, N2))]
    def bind(self, G, two, one, out, D, RP1, RP2, RZ1, RZ2, RQ1, RQ2, RX1, RX2, R, ss, rs):
        N, PU, QU, U = self.N, self.PU, self.QU, self.U
        c, z, q = lax.axis_index("section"), lax.axis_index("dp"), lax.axis_index("seq")
        xb, yb = lax.rem(q, 2), lax.div(q, 2)
        f = jnp.where(c == 0, xb, yb); s = jnp.where(c == 0, yb, xb)
        qx = xb ^ 1;
        nx = (c, z, yb*2 + 1 - xb); ny = (c, z, (1-yb)*2 + xb)
        n1 = (c, z, jnp.where(c == 0, nx[2], ny[2])); n2 = (c, z, jnp.where(c == 0, ny[2], nx[2]))
        side = lax.div(z, 2)
        zp = (c, side*2 + 1 - lax.rem(z, 2), q)
        far = (c, 3 - z, q)
        peer = (1 - c, z, q)
        inner = jnp.logical_or(z == 1, z == 2)
        outer = jnp.logical_not(inner)
        K = {k: i for i, k in enumerate(self.kinds)}
        def cp(k, i, src, dst, dev):
            return pltpu.make_async_remote_copy(src_ref=src, dst_ref=dst, send_sem=ss.at[K[k], i], recv_sem=rs.at[K[k], i], device_id=dev, device_id_type=MESH)
        ds = pl.ds
        H, Q4, E8 = PU//2, PU//4, PU//8
        h, q4, e8 = QU//2, QU//8, QU//8
        def add(dst, a, *bs):
            acc = a[...].astype(F32)
            for b in bs: acc = acc + b[...].astype(F32)
            dst[...] = acc.astype(BF)
        pq = lambda ff, s2: ds((2*ff + s2)*Q4, Q4)
        pch = lambda k: ds((2*f + s)*Q4 + k*E8, E8)
        def qn(k): return ds(PU + k*h, h)
        def qhalf(k, ff): return ds(PU + k*h + ff*(h//2), h//2)
        def qquart(k, ff, s2): return ds(PU + k*h + (2*ff+s2)*(h//4), h//4)
        near, farc = side, 1 - side
        C = dict(
          D=lambda i: cp("D", i, two.at[1-c, i], D.at[i], peer),
          E=lambda i: cp("D", i, one.at[1-c, i-N], D.at[i], peer),
          W=lambda i: cp("D", i, G.at[i], D.at[i], peer),
          P1=lambda i: cp("P1", i, D.at[i, ds((1-f)*H, H)], RP1.at[i], n1),
          P2=lambda i: cp("P2", i, D.at[i, pq(f, 1-s)], RP2.at[i], n2),
          PZ1=lambda i: cp("PZ1", i, D.at[i, pq(f, s)], RZ1.at[i], zp),
          PZ2=lambda i: cp("PZ2", i, D.at[i, pch(farc)], RZ2.at[i], far),
          PT1=lambda i: cp("PT1", i, R.at[i, pch(near)], R.at[i, pch(near)], far),
          PT2=lambda i: cp("PT2", i, R.at[i, pch(near)], R.at[i, pch(near)], zp),
          PT3=lambda i: cp("PT3", i, R.at[i, pch(farc)], R.at[i, pch(farc)], zp),
          G1=lambda i: cp("G1", i, R.at[i, pq(f, s)], R.at[i, pq(f, s)], n2),
          G2=lambda i: cp("G2", i, R.at[i, ds(f*H, H)], R.at[i, ds(f*H, H)], n1),
          Q1=lambda i: cp("Q1", i, D.at[i, ds(PU, QU)], RQ1.at[i], zp),
          Q2=lambda i: cp("Q2", i, D.at[i, qn(farc)], RQ2.at[i], far),
          X1=lambda i: cp("X1", i, D.at[i, qhalf(near, 1-f)], RX1.at[i], n1),
          X2=lambda i: cp("X2", i, D.at[i, qquart(near, f, 1-s)], RX2.at[i], n2),
          X3=lambda i: cp("X3", i, R.at[i, qquart(near, f, s)], R.at[i, qquart(near, f, s)], n2),
          X4=lambda i: cp("X4", i, R.at[i, qhalf(near, f)], R.at[i, qhalf(near, f)], n1),
          QT1=lambda i: cp("QT1", i, R.at[i, qn(near)], R.at[i, qn(near)], far),
          QT2=lambda i: cp("QT2", i, R.at[i, qn(near)], R.at[i, qn(near)], zp),
          QT3=lambda i: cp("QT3", i, R.at[i, qn(farc)], R.at[i, qn(farc)], zp),
        )
        def mine(i): return jnp.where(i < N, 1, 0) == c
        def slot(i): return jnp.where(i < N, i, i - N)
        Fr = lambda i: cp("F", i, R.at[i], out.at[c, slot(i)], peer)
        Fl = lambda i: pltpu.make_async_copy(R.at[i], out.at[c, slot(i)], ss.at[K["F"], i])
        def S0(i):
            @pl.when(i < N)
            def _(): C["D"](i).start()
            @pl.when(i >= N)
            def _(): C["E"](i).start()
        def S1(i):
            C["W"](i).wait()
            add(D.at[i], D.at[i], G.at[i])
            C["P1"](i).start()
            @pl.when(outer)
            def _(): C["Q1"](i).start()
        def S2(i):
            @pl.when(inner)
            def _():
                C["Q1"](i).wait_recv()
                add(D.at[i, qn(farc)], D.at[i, qn(farc)], RQ1.at[i, ds(farc*h, h)])
                C["Q2"](i).start()
            C["P1"](i).wait()
            add(D.at[i, ds(f*H, H)], D.at[i, ds(f*H, H)], RP1.at[i])
            C["P2"](i).start()
            @pl.when(outer)
            def _(): C["Q1"](i).wait_send()
        def S3(i):
            C["P2"](i).wait()
            add(D.at[i, pq(f, s)], D.at[i, pq(f, s)], RP2.at[i])
            @pl.when(outer)
            def _(): C["PZ1"](i).start()
            @pl.when(inner)
            def _():
                C["Q2"](i).wait()
                add(D.at[i, qn(near)], D.at[i, qn(near)], RQ1.at[i, ds(near*h, h)], RQ2.at[i])
                C["X1"](i).start()
        def S4(i):
            @pl.when(inner)
            def _():
                C["PZ1"](i).wait_recv()
                add(D.at[i, pch(farc)], D.at[i, pch(farc)], RZ1.at[i, ds(farc*E8, E8)])
                C["PZ2"](i).start()
                C["X1"](i).wait()
                add(D.at[i, qhalf(near, f)], D.at[i, qhalf(near, f)], RX1.at[i])
                C["X2"](i).start()
            @pl.when(outer)
            def _(): C["PZ1"](i).wait_send()
        def S5(i):
            @pl.when(inner)
            def _():
                C["PZ2"](i).wait()
                add(R.at[i, pch(near)], D.at[i, pch(near)], RZ1.at[i, ds(near*E8, E8)], RZ2.at[i])
                C["PT1"](i).start(); C["PT2"](i).start()
                C["X2"](i).wait()
                add(R.at[i, qquart(near, f, s)], D.at[i, qquart(near, f, s)], RX2.at[i])
                C["X3"](i).start()
        def S6(i):
            @pl.when(inner)
            def _():
                C["PT1"](i).wait()
                C["PT3"](i).start()
                C["X3"](i).wait()
                C["X4"](i).start()
        def S7(i):
            @pl.when(outer)
            def _():
                C["PT2"](i).wait_recv(); C["PT3"](i).wait_recv()
            @pl.when(inner)
            def _():
                C["PT2"](i).wait_send(); C["PT3"](i).wait_send()
            C["G1"](i).start()
            @pl.when(inner)
            def _():
                C["X4"](i).wait()
                C["QT1"](i).start(); C["QT2"](i).start()
        def S8(i):
            C["G1"](i).wait()
            C["G2"](i).start()
            @pl.when(inner)
            def _():
                C["QT1"](i).wait()
                C["QT3"](i).start()
        def S9(i):
            C["G2"](i).wait()
            @pl.when(outer)
            def _():
                C["QT2"](i).wait_recv(); C["QT3"](i).wait_recv()
            @pl.when(inner)
            def _():
                C["QT2"](i).wait_send(); C["QT3"](i).wait_send()
            m = mine(i)
            @pl.when(m)
            def _(): Fl(i).start()
            @pl.when(jnp.logical_not(m))
            def _(): Fr(i).start()
        def S10(i):
            m = mine(i)
            @pl.when(m)
            def _(): Fl(i).wait()
            @pl.when(jnp.logical_not(m))
            def _(): Fr(i).wait_send()
        stages = [S0,S1,S2,S3,S4,S5,S6,S7,S8,S9,S10]
        def step(t):
            for si in range(len(stages)):
                i = t - si
                @pl.when(jnp.logical_and(i >= 0, i < 2*N))
                def _(): stages[si](i)
        def recv_final():
            def body(j, _):
                i = jnp.where(c == 1, j, j + N)
                Fr(i).wait_recv()
                return 0
            lax.fori_loop(0, N, body, 0)
        def barrier():
            b = pltpu.get_barrier_semaphore()
            for d in (peer, n1, n2, zp):
                pl.semaphore_signal(b, inc=1, device_id=d, device_id_type=MESH)
            @pl.when(inner)
            def _():
                pl.semaphore_signal(b, inc=1, device_id=far, device_id_type=MESH)
                pl.semaphore_wait(b, 5)
            @pl.when(outer)
            def _(): pl.semaphore_wait(b, 4)
        self.R = R
        self.barrier, self.step, self.recv_final, self.iters = barrier, step, recv_final, 2*N + len(stages) - 1


def ar_kernel(ring, one, two, out, cnt, G, gsem, *scr):
    N = ring.N
    c = lax.axis_index("section")
    loads = [pltpu.make_async_copy(two.at[c], G.at[pl.ds(0, N)], gsem.at[0]), pltpu.make_async_copy(one.at[c], G.at[pl.ds(N, N)], gsem.at[1])]
    for cp in loads:
        cp.start()
    ring.bind(G, two, one, out, *scr)
    ring.barrier()
    for cp in loads:
        cp.wait()

    def body(t, _):
        ring.step(t)
        return 0

    lax.fori_loop(0, ring.iters, body, 0)
    ring.recv_final()
    cnt[...] = ring.R[N - 1, pl.ds(ring.U - 12, 12)]


def allreduce(one, two, N, PU, QU):
    ring = Ring(N, PU, QU)
    U = PU + QU
    any_ = pl.BlockSpec(memory_space=pl.ANY)
    split = lambda g: g.reshape(2, N, U, 16, 128)
    return pl.pallas_call(
        functools.partial(ar_kernel, ring),
        out_shape=[jax.ShapeDtypeStruct((2, N, U, 16, 128), BF), jax.ShapeDtypeStruct((12, 16, 128), BF)],
        in_specs=[any_, any_],
        out_specs=[any_, pl.BlockSpec(memory_space=pltpu.VMEM)],
        scratch_shapes=[pltpu.VMEM((2 * N, U, 16, 128), BF), pltpu.SemaphoreType.DMA((2,))] + ring.scratch(),
        compiler_params=pltpu.CompilerParams(collective_id=0, has_side_effects=True, vmem_limit_bytes=60 * 2**20),
    )(split(one), split(two))


def plane(c, z, q):
    out = []
    for i in range(1, 8):
        n = lax.rem(c * 4 + q + i, 8)
        out.append((lax.div(n, 4), z, lax.rem(n, 4)))
    return out


def greet(ids):
    barrier = pltpu.get_barrier_semaphore()
    for d in ids:
        pl.semaphore_signal(barrier, inc=1, device_id=d, device_id_type=MESH)
    pl.semaphore_wait(barrier, len(ids))


def remote(src, dst, ss, rs, dev):
    return pltpu.make_async_remote_copy(src_ref=src, dst_ref=dst, send_sem=ss, recv_sem=rs, device_id=dev, device_id_type=MESH)


def both_ways(cond, here, there):
    @pl.when(cond)
    def _():
        here()

    @pl.when(jnp.logical_not(cond))
    def _():
        there()


class Spread:
    def __init__(self, c, z, q, ss, rs, ls):
        self.c, self.z, self.q, self.ss, self.rs, self.ls = c, z, q, ss, rs, ls

    def go(self, a, src, dst, m, start):
        c, z, q = self.c, self.z, self.q
        for h in range(2):
            s, d, j = src.at[m, :, h], dst(q), 2 * m + h
            far = remote(s, d, self.ss.at[a, j], self.rs.at[a, q], (jnp.int32(h), z, 2 * c + m))
            near = pltpu.make_async_copy(s, d, self.ls.at[a])
            both_ways(jnp.logical_and(h == c, 2 * c + m == q), near.start if start else near.wait, far.start if start else far.wait_send)

    def arrive(self, a, src, dst):
        c, z, q = self.c, self.z, self.q
        fc = lax.div(q, 2)
        for p in range(4):
            @pl.when(jnp.logical_not(jnp.logical_and(c == fc, p == q)))
            def _():
                remote(src.at[0, :, 0], dst(p), self.ss.at[a, 0], self.rs.at[a, p], (fc, z, jnp.int32(p))).wait_recv()

    def back(self, a, src, dst, p, start):
        c, z, q = self.c, self.z, self.q
        tc, slot = lax.div(q, 2), lax.rem(q, 2)
        s, d = src.at[pl.ds(2 * p, 2)], dst.at[slot, :, c]
        far = remote(s, d, self.ss.at[a, p], self.rs.at[a, 2 * slot + c], (tc, z, jnp.int32(p)))
        near = pltpu.make_async_copy(s, d, self.ls.at[a])
        both_ways(jnp.logical_and(tc == c, p == q), near.start if start else near.wait, far.start if start else far.wait_send)

    def back_arrive(self, a, src, dst, m):
        c, z, q = self.c, self.z, self.q
        for h in range(2):
            @pl.when(jnp.logical_not(jnp.logical_and(h == c, 2 * c + m == q)))
            def _():
                remote(src.at[pl.ds(0, 2)], dst.at[m, :, h], self.ss.at[a, 0], self.rs.at[a, 2 * m + h], (jnp.int32(h), z, 2 * c + m)).wait_recv()


def edges(ref, m, seg, ss, rs, z, q, c):
    before = remote(ref.at[m, pl.ds(HALO, HALO)], ref.at[m, pl.ds(HALO + seg, HALO)], ss.at[0, m], rs.at[0, m], (c, z, q - 1))
    after = remote(ref.at[m, pl.ds(seg, HALO)], ref.at[m, pl.ds(0, HALO)], ss.at[1, m], rs.at[1, m], (c, z, q + 1))
    return ((q > 0, q < 3, before), (q < 3, q > 0, after))


def front(lengths, inputs, cot_all, params, w_in, conv_w, w_out, dec, mask, types,
          act, xe_o, ge_o, first1_o, hidden1_o, sec1_o, mixed1_o, third1_o, w_in1_o, conv1_o, w_out1_o, g_o, dgbi, dgbm, dgb, counts,
          WI, WC, WO, PR, xe, cot, out1, first1, hidden1, sec1, mixed1, third1, first2, hidden2, sec2, dth2, sp, dthr, thirdr, dpad, dsecr,
          third2, dsec2, out2, ge, G, fe, he, me, mx, dh, hold,
          ws, wr, wl, xs, xr, xl, ss, rs, ls, gs, gr, os_, acs, acr):
    c, z, q = lax.axis_index("section"), lax.axis_index("dp"), lax.axis_index("seq")
    peer = (1 - c, z, q)
    seg, D = cot.shape[1:]
    H = mixed1.shape[2]
    nd, nh = D // 128, H // 128
    rows = seg + 2 * HALO
    base = q * seg
    own = [pltpu.make_async_copy(inputs.at[2 * c + m, 0], xe.at[m, pl.ds(HALO, seg)], xl.at[m]) for m in range(2)]
    own += [pltpu.make_async_copy(cot_all.at[2 * c + m, 0], cot.at[m], xl.at[2 + m]) for m in range(2)]
    mats = [(params, PR.at[c]), (w_in.at[0], WI.at[c])] + [(conv_w.at[0, k], WC.at[c, k]) for k in range(5)] + [(w_out.at[0], WO.at[c])]
    loads = [pltpu.make_async_copy(s, d, wl.at[i]) for i, (s, d) in enumerate(mats)]
    for cp in own[:2] + loads + own[2:]:
        cp.start()
    greet(plane(c, z, q))
    sends = [remote(s, d, ws.at[i], wr.at[i], peer) for i, (s, d) in enumerate(mats)]
    halos = []
    for m in range(2):
        x = inputs.at[2 * c + m, 0]
        halos.append((q > 0, q < 3, remote(x.at[pl.ds(0, HALO)], xe.at[m, pl.ds(HALO + seg, HALO)], xs.at[0, m], xr.at[0, m], (c, z, q - 1))))
        halos.append((q < 3, q > 0, remote(x.at[pl.ds(seg - HALO, HALO)], xe.at[m, pl.ds(0, HALO)], xs.at[1, m], xr.at[1, m], (c, z, q + 1))))
    for cond, _, cp in halos:
        pl.when(cond)(cp.start)
    for cp in sends:
        cp.start()

    @pl.when(q == 0)
    def _():
        xe[:, pl.ds(0, HALO)] = jnp.zeros((2, HALO, D), BF)
        ge[:, pl.ds(0, HALO)] = jnp.zeros((2, HALO, D), BF)

    @pl.when(q == 3)
    def _():
        xe[:, pl.ds(HALO + seg, HALO)] = jnp.zeros((2, HALO, D), BF)
        ge[:, pl.ds(HALO + seg, HALO)] = jnp.zeros((2, HALO, D), BF)

    def have(i):
        loads[i].wait()
        sends[i].wait_recv()

    for ref in (dgbi, dgbm, dgb, counts):
        ref[...] = jnp.zeros_like(ref)
    zero = jnp.zeros((2, 64, H), BF)
    for ref in (sp, dpad):
        ref[pl.ds(0, 2)] = zero
        ref[pl.ds(10, 2)] = zero
    sec1[:, pl.ds(0, 8)] = jnp.zeros((2, 8, H), F32)
    sec1[:, pl.ds(rows + 8, 8)] = jnp.zeros((2, 8, H), F32)
    spread = Spread(c, z, q, ss, rs, ls)
    sp_at = lambda p: sp.at[pl.ds(2 + 2 * p, 2)]
    dthr_at = lambda p: dthr.at[pl.ds(2 * p, 2)]
    gi, bi = lambda l: row(PR.at[l], 0), lambda l: row(PR.at[l], 1)
    gm = lambda l, k: (lambda j: PR[l, pl.ds(2, 1), cols(k * nh + j)])
    bm = lambda l, k: (lambda j: PR[l, pl.ds(3, 1), cols(k * nh + j)])
    out_sem = [0]

    def out_copy(src, dst):
        cp = pltpu.make_async_copy(src, dst, os_.at[out_sem[0]])
        out_sem[0] += 1
        return cp

    have(0)
    for m in range(2):
        own[m].wait()
    for _, cond, cp in halos:
        pl.when(cond)(cp.wait_recv)
    have(1)

    def forward(m, _):
        length = lengths[2 * c + m]

        def a(i, size):
            r = pl.ds(i, size)
            norm_gelu(view(xe, m, r), nd, gi(0), bi(0), put(fe, r))

        chunks(rows, a)
        first1[m] = fe[pl.ds(HALO, seg)]
        he[...] = dot(fe[...], WI[0])
        hidden1[m] = he[pl.ds(HALO, seg)]

        def b(i, size):
            pos = positions(base - HALO, i, size)
            keep = jnp.logical_and(pos >= 0, pos < length)

            def store(j, v):
                sec1[m, pl.ds(i + 8, size), cols(j)] = jnp.where(keep, v, 0.0).astype(BF).astype(F32)

            norm_gelu(view(he, pl.ds(i, size)), nh, gm(0, 0), bm(0, 0), store)

        chunks(rows, b)

        @pl.when(m == 0)
        def _():
            for k in range(5):
                have(2 + k)

        acc = None
        for k in range(5):
            term = dot(sec1[m, pl.ds(8 + DIL * (k - 2), rows)].astype(BF), WC[0, k])
            acc = term if acc is None else acc + term
        mixed1[m] = acc

        def e(i, size):
            norm_gelu(view(mixed1, m, pl.ds(i + HALO, size)), nh, gm(0, 1), bm(0, 1), put(third1, m, pl.ds(i, size)))

        chunks(seg, e)

        @pl.when(m == 0)
        def _():
            have(7)

        he[pl.ds(0, seg)] = dot(third1[m], WO[0, :, :H])
        me[...] = dot(third1[m], WO[0, :, H:])

        def d(i, size):
            r = pl.ds(i, size)
            for j in range(nd):
                br = he[r, cols(j)] if j < nh else me[r, cols(j - nh)]
                out1[m, r, cols(j)] = (xe[m, pl.ds(i + HALO, size), cols(j)].astype(F32) + br).astype(BF)
            norm_gelu(view(out1, m, r), nd, gi(1), bi(1), put(first2, m, r))

        chunks(seg, d)
        hidden2[m] = dot(first2[m], WI[1])

        def f(jj, _):
            i = pl.multiple_of(jj * 64, 64)
            pos = positions(base, i, 64)

            def store(j, v):
                sec2[m, lax.div(jj, 2), lax.rem(jj, 2), :, cols(j)] = jnp.where(pos < length, v, 0.0).astype(BF)

            norm_gelu(view(hidden2, m, pl.ds(i, 64)), nh, gm(1, 0), bm(1, 0), store)
            return 0

        lax.fori_loop(0, seg // 64, f, 0)
        spread.go(0, sec2, sp_at, m, True)
        return 0

    lax.fori_loop(0, 2, forward, 0)
    for m in range(2):
        own[2 + m].wait()

    def third_grad(m, _):
        dth2[m] = dot_nt(cot[m], WO[1]).astype(BF).reshape(2, 2, 64, H)
        spread.go(1, dth2, dthr_at, m, True)
        return 0

    lax.fori_loop(0, 2, third_grad, 0)
    saves = [out_copy(s, d) for s, d in ((xe, xe_o), (first1, first1_o), (hidden1, hidden1_o), (sec1, sec1_o), (mixed1, mixed1_o),
                                         (third1, third1_o), (WI.at[0], w_in1_o), (WC.at[0], conv1_o), (WO.at[0], w_out1_o))]
    for cp in saves:
        cp.start()

    def place(i, src, layer):
        here = out_copy(src, act.at[pl.ds(2 * c, 2)])
        there = remote(src, act.at[pl.ds(2 * c, 2)], acs.at[i], acr.at[0], peer)
        both_ways(c == layer, here.start, there.start)
        return lambda: both_ways(c == layer, here.wait, there.wait_send)

    done1 = place(0, out1, 0)
    for m in range(2):
        spread.go(0, sec2, sp_at, m, False)
    spread.arrive(0, sec2, sp_at)

    def conv(r, _):
        acc = None
        for k in range(5):
            term = dot(sp[pl.ds(4 * r + k, 4)].reshape(256, H), WC[1, k])
            acc = term if acc is None else acc + term
        mx[pl.ds(4 * r, 4)] = acc.reshape(4, 64, H)
        return 0

    lax.fori_loop(0, 2, conv, 0)
    for m in range(2):
        spread.go(1, dth2, dthr_at, m, False)
    spread.arrive(1, dth2, dthr_at)

    def mid(i, _):
        every = pl.ds(0, 64)
        norm_gelu(view(mx, i, every), nh, gm(1, 1), bm(1, 1), put(thirdr, i, every))
        norm_gelu_back(view(mx, i, every), view(dthr, i, every), nh, gm(1, 1), bm(1, 1), dgb.at[0], dgb.at[1], hold, put(dpad, i + 2, every))
        return 0

    lax.fori_loop(0, 8, mid, 0)
    for p in range(4):
        spread.back(2, thirdr, third2, p, True)

    def conv_back(r, _):
        acc = None
        for k in range(5):
            term = dot_nt(dpad[pl.ds(4 * r + 4 - k, 4)].reshape(256, H), WC[1, k])
            acc = term if acc is None else acc + term
        dsecr[pl.ds(4 * r, 4)] = acc.astype(BF).reshape(4, 64, H)
        return 0

    lax.fori_loop(0, 2, conv_back, 0)
    for p in range(4):
        spread.back(3, dsecr, dsec2, p, True)
    dm = dpad[pl.ds(2, 8)].reshape(512, H)

    def conv_grads(k, _):
        put_grad(G, CONV0 + k * 100, dot_tn(sp[pl.ds(k, 8)].reshape(512, H), dm))
        return 0

    lax.fori_loop(0, 5, conv_grads, 0)
    g_conv = out_copy(G.at[:, pl.ds(CONV0, 500)], g_o.at[:, pl.ds(CONV0, 500)])
    g_conv.start()
    for p in range(4):
        spread.back(2, thirdr, third2, p, False)
        spread.back(3, dsecr, dsec2, p, False)
    for m in range(2):
        spread.back_arrive(2, thirdr, third2, m)
        spread.back_arrive(3, dsecr, dsec2, m)
    labels = lax.broadcasted_iota(jnp.int32, (1, 128), 1)

    def backward(m, _):
        length = lengths[2 * c + m]
        t = third2[m].reshape(seg, H)
        he[pl.ds(0, seg)] = dot(t, WO[1, :, :H])
        me[...] = dot(t, WO[1, :, H:])

        def a(i, size):
            r = pl.ds(i, size)
            for j in range(nd):
                br = he[r, cols(j)] if j < nh else me[r, cols(j - nh)]
                out2[m, r, cols(j)] = (out1[m, r, cols(j)].astype(F32) + br).astype(BF)

        chunks(seg, a)
        logits = jnp.where(labels < 30, dot(out2[m], dec[...]), -1e30)
        ex = jnp.exp(logits - jnp.max(logits, axis=-1, keepdims=True))
        probs = ex / jnp.sum(ex, axis=-1, keepdims=True)
        weight = jnp.where(positions(base, 0, seg) < length, mask[2 * c + m].astype(F32), 0.0)
        counts[...] += fold(jnp.where(types[2 * c + m] == labels, probs * weight, 0.0))

        def b(jj, _):
            r = pl.ds(pl.multiple_of(jj * 64, 64), 64)
            pos = positions(base, jj * 64, 64)
            u, h = lax.div(jj, 2), lax.rem(jj, 2)
            ds = lambda j: jnp.where(pos < length, dsec2[m, u, h, :, cols(j)].astype(F32), 0.0)
            norm_gelu_back(view(hidden2, m, r), ds, nh, gm(1, 0), bm(1, 0), dgbm.at[0], dgbm.at[1], hold, put(dh, m, r))
            return 0

        lax.fori_loop(0, seg // 64, b, 0)
        he[pl.ds(0, seg)] = dot_nt(dh[m], WI[1, :H])
        me[...] = dot_nt(dh[m], WI[1, H:])

        def e(i, size):
            r = pl.ds(i, size)
            df = lambda j: he[r, cols(j)] if j < nh else me[r, cols(j - nh)]

            def store(j, v):
                ge[m, pl.ds(i + HALO, size), cols(j)] = (cot[m, r, cols(j)].astype(F32) + v).astype(BF)

            norm_gelu_back(view(out1, m, r), df, nd, gi(1), bi(1), dgbi.at[0], dgbi.at[1], hold, store)

        chunks(seg, e)
        for cond, _, cp in edges(ge, m, seg, gs, gr, z, q, c):
            pl.when(cond)(cp.start)
        return 0

    lax.fori_loop(0, 2, backward, 0)
    done2 = place(1, out2, 1)
    flat = lambda v: v.reshape(2 * seg, v.shape[-1])
    t2 = flat(third2[...])
    for j in range(2):
        put_grad(G, OUT0, dot_tn(t2, flat(cot[:, :, pl.ds(j * H, H)])), nh * j)
    put_grad(G, IN0, dot_tn(flat(first2[...]), flat(dh[...])))
    g_rest = out_copy(G.at[:, pl.ds(0, CONV0)], g_o.at[:, pl.ds(0, CONV0)])
    g_rest.start()
    for m in range(2):
        for s_cond, r_cond, cp in edges(ge, m, seg, gs, gr, z, q, c):
            pl.when(s_cond)(cp.wait_send)
            pl.when(r_cond)(cp.wait_recv)
    g_ge = out_copy(ge, ge_o)
    g_ge.start()
    for cp in saves + [g_conv, g_rest, g_ge]:
        cp.wait()
    done1()
    done2()
    remote(out1, act.at[pl.ds(2 * (1 - c), 2)], acs.at[0], acr.at[0], peer).wait_recv()
    for cp in sends:
        cp.wait_send()
    for cond, _, cp in halos:
        pl.when(cond)(cp.wait_send)


def run_front(lengths, inputs, cot, params, w_in, conv_w, w_out, dec, mask, types):
    seg, D, H = inputs.shape[2], inputs.shape[3], w_in.shape[2]
    rows = seg + 2 * HALO
    any_, vm, sm = (pl.BlockSpec(memory_space=s) for s in (pl.ANY, pltpu.VMEM, pltpu.SMEM))
    sh = jax.ShapeDtypeStruct
    dma = lambda *s: pltpu.SemaphoreType.DMA(s)
    saved = [((2, rows, D), BF), ((2, rows, D), BF), ((2, seg, D), BF), ((2, seg, H), F32), ((2, rows + 16, H), F32), ((2, rows, H), F32),
             ((2, seg, H), BF), ((D, H), BF), ((5, H, H), BF), ((H, D), BF), ((2, UNITS, 16, 128), BF)]
    small = [((2, 8, D), F32), ((2, 8, H), F32), ((2, 8, H), F32), ((8, 128), F32)]
    part = (2, 2, 2, 64, H)
    scratch = [((2, D, H), BF), ((2, 5, H, H), BF), ((2, H, D), BF), ((2, 8, D), F32), ((2, rows, D), BF), ((2, seg, D), BF),
               ((2, seg, D), BF), ((2, seg, D), BF), ((2, seg, H), F32), ((2, rows + 16, H), F32), ((2, rows, H), F32), ((2, seg, H), BF),
               ((2, seg, D), BF), ((2, seg, H), F32), (part, BF), (part, BF), ((12, 64, H), BF), ((8, 64, H), BF), ((8, 64, H), BF),
               ((12, 64, H), BF), ((8, 64, H), BF), (part, BF), (part, BF), ((2, seg, D), BF), ((2, rows, D), BF), ((2, UNITS, 16, 128), BF),
               ((rows, D), BF), ((rows, H), F32), ((seg, H), F32), ((8, 64, H), F32), ((2, seg, H), BF), ((2, 64, D), F32)]
    return pl.pallas_call(
        front,
        out_shape=[sh((4, seg, D), BF)] + [sh(s, d) for s, d in saved + small],
        in_specs=[sm, any_, any_, any_, any_, any_, any_, vm, vm, vm],
        out_specs=[any_] * (1 + len(saved)) + [vm] * len(small),
        scratch_shapes=[pltpu.VMEM(s, d) for s, d in scratch]
        + [dma(8), dma(8), dma(8), dma(2, 2), dma(2, 2), dma(4), dma(4, 4), dma(4, 4), dma(4), dma(2, 2), dma(2, 2), dma(16), dma(2), dma(1)],
        compiler_params=pltpu.CompilerParams(collective_id=1, has_side_effects=True, vmem_limit_bytes=62 * 2**20),
    )(lengths, inputs, cot, params, w_in, conv_w, w_out, dec, mask, types)


def call(fn, outs, scratch, args, scal_at=(), layer={}):
    vm = pl.BlockSpec(memory_space=pltpu.VMEM)
    whole, place = [], []
    for a in args:
        if not any(a is w for w in whole):
            whole.append(a)
        place.append(next(i for i, w in enumerate(whole) if w is a))
    specs = [pl.BlockSpec(memory_space=pltpu.SMEM) if place.index(i) in scal_at else vm for i in range(len(whole))]

    def kernel(*refs):
        ins = [refs[p].at[pl.ds(layer[i], 1)] if i in layer else refs[p] for i, p in enumerate(place)]
        fn(*ins, *refs[len(whole):])

    return pl.pallas_call(
        kernel,
        out_shape=[jax.ShapeDtypeStruct(s, d) for s, d in outs],
        in_specs=specs,
        out_specs=[vm] * len(outs),
        scratch_shapes=[pltpu.VMEM(s, d) for s, d in scratch],
        compiler_params=pltpu.CompilerParams(vmem_limit_bytes=60 * 2**20),
    )(*whole)


def unpack_kernel(conv, w_out, w_in, extra, cnt, s_conv, s_out, s_in, gi, bi, gm, bm, counts):
    H = s_conv.shape[-1]
    for j in range(5):
        for h in range(2):
            s_conv[0, 0, pl.ds(h * 320, 320), cols(j)] = conv[h, pl.ds(j * 20, 20)].reshape(320, 128).astype(F32)
    for j in range(2):
        for h in range(2):
            s_out[0, pl.ds(h * 320, 320), cols(j)] = w_out[h, pl.ds(j * 20, 20)].reshape(320, 128).astype(F32)
    for h in range(2):
        s_in[0, pl.ds(h * 640, 640)] = w_in[h].reshape(640, 128).astype(F32)

    @pl.when(pl.program_id(0) == 0)
    def _():
        small = extra[0].reshape(192, 128).astype(F32)
        for j in range(10):
            gi[:, cols(j)] = small[j : j + 1]
            bi[:, cols(j)] = small[10 + j : 11 + j]
        for k in range(2):
            for j in range(5):
                gm[0, pl.ds(k, 1), cols(j)] = small[20 + 10 * k + j : 21 + 10 * k + j]
                bm[0, pl.ds(k, 1), cols(j)] = small[25 + 10 * k + j : 26 + 10 * k + j]
        counts[...] = cnt[...].reshape(192, 128)[40:41].astype(F32)


def unpack(total, cnt, D, H):
    def spec(units, first):
        return pl.BlockSpec((2, units, 16, 128), lambda k: (0, first + k, 0, 0))

    def full(*s):
        return pl.BlockSpec(s, lambda k: (0,) * len(s))

    sh = lambda *s: jax.ShapeDtypeStruct(s, F32)
    return pl.pallas_call(
        unpack_kernel,
        grid=(5,),
        out_shape=[sh(1, 5, H, H), sh(1, H, D), sh(1, D, H), sh(1, D), sh(1, D), sh(1, 2, H), sh(1, 2, H), sh(1, 128)],
        in_specs=[spec(100, CONV0 // 100), spec(40, 0), spec(40, 5), pl.BlockSpec((2, 12, 16, 128), lambda k: (0, 75, 0, 0)), full(12, 16, 128)],
        out_specs=[pl.BlockSpec((1, 1, H, H), lambda k: (0, k, 0, 0)), pl.BlockSpec((1, H, 256), lambda k: (0, 0, k)),
                   pl.BlockSpec((1, D, 128), lambda k: (0, 0, k)), full(1, D), full(1, D), full(1, 2, H), full(1, 2, H), full(1, 128)],
        compiler_params=pltpu.CompilerParams(vmem_limit_bytes=60 * 2**20),
    )(total, total, total, total, cnt)


def body(inputs, lengths, mlm_mask, true_types, gain_in, bias_in, gain_mid, bias_mid, w_in, conv_w, w_out, decoder, cotangent, fast):
    c = lax.axis_index("section")
    seg, D, H = inputs.shape[2], inputs.shape[3], w_in.shape[2]
    rows = seg + 2 * HALO
    params = jnp.concatenate([gain_in, bias_in, gain_mid.reshape(1, D), bias_mid.reshape(1, D), jnp.zeros((4, D), BF)]).astype(F32)
    dec = jnp.pad(decoder, ((0, 0), (0, 128 - decoder.shape[1])))
    (act, xe, ge, first1, hidden1, sec1, mixed1, third1, w_in1, conv1, w_out1, g_two, dgbi2, dgbm2, dgb2, counts) = run_front(
        lengths[:, 0], inputs, cotangent, params, w_in, conv_w, w_out, dec, mlm_mask[:, 0][..., None], true_types[:, 0][..., None])
    q = lax.axis_index("seq")
    scal = jnp.concatenate([jnp.reshape(q * seg, (1,)), lax.dynamic_slice_in_dim(lengths[:, 0], 2 * c, 2, 0)]).astype(jnp.int32)
    both = lambda w: lax.all_gather(w, "section", axis=0, tiled=True)
    gi, bi, gm, bm = (both(v.astype(F32)) for v in (gain_in, bias_in, gain_mid, bias_mid))
    grad1, dgbi1, dgbm1, g_one = call(
        k4,
        [((2, seg, D), BF), ((2, 8, D), F32), ((4, 8, H), F32), ((2, 900, 16, 128), BF)],
        [((rows, H), F32), ((seg, H), F32), ((rows, H), F32), ((2, seg, H), BF), ((2, seg, H), BF), ((2 * seg, H), BF), ((2, 64, D), F32)],
        (xe, ge, scal, first1, hidden1, sec1, mixed1, third1, w_in1[None], conv1[None], w_out1[None], gi[:1], bi[:1], gm[0], bm[0]),
        (2,), {8: 0, 9: 0, 10: 0})

    def extra(dgbi, dgbm, cnt):
        flat = jnp.concatenate([dgbi.sum(1).reshape(-1), dgbm.sum(1).reshape(-1), cnt.sum(0)])
        flat = jnp.pad(flat, (0, 12 * 2048 - flat.shape[0])).astype(BF).reshape(1, 12, 16, 128)
        return jnp.concatenate([flat, flat], 0)

    g_two = jnp.concatenate([g_two[:, :EXTRA0], extra(dgbi2, jnp.concatenate([dgbm2, dgb2]), counts)], 1)
    g_one = jnp.concatenate([g_one, extra(dgbi1, dgbm1, jnp.zeros_like(counts))], 1)
    if fast:
        N, PU, QU = 6, 88, 64
        total, cnt = allreduce(g_one, g_two, N, PU, QU)
        total = total.reshape(2, UNITS, 16, 128)
    else:
        own, other = jnp.where(c == 0, g_one, g_two), jnp.where(c == 0, g_two, g_one)
        got = lax.ppermute(other, "section", [(0, 1), (1, 0)])
        total = lax.psum(own.astype(F32) + got.astype(F32), ("dp", "seq")).astype(BF)
        cnt = lax.psum(g_two[0, EXTRA0:].astype(F32), ("section", "dp", "seq")).astype(BF)
    s_conv, s_out, s_in, s_gi, s_bi, s_gm, s_bm, s_cnt = unpack(total, cnt, D, H)

    def placed(one, two):
        own, other = jnp.where(c == 0, one, two), jnp.where(c == 0, two, one)
        got = lax.ppermute(other, "section", [(0, 1), (1, 0)])
        return jnp.where(c == 0, jnp.concatenate([own, got]), jnp.concatenate([got, own]))[None, :, None]

    return (act[None, :, None], placed(grad1, ge[:, HALO : HALO + seg]), s_gi, s_bi, s_gm, s_bm, s_in, s_conv, s_out, s_cnt[0, : decoder.shape[1]])


def solution(mesh):
    fast = mesh.shape["dp"] == 4 and mesh.shape["seq"] == 4
    return jax.shard_map(
        functools.partial(body, fast=fast),
        mesh=mesh,
        in_specs=(P(None, "dp", "seq", None), P(None, "dp"), P(None, "dp", "seq"), P(None, "dp", "seq"), P("section", None),
                  P("section", None), P("section", None, None), P("section", None, None), P("section", None, None),
                  P("section", None, None, None), P("section", None, None), P(), P(None, "dp", "seq", None)),
        out_specs=(P("section", None, "dp", "seq", None), P("section", None, "dp", "seq", None), P("section", None), P("section", None),
                   P("section", None, None), P("section", None, None), P("section", None, None), P("section", None, None, None),
                   P("section", None, None), P()),
        check_vma=False,
    )
```

time: 536 us -> 326 us (0.61); the launches traced: 525 us -> 325 us
  Pallas kernels: 352 us -> 275 us
  local copies, waits for them, and re-layouts: 62.9 us -> 16.3 us
  waiting for transfers between devices: 30.3 us -> 0.01 us
  other arithmetic: 46.8 us -> 24.7 us
  between operations: 14.4 us -> 0.76 us
  starting transfers between devices: 11.7 us -> 0.9 us
    pallas_call x4 -> x1, Pallas kernels: 168 us -> 34.7 us  [call(): pl.pallas_call(kernel, out_shape=[jax.ShapeDtypeStruct(s, d) for s, d in...]
    pallas_call x2, Pallas kernels: 35 us -> 93.5 us  [the longest x1 84.5 us: run_front(): pl.pallas_call(front, out_shape=[sh((4, seg, D), BF)] + [sh(s, d) for s,...]
    unnamed x45 -> x14, local copies, waits for them, and re-layouts: 46.3 us -> 4.01 us
    all_gather x3 -> x0, waiting for transfers between devices: 28.3 us -> none  [body(): both = lambda w: lax.all_gather(w, 'section', axis=0, tiled=True)]
    concatenate x3 -> x1, other arithmetic: 21 us -> 5.52 us  [body(): jnp.concatenate([g_two[:, :EXTRA0], extra(dgbi2, jnp.concatenate([dgbm2,...]
    ppermute x4 -> x0, starting transfers between devices: 10.6 us -> none  [the longest x2 8.02 us: haloed(): before = lax.ppermute(v[:, seg - HALO:], 'seq', up)]
  transfers between devices with their start and end apart: 9 -> 1, of which waited for: 2 -> 0; matrix products, arithmetic and copies ran while one was open for 19% -> 6% of each run, Pallas kernels for 39% -> 48%
where the time goes in v2:
time: 326 us; the launch traced here: 325 us
  Pallas kernels  275 us (84%)
  other arithmetic  24.7 us (8%)
  local copies, waits for them, and re-layouts  16.3 us (5%)
  blocking collectives  7.3 us (2%)
    pallas_call x1, Pallas kernels, allreduce(): pl.pallas_call(functools.partial(ar_kernel, ring), out_shape=[jax.ShapeDt...  147 us
    pallas_call x1, Pallas kernels, run_front(): pl.pallas_call(front, out_shape=[sh((4, seg, D), BF)] + [sh(s, d) for s,...  84.5 us
    pallas_call x1, Pallas kernels, call(): pl.pallas_call(kernel, out_shape=[jax.ShapeDtypeStruct(s, d) for s, d in...  34.7 us
    pallas_call x1, Pallas kernels, unpack(): pl.pallas_call(unpack_kernel, grid=(5,), out_shape=[sh(1, 5, H, H), sh(1,...  9.01 us
    all_gather x4, blocking collectives, body(): both = lambda w: lax.all_gather(w, 'section', axis=0, tiled=True)  7.3 us
  transfers between devices with their start and end apart: 1, of which 0 were waited for; matrix products, arithmetic and copies ran while one was open for 6% of the time, Pallas kernels for 48%

profile of v2, /device:TPU:0, one launch (start us, length us, event | category | flops | bytes accessed | tf_op | source)
XLA Modules:
  0.0 325.0 jit_solution(10162256394952192463)
XLA Ops:
  0.7 0.7 reduce
  1.4 0.7 reduce.1
  2.1 0.7 convert_element_type.26
  2.8 0.7 copy.37
  3.4 0.7 convert_element_type.25
  4.1 0.7 copy.36
  4.8 0.7 bitcast_convert_fusion.1
  5.5 1.9 all-gather
  7.4 0.6 slice_bitcast_fusion.3.refs_11_
  8.0 0.7 bitcast_convert_fusion
  8.7 1.8 all-gather.1
  10.5 0.6 slice_bitcast_fusion.2.refs_12_
  11.1 1.8 all_gather.14
  12.9 0.6 slice_bitcast_fusion.1.refs_13_
  13.5 1.8 all_gather.15
  15.3 0.6 slice_bitcast_fusion.refs_14_
  15.9 0.8 concatenate.53
  16.6 0.6 convert_element_type.22.params
  17.3 1.1 copy.31
  18.4 0.8 pad.13.dec
  19.2 1.0 broadcast_in_dim_squeeze.9.types
  20.2 1.0 broadcast_in_dim_squeeze.8.mask
  21.2 0.7 dynamic-slice_bitcast_fusion
  21.9 0.6 pad_add_fusion.refs_2_
  22.5 84.5 %shard_map.204 = (bf16[4,256,1280]{2,1,0:T(8,128)(2,1)}, bf16[2,288,1280]{2,1,0:T(8,128)(2,1)}, bf16[2,288,1280]{2,1,0:T(8,128)(2,1)}, bf16[2,256,1280]{2,1,0:T(...) custom-call(s32[4]{0:T(128)} %bitcast.58, ...), custom_call_target="tpu_custom_call" | custom-call | tf_op jit(solution)/shard_map/pallas_call | solution.py:807
  107.0 0.0 copy-start
  107.0 34.7 %shard_map.205 = (bf16[2,256,1280]{2,1,0:T(8,128)(2,1)}, f32[2,8,1280]{2,1,0:T(8,128)}, f32[4,8,640]{2,1,0:T(8,128)}, bf16[2,900,16,128]{3,2,1,0:T(8,128)(2,1)}) custom-call(bf16[2,288,1280]{2,1,0:T(8,128)(2,1)} %get-tuple-element.41.refs_0_, bf16[2,288,1280]{2,1,0:T(8,128)(2,1)} %get-tuple-element.42.refs_1_, s32[3]{0:T(128)} %pad_add_fusion.refs_2_, ...), custom_call_target="tpu_custom_call" | custom-call | tf_op jit(solution)/shard_map/pallas_call | solution.py:831
  141.7 0.0 copy-done
  141.7 0.0 copy-start.2
  141.7 1.5 select_bitcast_fusion
  143.2 0.9 collective-permute-start
  144.1 0.0 copy-done.2
  144.2 0.9 reduce_sum.54
  145.1 0.8 maximum_reduce_fusion
  146.0 0.9 reduce_sum.51
  146.9 0.9 reduce_sum.52
  147.9 4.4 %slice.26 = bf16[2,900,16,128]{3,2,1,0:T(8,128)(2,1)S(1)} slice(bf16[2,912,16,128]{3,2,1,0:T(8,128)(2,1)} %get-tuple-element.55), slice={[0:2], [0:900], [0:16], [0:128]} | slice | bytes 14745600 | tf_op jit(solution)/shard_map/slice | solution.py:908
  152.2 0.0 slice-start
  152.3 0.0 slice-start.1
  152.3 5.5 %maximum_maximum_fusion.1 = bf16[2,912,16,128]{3,2,1,0:T(8,128)(2,1)} fusion(bf16[1,12,16,128]{3,2,1,0:T(8,128)(2,1)S(1)} %bitcast.52, bf16[2,900,16,128]{3,2,1,0:T(8,128)(2,1)S(1)} %slice.26), kind=kLoop, calls=%fused_computation.1 | loop fusion | flops 7471104 | bytes 14893056 | tf_op jit(solution)/shard_map/concatenate | solution.py:908
  157.8 0.0 slice-done
  157.8 0.0 slice-done.1
  157.8 5.5 %maximum_maximum_fusion = bf16[2,912,16,128]{3,2,1,0:T(8,128)(2,1)} fusion(bf16[1,12,16,128]{3,2,1,0:T(8,128)(2,1)S(1)} %bitcast.53, bf16[2,900,16,128]{3,2,1,0:T(8,128)(2,1)S(1)} %bitcast.47), kind=kLoop, calls=%fused_computation | loop fusion | flops 7471104 | bytes 14893056 | tf_op jit(solution)/shard_map/concatenate | solution.py:909
  163.3 146.9 %shard_map.206 = (bf16[2,6,152,16,128]{4,3,2,1,0:T(8,128)(2,1)}, bf16[12,16,128]{2,1,0:T(8,128)(2,1)}) custom-call(bf16[2,6,152,16,128]{4,3,2,1,0:T(8,128)(2,1)} %bitcast.45, bf16[2,6,152,16,128]{4,3,2,1,0:T(8,128)(2,1)} %bitcast.44), custom_call_target="tpu_custom_call" | custom-call | tf_op jit(solution)/shard_map/pallas_call | solution.py:421
  310.2 9.0 %shard_map.207 = (f32[1,5,640,640]{3,2,1,0:T(8,128)}, f32[1,640,1280]{2,1,0:T(8,128)}, f32[1,1280,640]{2,1,0:T(8,128)}, f32[1,1280]{1,0:T(1,128)}, f32[1,1280]{1...) custom-call(bf16[2,912,16,128]{3,2,1,0:T(8,128)(2,1)} %bitcast.40, ...), custom_call_target="tpu_custom_call" | custom-call | tf_op jit(solution)/shard_map/pallas_call | solution.py:873
  319.2 1.2 slice_bitcast_fusion.4
  320.4 0.0 collective-permute-done
  320.4 0.0 copy-start.1
  320.4 3.1 fusion
  323.5 0.0 copy-done.1
  323.6 1.5 copy.39
  (10 shorter events, 0.1 us)
Async XLA Ops:
  107.0 34.7 %copy-start = (bf16[2,288,1280]{2,1,0:T(8,128)(2,1)S(1)}, bf16[2,288,1280]{2,1,0:T(8,128)(2,1)}, u32[]{:S(2)}) copy-start(bf16[2,288,1280]{2,1,0:T(8,128)(2,1)} %get-tuple-element.42.refs_1_) | copy-start | bytes 4423684
  141.7 2.4 copy-start.2
  143.2 177.2 %collective-permute-start = (bf16[2,256,1280]{2,1,0:T(8,128)(2,1)S(1)}, bf16[2,256,1280]{2,1,0:T(8,128)(2,1)}, u32[]{:S(2)}, u32[]{:S(2)}) collective-permute-start(bf16[2,256,1280]{2,1,0:T(8,128)(2,1)S(1)} %get-tuple-element.101), channel_id=1, source_target_pairs={{0,16},{16,0},{1,17},{17,1},{2,18},{18,2},{3,19},{19,3},{4,20},{20... | collective-permute-start | bytes 3932168 | tf_op jit(solution)/shard_map/ppermute | solution.py:923
  152.2 5.6 %slice-start = ((s8[7372800]{0:T(1024)(128)(4,1)}), s8[4194304]{0:T(1024)(128)(4,1)S(1)}, s32[]{:S(2)}) async-start(s8[7372800]{0:T(1024)(128)(4,1)} %bitcast.46), calls=%async_computation | async-start | bytes 8388608
  152.3 5.5 %slice-start.1 = ((s8[7372800]{0:T(1024)(128)(4,1)}), s8[3178496]{0:T(1024)(128)(4,1)S(1)}, s32[]{:S(2)}) async-start(s8[7372800]{0:T(1024)(128)(4,1)} %bitcast.46), calls=%async_computation.1 | async-start | bytes 6356992
  320.4 3.1 copy-start.1

commit v3 on v2

--- a/solution.py
+++ b/solution.py
@@ -114,7 +114,7 @@
             g_ref[h, pl.ds(unit + (col0 + j) * per, per)] = block[h * per : (h + 1) * per]
 
 
-OUT0, IN0, CONV0, EXTRA0, UNITS = 0, 200, 400, 900, 912
+EXTRA0, OUT0, IN0, CONV0, UNITS = 0, 12, 212, 412, 912
 
 
 def put(ref, *at):
@@ -128,97 +128,24 @@
     return first + i + lax.broadcasted_iota(jnp.int32, (size, 1), 0)
 
 
-def k4(xe, ge, scal, first1, hidden1, sec1, mixed1, third1, w_in1, conv1, w_out1, gi1, bi1, gm1, bm1,
-       grad1, dgbi, dgbm, g_ref, he, me, dme, dh, dm, swin, hold):
-    base = scal[0]
-    rows, D = xe.shape[1:]
-    seg, H = grad1.shape[1], hidden1.shape[2]
-    nd, nh = D // 128, H // 128
-    for ref in (dgbi, dgbm):
-        ref[...] = jnp.zeros_like(ref)
-
-    def micro(m, _):
-        length = scal[1 + m]
-        he[...] = dot_nt(ge[m], w_out1[0])
-
-        def a(i, size):
-            r = pl.ds(i + HALO, size)
-
-            def store(j, v):
-                v = v.astype(BF)
-                dme[r, cols(j)] = v.astype(F32)
-                dm[m, pl.ds(i, size), cols(j)] = v
-
-            norm_gelu_back(view(mixed1, m, r), view(he, r), nh, row(gm1, 1), row(bm1, 1), dgbm.at[2], dgbm.at[3], hold, store)
-
-        chunks(seg, a)
-        for edge in (0, rows - HALO):
-            r = pl.ds(edge, HALO)
-            pos = positions(base - HALO, edge, HALO)
-            inside = jnp.logical_and(pos >= 0, pos < 1024)
-
-            def store(j, v):
-                dme[r, cols(j)] = jnp.where(inside, v, 0.0).astype(BF).astype(F32)
-
-            norm_gelu_back(view(mixed1, m, r), view(he, r), nh, row(gm1, 1), row(bm1, 1), None, None, hold.at[:, pl.ds(0, HALO)], store)
-        acc = None
-        for k in range(5):
-            term = dot_nt(dme[pl.ds(HALO - DIL * (k - 2), seg)].astype(BF), conv1[0, k])
-            acc = term if acc is None else acc + term
-        he[pl.ds(0, seg)] = acc
-
-        def b(i, size):
-            r = pl.ds(i, size)
-            pos = positions(base, i, size)
-            ds = lambda j: jnp.where(pos < length, he[r, cols(j)], 0.0)
-            norm_gelu_back(view(hidden1, m, r), ds, nh, row(gm1, 0), row(bm1, 0), dgbm.at[0], dgbm.at[1], hold, put(dh, m, r))
-
-        chunks(seg, b)
-        he[pl.ds(0, seg)] = dot_nt(dh[m], w_in1[0, :H])
-        me[...] = dot_nt(dh[m], w_in1[0, H:])
-
-        def c(i, size):
-            r, e = pl.ds(i, size), pl.ds(i + HALO, size)
-            df = lambda j: he[r, cols(j)] if j < nh else me[r, cols(j - nh)]
-
-            def store(j, v):
-                grad1[m, r, cols(j)] = (ge[m, e, cols(j)].astype(F32) + v).astype(BF)
-
-            norm_gelu_back(view(xe, m, e), df, nd, row(gi1, 0), row(bi1, 0), dgbi.at[0], dgbi.at[1], hold, store)
-
-        chunks(seg, c)
-        return 0
-
-    lax.fori_loop(0, 2, micro, 0)
-    flat = lambda v: v.reshape(2 * seg, v.shape[-1])
-    t1 = flat(third1[...])
-    for j in range(2):
-        g1 = flat(ge[:, pl.ds(HALO, seg), pl.ds(j * H, H)])
-        put_grad(g_ref, OUT0, dot_tn(t1, g1), nh * j)
-    d1 = flat(dm[...])
-    for k in range(5):
-        for m in range(2):
-            swin[pl.ds(m * seg, seg)] = sec1[m, pl.ds(8 + HALO + DIL * (k - 2), seg)].astype(BF)
-        put_grad(g_ref, CONV0 + k * 100, dot_tn(swin[...], d1))
-    put_grad(g_ref, IN0, dot_tn(flat(first1[...]), flat(dh[...])))
-
-
 class Ring:
-    def __init__(self, N, PU, QU):
+    def __init__(self, N, PU, QU, M, gap):
+        self.M, self.gap = M, gap
         self.N, self.PU, self.QU, self.U = N, PU, QU, PU + QU
+        self.out_units = N * self.U
         self.kinds = ["D","P1","P2","PZ1","PZ2","PT1","PT2","PT3","G1","G2","Q1","Q2","X1","X2","X3","X4","QT1","QT2","QT3","F"]
     def scratch(self):
-        N2, PU, QU, U = 2*self.N, self.PU, self.QU, self.U
-        b = lambda u: pltpu.VMEM((N2, u, 16, 128), BF)
+        N2, PU, QU, U = 2 * self.N, self.PU, self.QU, self.U
+        b = lambda u, n=N2: pltpu.VMEM((n, u, 16, 128), BF)
         nk = len(self.kinds)
-        return [b(U), b(PU//2), b(PU//4), b(PU//4), b(PU//8), b(QU), b(QU//2), b(QU//4), b(QU//8), b(U),
+        return [b(U), b(U, 4), b(PU//2), b(PU//4), b(PU//4), b(PU//8), b(QU), b(QU//2), b(QU//4), b(QU//8), b(PU//4), b(QU//8),
                 pltpu.SemaphoreType.DMA((nk, N2)), pltpu.SemaphoreType.DMA((nk, N2))]
-    def bind(self, G, two, one, out, D, RP1, RP2, RZ1, RZ2, RQ1, RQ2, RX1, RX2, R, ss, rs):
-        N, PU, QU, U = self.N, self.PU, self.QU, self.U
+    def bind(self, conv, GV, out, D, RD, RP1, RP2, RZ1, RZ2, RQ1, RQ2, RX1, RX2, TQ, TX, ss, rs):
+        N, PU, QU, U, M = self.N, self.PU, self.QU, self.U, self.M
+        R = D
         c, z, q = lax.axis_index("section"), lax.axis_index("dp"), lax.axis_index("seq")
         xb, yb = lax.rem(q, 2), lax.div(q, 2)
         f = jnp.where(c == 0, xb, yb); s = jnp.where(c == 0, yb, xb)
-        qx = xb ^ 1;
         nx = (c, z, yb*2 + 1 - xb); ny = (c, z, (1-yb)*2 + xb)
         n1 = (c, z, jnp.where(c == 0, nx[2], ny[2])); n2 = (c, z, jnp.where(c == 0, ny[2], nx[2]))
         side = lax.div(z, 2)
@@ -227,10 +154,10 @@
         peer = (1 - c, z, q)
         inner = jnp.logical_or(z == 1, z == 2)
         outer = jnp.logical_not(inner)
+        ds = pl.ds
         K = {k: i for i, k in enumerate(self.kinds)}
         def cp(k, i, src, dst, dev):
             return pltpu.make_async_remote_copy(src_ref=src, dst_ref=dst, send_sem=ss.at[K[k], i], recv_sem=rs.at[K[k], i], device_id=dev, device_id_type=MESH)
-        ds = pl.ds
         H, Q4, E8 = PU//2, PU//4, PU//8
         h, q4, e8 = QU//2, QU//8, QU//8
         def add(dst, a, *bs):
@@ -239,45 +166,49 @@
             dst[...] = acc.astype(BF)
         pq = lambda ff, s2: ds((2*ff + s2)*Q4, Q4)
         pch = lambda k: ds((2*f + s)*Q4 + k*E8, E8)
+        tch = lambda k: ds(k*E8, E8)
         def qn(k): return ds(PU + k*h, h)
         def qhalf(k, ff): return ds(PU + k*h + ff*(h//2), h//2)
         def qquart(k, ff, s2): return ds(PU + k*h + (2*ff+s2)*(h//4), h//4)
         near, farc = side, 1 - side
         C = dict(
-          D=lambda i: cp("D", i, two.at[1-c, i], D.at[i], peer),
-          E=lambda i: cp("D", i, one.at[1-c, i-N], D.at[i], peer),
-          W=lambda i: cp("D", i, G.at[i], D.at[i], peer),
+          D=lambda i: cp("D", i, GV.at[1-c, ds((i-M)*U, U)], RD.at[lax.rem(i, 4)], peer),
+          E=lambda i: cp("D", i, conv.at[1-c, pl.ds(self.first + i*U, U)], RD.at[lax.rem(i, 4)], peer),
+          W=lambda i: cp("D", i, D.at[i], RD.at[lax.rem(i, 4)], peer),
           P1=lambda i: cp("P1", i, D.at[i, ds((1-f)*H, H)], RP1.at[i], n1),
           P2=lambda i: cp("P2", i, D.at[i, pq(f, 1-s)], RP2.at[i], n2),
           PZ1=lambda i: cp("PZ1", i, D.at[i, pq(f, s)], RZ1.at[i], zp),
           PZ2=lambda i: cp("PZ2", i, D.at[i, pch(farc)], RZ2.at[i], far),
-          PT1=lambda i: cp("PT1", i, R.at[i, pch(near)], R.at[i, pch(near)], far),
-          PT2=lambda i: cp("PT2", i, R.at[i, pch(near)], R.at[i, pch(near)], zp),
-          PT3=lambda i: cp("PT3", i, R.at[i, pch(farc)], R.at[i, pch(farc)], zp),
+          PT1=lambda i: cp("PT1", i, TQ.at[i, tch(near)], TQ.at[i, tch(near)], far),
+          PT2=lambda i: cp("PT2", i, TQ.at[i, tch(near)], TQ.at[i, tch(near)], zp),
+          PT3=lambda i: cp("PT3", i, TQ.at[i, tch(farc)], TQ.at[i, tch(farc)], zp),
           G1=lambda i: cp("G1", i, R.at[i, pq(f, s)], R.at[i, pq(f, s)], n2),
           G2=lambda i: cp("G2", i, R.at[i, ds(f*H, H)], R.at[i, ds(f*H, H)], n1),
           Q1=lambda i: cp("Q1", i, D.at[i, ds(PU, QU)], RQ1.at[i], zp),
           Q2=lambda i: cp("Q2", i, D.at[i, qn(farc)], RQ2.at[i], far),
           X1=lambda i: cp("X1", i, D.at[i, qhalf(near, 1-f)], RX1.at[i], n1),
           X2=lambda i: cp("X2", i, D.at[i, qquart(near, f, 1-s)], RX2.at[i], n2),
-          X3=lambda i: cp("X3", i, R.at[i, qquart(near, f, s)], R.at[i, qquart(near, f, s)], n2),
+          X3=lambda i: cp("X3", i, R.at[i, qquart(near, f, s)], TX.at[i], n2),
           X4=lambda i: cp("X4", i, R.at[i, qhalf(near, f)], R.at[i, qhalf(near, f)], n1),
           QT1=lambda i: cp("QT1", i, R.at[i, qn(near)], R.at[i, qn(near)], far),
           QT2=lambda i: cp("QT2", i, R.at[i, qn(near)], R.at[i, qn(near)], zp),
           QT3=lambda i: cp("QT3", i, R.at[i, qn(farc)], R.at[i, qn(farc)], zp),
         )
         def mine(i): return jnp.where(i < N, 1, 0) == c
-        def slot(i): return jnp.where(i < N, i, i - N)
-        Fr = lambda i: cp("F", i, R.at[i], out.at[c, slot(i)], peer)
-        Fl = lambda i: pltpu.make_async_copy(R.at[i], out.at[c, slot(i)], ss.at[K["F"], i])
+        def slot(i): return jnp.where(i < N, lax.rem(i + N - M, N), i - N)
+        Fr = lambda i: cp("F", i, R.at[i], out.at[c, ds(slot(i)*U, U)], peer)
+        Fl = lambda i: pltpu.make_async_copy(R.at[i], out.at[c, ds(slot(i)*U, U)], ss.at[K["F"], i])
         def S0(i):
-            @pl.when(i < N)
+            @pl.when(i < M)
+            def _(): C["E"](i).start()
+            @pl.when(i >= M)
             def _(): C["D"](i).start()
-            @pl.when(i >= N)
-            def _(): C["E"](i).start()
         def S1(i):
             C["W"](i).wait()
-            add(D.at[i], D.at[i], G.at[i])
+            @pl.when(i < M)
+            def _(): add(D.at[i], D.at[i], RD.at[lax.rem(i, 4)])
+            @pl.when(i >= M)
+            def _(): add(D.at[i], GV.at[c, ds((i-M)*U, U)], RD.at[lax.rem(i, 4)])
             C["P1"](i).start()
             @pl.when(outer)
             def _(): C["Q1"](i).start()
@@ -317,7 +248,7 @@
             @pl.when(inner)
             def _():
                 C["PZ2"](i).wait()
-                add(R.at[i, pch(near)], D.at[i, pch(near)], RZ1.at[i, ds(near*E8, E8)], RZ2.at[i])
+                add(TQ.at[i, tch(near)], D.at[i, pch(near)], RZ1.at[i, ds(near*E8, E8)], RZ2.at[i])
                 C["PT1"](i).start(); C["PT2"](i).start()
                 C["X2"](i).wait()
                 add(R.at[i, qquart(near, f, s)], D.at[i, qquart(near, f, s)], RX2.at[i])
@@ -328,6 +259,7 @@
                 C["PT1"](i).wait()
                 C["PT3"](i).start()
                 C["X3"](i).wait()
+                D[i, qquart(near, f, 1-s)] = TX[i]
                 C["X4"](i).start()
         def S7(i):
             @pl.when(outer)
@@ -336,6 +268,7 @@
             @pl.when(inner)
             def _():
                 C["PT2"](i).wait_send(); C["PT3"](i).wait_send()
+            D[i, pq(f, s)] = TQ[i]
             C["G1"](i).start()
             @pl.when(inner)
             def _():
@@ -369,10 +302,11 @@
             def _(): Fr(i).wait_send()
         stages = [S0,S1,S2,S3,S4,S5,S6,S7,S8,S9,S10]
         def step(t):
-            for si in range(len(stages)):
-                i = t - si
-                @pl.when(jnp.logical_and(i >= 0, i < 2*N))
-                def _(): stages[si](i)
+            for si, stage in enumerate(stages):
+                j = t - si
+                first, second = jnp.logical_and(j >= 0, j < N), jnp.logical_and(j >= N + self.gap, j < 2*N + self.gap)
+                i = jnp.where(j < N, j, j - self.gap)
+                pl.when(jnp.logical_or(first, second))(functools.partial(stage, i))
         def recv_final():
             def body(j, _):
                 i = jnp.where(c == 1, j, j + N)
@@ -381,51 +315,26 @@
             lax.fori_loop(0, N, body, 0)
         def barrier():
             b = pltpu.get_barrier_semaphore()
-            for d in (peer, n1, n2, zp):
+            for d in plane(c, z, q) + [zp]:
                 pl.semaphore_signal(b, inc=1, device_id=d, device_id_type=MESH)
             @pl.when(inner)
             def _():
                 pl.semaphore_signal(b, inc=1, device_id=far, device_id_type=MESH)
-                pl.semaphore_wait(b, 5)
+                pl.semaphore_wait(b, 9)
             @pl.when(outer)
-            def _(): pl.semaphore_wait(b, 4)
-        self.R = R
-        self.barrier, self.step, self.recv_final, self.iters = barrier, step, recv_final, 2*N + len(stages) - 1
-
-
-def ar_kernel(ring, one, two, out, cnt, G, gsem, *scr):
-    N = ring.N
-    c = lax.axis_index("section")
-    loads = [pltpu.make_async_copy(two.at[c], G.at[pl.ds(0, N)], gsem.at[0]), pltpu.make_async_copy(one.at[c], G.at[pl.ds(N, N)], gsem.at[1])]
-    for cp in loads:
-        cp.start()
-    ring.bind(G, two, one, out, *scr)
-    ring.barrier()
-    for cp in loads:
-        cp.wait()
-
-    def body(t, _):
-        ring.step(t)
-        return 0
-
-    lax.fori_loop(0, ring.iters, body, 0)
-    ring.recv_final()
-    cnt[...] = ring.R[N - 1, pl.ds(ring.U - 12, 12)]
-
-
-def allreduce(one, two, N, PU, QU):
-    ring = Ring(N, PU, QU)
-    U = PU + QU
-    any_ = pl.BlockSpec(memory_space=pl.ANY)
-    split = lambda g: g.reshape(2, N, U, 16, 128)
-    return pl.pallas_call(
-        functools.partial(ar_kernel, ring),
-        out_shape=[jax.ShapeDtypeStruct((2, N, U, 16, 128), BF), jax.ShapeDtypeStruct((12, 16, 128), BF)],
-        in_specs=[any_, any_],
-        out_specs=[any_, pl.BlockSpec(memory_space=pltpu.VMEM)],
-        scratch_shapes=[pltpu.VMEM((2 * N, U, 16, 128), BF), pltpu.SemaphoreType.DMA((2,))] + ring.scratch(),
-        compiler_params=pltpu.CompilerParams(collective_id=0, has_side_effects=True, vmem_limit_bytes=60 * 2**20),
-    )(split(one), split(two))
+            def _(): pl.semaphore_wait(b, 8)
+        self.D = D
+        self.barrier, self.step, self.recv_final, self.iters = barrier, step, recv_final, 2*N + self.gap + len(stages) - 1
+
+
+class NoRing:
+    def __init__(self, N, U, M):
+        self.N, self.U, self.M, self.D = N, U, M, None
+        self.out_units = (2 * N - M) * U
+    def scratch(self): return []
+    def bind(self, *refs): pass
+    def barrier(self): greet(plane(lax.axis_index("section"), lax.axis_index("dp"), lax.axis_index("seq")))
+    def step(self, t): pass
 
 
 def plane(c, z, q):
@@ -499,11 +408,12 @@
     return ((q > 0, q < 3, before), (q < 3, q > 0, after))
 
 
-def front(lengths, inputs, cot_all, params, w_in, conv_w, w_out, dec, mask, types,
-          act, xe_o, ge_o, first1_o, hidden1_o, sec1_o, mixed1_o, third1_o, w_in1_o, conv1_o, w_out1_o, g_o, dgbi, dgbm, dgb, counts,
+def front(lengths, inputs, cot_all, params, w_in, conv_w, w_out,
+          xe_o, out1_o, first1_o, hidden1_o, sec1_o, mixed1_o, third1_o, first2_o, hidden2_o, w_in_o, conv1_o, w_out_o, pr_o, g_o,
+          third2, dsec2, dgb,
           WI, WC, WO, PR, xe, cot, out1, first1, hidden1, sec1, mixed1, third1, first2, hidden2, sec2, dth2, sp, dthr, thirdr, dpad, dsecr,
-          third2, dsec2, out2, ge, G, fe, he, me, mx, dh, hold,
-          ws, wr, wl, xs, xr, xl, ss, rs, ls, gs, gr, os_, acs, acr):
+          G, fe, he, me, mx, hold,
+          ws, wr, wl, xs, xr, xl, ss, rs, ls, os_):
     c, z, q = lax.axis_index("section"), lax.axis_index("dp"), lax.axis_index("seq")
     peer = (1 - c, z, q)
     seg, D = cot.shape[1:]
@@ -532,19 +442,16 @@
     @pl.when(q == 0)
     def _():
         xe[:, pl.ds(0, HALO)] = jnp.zeros((2, HALO, D), BF)
-        ge[:, pl.ds(0, HALO)] = jnp.zeros((2, HALO, D), BF)
 
     @pl.when(q == 3)
     def _():
         xe[:, pl.ds(HALO + seg, HALO)] = jnp.zeros((2, HALO, D), BF)
-        ge[:, pl.ds(HALO + seg, HALO)] = jnp.zeros((2, HALO, D), BF)
 
     def have(i):
         loads[i].wait()
         sends[i].wait_recv()
 
-    for ref in (dgbi, dgbm, dgb, counts):
-        ref[...] = jnp.zeros_like(ref)
+    dgb[...] = jnp.zeros_like(dgb)
     zero = jnp.zeros((2, 64, H), BF)
     for ref in (sp, dpad):
         ref[pl.ds(0, 2)] = zero
@@ -652,17 +559,11 @@
 
     lax.fori_loop(0, 2, third_grad, 0)
     saves = [out_copy(s, d) for s, d in ((xe, xe_o), (first1, first1_o), (hidden1, hidden1_o), (sec1, sec1_o), (mixed1, mixed1_o),
-                                         (third1, third1_o), (WI.at[0], w_in1_o), (WC.at[0], conv1_o), (WO.at[0], w_out1_o))]
+                                         (third1, third1_o), (WI, w_in_o), (WC.at[0], conv1_o), (WO, w_out_o), (PR, pr_o),
+                                         (out1, out1_o), (first2, first2_o), (hidden2, hidden2_o))]
     for cp in saves:
         cp.start()
 
-    def place(i, src, layer):
-        here = out_copy(src, act.at[pl.ds(2 * c, 2)])
-        there = remote(src, act.at[pl.ds(2 * c, 2)], acs.at[i], acr.at[0], peer)
-        both_ways(c == layer, here.start, there.start)
-        return lambda: both_ways(c == layer, here.wait, there.wait_send)
-
-    done1 = place(0, out1, 0)
     for m in range(2):
         spread.go(0, sec2, sp_at, m, False)
     spread.arrive(0, sec2, sp_at)
@@ -704,11 +605,11 @@
     dm = dpad[pl.ds(2, 8)].reshape(512, H)
 
     def conv_grads(k, _):
-        put_grad(G, CONV0 + k * 100, dot_tn(sp[pl.ds(k, 8)].reshape(512, H), dm))
+        put_grad(G, k * 100, dot_tn(sp[pl.ds(k, 8)].reshape(512, H), dm))
         return 0
 
     lax.fori_loop(0, 5, conv_grads, 0)
-    g_conv = out_copy(G.at[:, pl.ds(CONV0, 500)], g_o.at[:, pl.ds(CONV0, 500)])
+    g_conv = out_copy(G, g_o)
     g_conv.start()
     for p in range(4):
         spread.back(2, thirdr, third2, p, False)
@@ -716,126 +617,296 @@
     for m in range(2):
         spread.back_arrive(2, thirdr, third2, m)
         spread.back_arrive(3, dsecr, dsec2, m)
-    labels = lax.broadcasted_iota(jnp.int32, (1, 128), 1)
-
-    def backward(m, _):
-        length = lengths[2 * c + m]
-        t = third2[m].reshape(seg, H)
-        he[pl.ds(0, seg)] = dot(t, WO[1, :, :H])
-        me[...] = dot(t, WO[1, :, H:])
-
-        def a(i, size):
-            r = pl.ds(i, size)
-            for j in range(nd):
-                br = he[r, cols(j)] if j < nh else me[r, cols(j - nh)]
-                out2[m, r, cols(j)] = (out1[m, r, cols(j)].astype(F32) + br).astype(BF)
-
-        chunks(seg, a)
-        logits = jnp.where(labels < 30, dot(out2[m], dec[...]), -1e30)
-        ex = jnp.exp(logits - jnp.max(logits, axis=-1, keepdims=True))
-        probs = ex / jnp.sum(ex, axis=-1, keepdims=True)
-        weight = jnp.where(positions(base, 0, seg) < length, mask[2 * c + m].astype(F32), 0.0)
-        counts[...] += fold(jnp.where(types[2 * c + m] == labels, probs * weight, 0.0))
-
-        def b(jj, _):
-            r = pl.ds(pl.multiple_of(jj * 64, 64), 64)
-            pos = positions(base, jj * 64, 64)
-            u, h = lax.div(jj, 2), lax.rem(jj, 2)
-            ds = lambda j: jnp.where(pos < length, dsec2[m, u, h, :, cols(j)].astype(F32), 0.0)
-            norm_gelu_back(view(hidden2, m, r), ds, nh, gm(1, 0), bm(1, 0), dgbm.at[0], dgbm.at[1], hold, put(dh, m, r))
-            return 0
-
-        lax.fori_loop(0, seg // 64, b, 0)
-        he[pl.ds(0, seg)] = dot_nt(dh[m], WI[1, :H])
-        me[...] = dot_nt(dh[m], WI[1, H:])
-
-        def e(i, size):
-            r = pl.ds(i, size)
-            df = lambda j: he[r, cols(j)] if j < nh else me[r, cols(j - nh)]
-
-            def store(j, v):
-                ge[m, pl.ds(i + HALO, size), cols(j)] = (cot[m, r, cols(j)].astype(F32) + v).astype(BF)
-
-            norm_gelu_back(view(out1, m, r), df, nd, gi(1), bi(1), dgbi.at[0], dgbi.at[1], hold, store)
-
-        chunks(seg, e)
-        for cond, _, cp in edges(ge, m, seg, gs, gr, z, q, c):
-            pl.when(cond)(cp.start)
-        return 0
-
-    lax.fori_loop(0, 2, backward, 0)
-    done2 = place(1, out2, 1)
-    flat = lambda v: v.reshape(2 * seg, v.shape[-1])
-    t2 = flat(third2[...])
-    for j in range(2):
-        put_grad(G, OUT0, dot_tn(t2, flat(cot[:, :, pl.ds(j * H, H)])), nh * j)
-    put_grad(G, IN0, dot_tn(flat(first2[...]), flat(dh[...])))
-    g_rest = out_copy(G.at[:, pl.ds(0, CONV0)], g_o.at[:, pl.ds(0, CONV0)])
-    g_rest.start()
-    for m in range(2):
-        for s_cond, r_cond, cp in edges(ge, m, seg, gs, gr, z, q, c):
-            pl.when(s_cond)(cp.wait_send)
-            pl.when(r_cond)(cp.wait_recv)
-    g_ge = out_copy(ge, ge_o)
-    g_ge.start()
-    for cp in saves + [g_conv, g_rest, g_ge]:
+    for cp in saves + [g_conv]:
         cp.wait()
-    done1()
-    done2()
-    remote(out1, act.at[pl.ds(2 * (1 - c), 2)], acs.at[0], acr.at[0], peer).wait_recv()
     for cp in sends:
         cp.wait_send()
     for cond, _, cp in halos:
         pl.when(cond)(cp.wait_send)
 
 
-def run_front(lengths, inputs, cot, params, w_in, conv_w, w_out, dec, mask, types):
+def run_front(lengths, inputs, cot, params, w_in, conv_w, w_out):
     seg, D, H = inputs.shape[2], inputs.shape[3], w_in.shape[2]
     rows = seg + 2 * HALO
     any_, vm, sm = (pl.BlockSpec(memory_space=s) for s in (pl.ANY, pltpu.VMEM, pltpu.SMEM))
     sh = jax.ShapeDtypeStruct
     dma = lambda *s: pltpu.SemaphoreType.DMA(s)
-    saved = [((2, rows, D), BF), ((2, rows, D), BF), ((2, seg, D), BF), ((2, seg, H), F32), ((2, rows + 16, H), F32), ((2, rows, H), F32),
-             ((2, seg, H), BF), ((D, H), BF), ((5, H, H), BF), ((H, D), BF), ((2, UNITS, 16, 128), BF)]
-    small = [((2, 8, D), F32), ((2, 8, H), F32), ((2, 8, H), F32), ((8, 128), F32)]
     part = (2, 2, 2, 64, H)
+    saved = [((2, rows, D), BF), ((2, seg, D), BF), ((2, seg, D), BF), ((2, seg, H), F32), ((2, rows + 16, H), F32),
+             ((2, rows, H), F32), ((2, seg, H), BF), ((2, seg, D), BF), ((2, seg, H), F32), ((2, D, H), BF), ((5, H, H), BF), ((2, H, D), BF),
+             ((2, 8, D), F32), ((2, 500, 16, 128), BF), (part, BF), (part, BF)]
     scratch = [((2, D, H), BF), ((2, 5, H, H), BF), ((2, H, D), BF), ((2, 8, D), F32), ((2, rows, D), BF), ((2, seg, D), BF),
                ((2, seg, D), BF), ((2, seg, D), BF), ((2, seg, H), F32), ((2, rows + 16, H), F32), ((2, rows, H), F32), ((2, seg, H), BF),
                ((2, seg, D), BF), ((2, seg, H), F32), (part, BF), (part, BF), ((12, 64, H), BF), ((8, 64, H), BF), ((8, 64, H), BF),
-               ((12, 64, H), BF), ((8, 64, H), BF), (part, BF), (part, BF), ((2, seg, D), BF), ((2, rows, D), BF), ((2, UNITS, 16, 128), BF),
-               ((rows, D), BF), ((rows, H), F32), ((seg, H), F32), ((8, 64, H), F32), ((2, seg, H), BF), ((2, 64, D), F32)]
+               ((12, 64, H), BF), ((8, 64, H), BF), ((2, 500, 16, 128), BF),
+               ((rows, D), BF), ((rows, H), F32), ((seg, H), F32), ((8, 64, H), F32), ((2, 64, D), F32)]
     return pl.pallas_call(
         front,
-        out_shape=[sh((4, seg, D), BF)] + [sh(s, d) for s, d in saved + small],
-        in_specs=[sm, any_, any_, any_, any_, any_, any_, vm, vm, vm],
-        out_specs=[any_] * (1 + len(saved)) + [vm] * len(small),
+        out_shape=[sh(s, d) for s, d in saved] + [sh((2, 8, H), F32)],
+        in_specs=[sm] + [any_] * 6,
+        out_specs=[any_] * len(saved) + [vm],
         scratch_shapes=[pltpu.VMEM(s, d) for s, d in scratch]
-        + [dma(8), dma(8), dma(8), dma(2, 2), dma(2, 2), dma(4), dma(4, 4), dma(4, 4), dma(4), dma(2, 2), dma(2, 2), dma(16), dma(2), dma(1)],
+        + [dma(8), dma(8), dma(8), dma(2, 2), dma(2, 2), dma(4), dma(4, 4), dma(4, 4), dma(4), dma(20)],
         compiler_params=pltpu.CompilerParams(collective_id=1, has_side_effects=True, vmem_limit_bytes=62 * 2**20),
-    )(lengths, inputs, cot, params, w_in, conv_w, w_out, dec, mask, types)
-
-
-def call(fn, outs, scratch, args, scal_at=(), layer={}):
-    vm = pl.BlockSpec(memory_space=pltpu.VMEM)
-    whole, place = [], []
-    for a in args:
-        if not any(a is w for w in whole):
-            whole.append(a)
-        place.append(next(i for i, w in enumerate(whole) if w is a))
-    specs = [pl.BlockSpec(memory_space=pltpu.SMEM) if place.index(i) in scal_at else vm for i in range(len(whole))]
-
-    def kernel(*refs):
-        ins = [refs[p].at[pl.ds(layer[i], 1)] if i in layer else refs[p] for i, p in enumerate(place)]
-        fn(*ins, *refs[len(whole):])
-
+    )(lengths, inputs, cot, params, w_in, conv_w, w_out)
+
+
+def back(lengths, cot_all, dec, mask, types, dgb, conv, xe_h, out1_h, first1_h, hidden1_h, sec1_h, mixed1_h, third1_h, first2_h, hidden2_h,
+         third2_h, dsec2_h, w_in_h, conv1_h, w_out_h, pr_h,
+         act, igr, total, cnt,
+         WI, WO2, WO1, WC, PR, xo, ge, cot, og, first, hidden, third, dsec, dh, sec1, mixed1, he, me, dme, swin, hold, dgbi, dgbm, counts, GV,
+         ls, gs, gr, ps, pr, *ring_refs, ring):
+    c, z, q = lax.axis_index("section"), lax.axis_index("dp"), lax.axis_index("seq")
+    peer = (1 - c, z, q)
+    seg, D = cot.shape[1:]
+    H = hidden.shape[2]
+    nd, nh = D // 128, H // 128
+    rows = seg + 2 * HALO
+    base = q * seg
+    N, U, M = ring.N, ring.U, ring.M
+    low = N * U - M * U
+    head = low - CONV0
+    ring.first = head
+    ring.bind(conv, GV, total, *ring_refs)
+    count = [0]
+
+    def load(src, dst):
+        cp = pltpu.make_async_copy(src, dst, ls.at[count[0]])
+        count[0] += 1
+        return cp
+
+    out1, xe = xo.at[:, pl.ds(0, seg)], xo
+    l_ring = [] if ring.D is None else [load(conv.at[c, pl.ds(head + i * U, U)], ring.D.at[i]) for i in range(M)]
+    l_two = [load(s, d) for s, d in ((pr_h, PR), (third2_h, third), (w_out_h.at[1], WO2), (out1_h, out1), (dsec2_h, dsec), (hidden2_h, hidden),
+                                     (w_in_h.at[1], WI))]
+    l_two += [load(cot_all.at[2 * c + m, 0], cot.at[m]) for m in range(2)]
+    l_grad = [load(first2_h, first), load(conv.at[:, pl.ds(0, head)], GV.at[:, pl.ds(CONV0, head)])]
+    l_one = [load(s, d) for s, d in ((w_out_h.at[0], WO1), (conv1_h, WC), (mixed1_h, mixed1), (sec1_h, sec1))]
+    for cp in l_ring + l_two + l_grad + l_one:
+        cp.start()
+    ring.barrier()
+    ring.step(0)
+
+    @pl.when(q == 0)
+    def _():
+        ge[:, pl.ds(0, HALO)] = jnp.zeros((2, HALO, D), BF)
+
+    @pl.when(q == 3)
+    def _():
+        ge[:, pl.ds(HALO + seg, HALO)] = jnp.zeros((2, HALO, D), BF)
+
+    for ref in (dgbi, dgbm, counts):
+        ref[...] = jnp.zeros_like(ref)
+    gi, bi = lambda l: row(PR.at[l], 0), lambda l: row(PR.at[l], 1)
+    gm = lambda l, k: (lambda j: PR[l, pl.ds(2, 1), cols(k * nh + j)])
+    bm = lambda l, k: (lambda j: PR[l, pl.ds(3, 1), cols(k * nh + j)])
+    for cp in l_two + l_ring:
+        cp.wait()
+    labels = lax.broadcasted_iota(jnp.int32, (1, 128), 1)
+
+    def two(m, _):
+        length = lengths[2 * c + m]
+        he[pl.ds(0, seg)] = dot(third[m], WO2[:, :H])
+        me[...] = dot(third[m], WO2[:, H:])
+
+        def a(i, size):
+            r = pl.ds(i, size)
+            for j in range(nd):
+                br = he[r, cols(j)] if j < nh else me[r, cols(j - nh)]
+                og[m, r, cols(j)] = (out1[m, r, cols(j)].astype(F32) + br).astype(BF)
+
+        chunks(seg, a)
+        logits = jnp.where(labels < 30, dot(og[m], dec[...]), -1e30)
+        ex = jnp.exp(logits - jnp.max(logits, axis=-1, keepdims=True))
+        probs = ex / jnp.sum(ex, axis=-1, keepdims=True)
+        weight = jnp.where(positions(base, 0, seg) < length, mask[2 * c + m].astype(F32), 0.0)
+        counts[...] += fold(jnp.where(types[2 * c + m] == labels, probs * weight, 0.0))
+
+        def b(i, size):
+            r = pl.ds(i, size)
+            pos = positions(base, i, size)
+            ds = lambda j: jnp.where(pos < length, dsec[m, r, cols(j)].astype(F32), 0.0)
+            norm_gelu_back(view(hidden, m, r), ds, nh, gm(1, 0), bm(1, 0), dgbm.at[0], dgbm.at[1], hold, put(dh, m, r))
+
+        chunks(seg, b)
+        he[pl.ds(0, seg)] = dot_nt(dh[m], WI[:H])
+        me[...] = dot_nt(dh[m], WI[H:])
+
+        def e(i, size):
+            r = pl.ds(i, size)
+            df = lambda j: he[r, cols(j)] if j < nh else me[r, cols(j - nh)]
+
+            def store(j, v):
+                ge[m, pl.ds(i + HALO, size), cols(j)] = (cot[m, r, cols(j)].astype(F32) + v).astype(BF)
+
+            norm_gelu_back(view(out1, m, r), df, nd, gi(1), bi(1), dgbi.at[0], dgbi.at[1], hold, store)
+
+        chunks(seg, e)
+        for cond, _, cp in edges(ge, m, seg, gs, gr, z, q, c):
+            pl.when(cond)(cp.start)
+        ring.step(1 + m)
+        return 0
+
+    lax.fori_loop(0, 2, two, 0)
+
+    def place(i, src, dst, layer):
+        here = load(src, dst.at[pl.ds(2 * c, 2)])
+        there = remote(src, dst.at[pl.ds(2 * c, 2)], ps.at[i], pr.at[i // 2], peer)
+        both_ways(c == layer, here.start, there.start)
+        return lambda: both_ways(c == layer, here.wait, there.wait_send)
+
+    inside = ge.at[:, pl.ds(HALO, seg)]
+    placed = [place(0, out1, act, 0), place(1, og, act, 1), place(2, inside, igr, 1)]
+    flat = lambda v: v.reshape(2 * seg, v.shape[-1])
+    for cp in l_grad:
+        cp.wait()
+    t2 = flat(third[...])
+    for j in range(2):
+        put_grad(GV, OUT0, dot_tn(t2, flat(cot[:, :, pl.ds(j * H, H)])), nh * j)
+    put_grad(GV, IN0, dot_tn(flat(first[...]), flat(dh[...])))
+
+    def extra(first_unit, third_norm, with_counts):
+        flat_rows = [dgbi[k, :, cols(j)] for k in range(2) for j in range(nd)]
+        flat_rows += [dgbm[k, :, cols(j)] for k in range(2) for j in range(nh)]
+        flat_rows += [third_norm(k, j) for k in range(2) for j in range(nh)]
+        small = [jnp.sum(v, axis=0, keepdims=True) for v in flat_rows]
+        small.append(jnp.sum(counts[...], axis=0, keepdims=True) if with_counts else jnp.zeros((1, 128), F32))
+        small.append(jnp.zeros((192 - len(small), 128), F32))
+        block = jnp.concatenate(small, axis=0).astype(BF).reshape(12, 16, 128)
+        for h in range(2):
+            GV[h, pl.ds(first_unit, 12)] = block
+
+    extra(0, lambda k, j: dgb[k, :, cols(j)], True)
+    l_late = [load(s, d) for s, d in ((third1_h, third), (hidden1_h, hidden), (w_in_h.at[0], WI), (first1_h, first))]
+    for cp in l_late:
+        cp.start()
+    ring.step(3)
+    for ref in (dgbi, dgbm):
+        ref[...] = jnp.zeros_like(ref)
+    for m in range(2):
+        for s_cond, r_cond, cp in edges(ge, m, seg, gs, gr, z, q, c):
+            pl.when(s_cond)(cp.wait_send)
+            pl.when(r_cond)(cp.wait_recv)
+    for cp in l_one + l_late[1:3]:
+        cp.wait()
+    for done in placed[:2]:
+        done()
+    l_x = load(xe_h, xe)
+    l_x.start()
+    ring.step(4)
+
+    def one(m, _):
+        length = lengths[2 * c + m]
+        he[...] = dot_nt(ge[m], WO1[...])
+
+        def a(i, size):
+            r = pl.ds(i + HALO, size)
+
+            def store(j, v):
+                v = v.astype(BF)
+                dme[r, cols(j)] = v.astype(F32)
+                dsec[m, pl.ds(i, size), cols(j)] = v
+
+            norm_gelu_back(view(mixed1, m, r), view(he, r), nh, gm(0, 1), bm(0, 1), dgbm.at[2], dgbm.at[3], hold, store)
+
+        chunks(seg, a)
+        for edge in (0, rows - HALO):
+            r = pl.ds(edge, HALO)
+            pos = positions(base - HALO, edge, HALO)
+            within = jnp.logical_and(pos >= 0, pos < 4 * seg)
+
+            def store(j, v):
+                dme[r, cols(j)] = jnp.where(within, v, 0.0).astype(BF).astype(F32)
+
+            norm_gelu_back(view(mixed1, m, r), view(he, r), nh, gm(0, 1), bm(0, 1), None, None, hold.at[:, pl.ds(0, HALO)], store)
+        ring.step(5 + 2 * m)
+        acc = None
+        for k in range(5):
+            term = dot_nt(dme[pl.ds(HALO - DIL * (k - 2), seg)].astype(BF), WC[k])
+            acc = term if acc is None else acc + term
+        he[pl.ds(0, seg)] = acc
+
+        def b(i, size):
+            r = pl.ds(i, size)
+            pos = positions(base, i, size)
+            ds = lambda j: jnp.where(pos < length, he[r, cols(j)], 0.0)
+            norm_gelu_back(view(hidden, m, r), ds, nh, gm(0, 0), bm(0, 0), dgbm.at[0], dgbm.at[1], hold, put(dh, m, r))
+
+        chunks(seg, b)
+        he[pl.ds(0, seg)] = dot_nt(dh[m], WI[:H])
+        me[...] = dot_nt(dh[m], WI[H:])
+
+        @pl.when(m == 0)
+        def _():
+            l_x.wait()
+
+        def e(i, size):
+            r, x = pl.ds(i, size), pl.ds(i + HALO, size)
+            df = lambda j: he[r, cols(j)] if j < nh else me[r, cols(j - nh)]
+
+            def store(j, v):
+                og[m, r, cols(j)] = (ge[m, x, cols(j)].astype(F32) + v).astype(BF)
+
+            norm_gelu_back(view(xe, m, x), df, nd, gi(0), bi(0), dgbi.at[0], dgbi.at[1], hold, store)
+
+        chunks(seg, e)
+        ring.step(6 + 2 * m)
+        return 0
+
+    lax.fori_loop(0, 2, one, 0)
+    placed.append(place(3, og, igr, 0))
+    for cp in (l_late[0], l_late[3]):
+        cp.wait()
+    t1 = flat(third[...])
+    for j in range(2):
+        put_grad(GV, low + OUT0, dot_tn(t1, flat(ge[:, pl.ds(HALO, seg), pl.ds(j * H, H)])), nh * j)
+    put_grad(GV, low + IN0, dot_tn(flat(first[...]), flat(dh[...])))
+    extra(low, lambda k, j: dgbm[2 + k, :, cols(j)], False)
+    d1 = flat(dsec[...])
+    for k in range(5):
+        for m in range(2):
+            swin[pl.ds(m * seg, seg)] = sec1[m, pl.ds(8 + HALO + DIL * (k - 2), seg)].astype(BF)
+        put_grad(GV, low + CONV0 + k * 100, dot_tn(swin[...], d1))
+
+    def rest(t, _):
+        ring.step(t)
+        return 0
+
+    if ring.D is None:
+        l_all = load(GV, total)
+        l_all.start()
+        l_all.wait()
+        cnt[...] = jnp.zeros_like(cnt)
+    else:
+        lax.fori_loop(9, ring.iters, rest, 0)
+        ring.recv_final()
+        cnt[...] = ring.D[M, pl.ds(EXTRA0, 12)]
+    for done in placed[2:]:
+        done()
+    for i, dst in ((0, act), (1, igr)):
+        remote(og, dst.at[pl.ds(2 * (1 - c), 2)], ps.at[0], pr.at[i], peer).wait_recv()
+
+
+def run_back(ring, lengths, cot, dec, mask, types, dgb, conv, saved):
+    seg, D, H = cot.shape[2], cot.shape[3], saved[3].shape[-1]
+    rows = seg + 2 * HALO
+    N, M, U = ring.N, ring.M, ring.U
+    any_, vm, sm = (pl.BlockSpec(memory_space=s) for s in (pl.ANY, pltpu.VMEM, pltpu.SMEM))
+    sh = jax.ShapeDtypeStruct
+    dma = lambda *s: pltpu.SemaphoreType.DMA(s)
+    scratch = [((D, H), BF), ((H, D), BF), ((H, D), BF), ((5, H, H), BF), ((2, 8, D), F32), ((2, rows, D), BF), ((2, rows, D), BF),
+               ((2, seg, D), BF), ((2, seg, D), BF), ((2, seg, D), BF), ((2, seg, H), F32), ((2, seg, H), BF), ((2, seg, H), BF),
+               ((2, seg, H), BF), ((2, rows + 16, H), F32), ((2, rows, H), F32), ((rows, H), F32), ((seg, H), F32), ((rows, H), F32),
+               ((2 * seg, H), BF), ((2, 64, D), F32), ((2, 8, D), F32), ((4, 8, H), F32), ((8, 128), F32),
+               ((2, (2 * N - M) * U, 16, 128), BF)]
     return pl.pallas_call(
-        kernel,
-        out_shape=[jax.ShapeDtypeStruct(s, d) for s, d in outs],
-        in_specs=specs,
-        out_specs=[vm] * len(outs),
-        scratch_shapes=[pltpu.VMEM(s, d) for s, d in scratch],
-        compiler_params=pltpu.CompilerParams(vmem_limit_bytes=60 * 2**20),
-    )(*whole)
+        functools.partial(back, ring=ring),
+        out_shape=[sh((4, seg, D), BF), sh((4, seg, D), BF), sh((2, ring.out_units, 16, 128), BF), sh((12, 16, 128), BF)],
+        in_specs=[sm, any_, vm, vm, vm, vm] + [any_] * (1 + len(saved)),
+        out_specs=[any_, any_, any_, vm],
+        scratch_shapes=[pltpu.VMEM(s, d) for s, d in scratch] + [dma(32), dma(2, 2), dma(2, 2), dma(4), dma(2)] + ring.scratch(),
+        compiler_params=pltpu.CompilerParams(collective_id=2, has_side_effects=True, vmem_limit_bytes=63 * 2**20),
+    )(lengths, cot, dec, mask, types, dgb, conv, *saved)
 
 
 def unpack_kernel(conv, w_out, w_in, extra, cnt, s_conv, s_out, s_in, gi, bi, gm, bm, counts):
@@ -864,7 +935,7 @@
 
 def unpack(total, cnt, D, H):
     def spec(units, first):
-        return pl.BlockSpec((2, units, 16, 128), lambda k: (0, first + k, 0, 0))
+        return pl.BlockSpec(tuple(pl.Element(n) for n in (2, units, 16, 128)), lambda k: (0, first + units * k, 0, 0))
 
     def full(*s):
         return pl.BlockSpec(s, lambda k: (0,) * len(s))
@@ -874,7 +945,7 @@
         unpack_kernel,
         grid=(5,),
         out_shape=[sh(1, 5, H, H), sh(1, H, D), sh(1, D, H), sh(1, D), sh(1, D), sh(1, 2, H), sh(1, 2, H), sh(1, 128)],
-        in_specs=[spec(100, CONV0 // 100), spec(40, 0), spec(40, 5), pl.BlockSpec((2, 12, 16, 128), lambda k: (0, 75, 0, 0)), full(12, 16, 128)],
+        in_specs=[spec(100, CONV0), spec(40, OUT0), spec(40, IN0), pl.BlockSpec((2, 12, 16, 128), lambda k: (0, 0, 0, 0)), full(12, 16, 128)],
         out_specs=[pl.BlockSpec((1, 1, H, H), lambda k: (0, k, 0, 0)), pl.BlockSpec((1, H, 256), lambda k: (0, 0, k)),
                    pl.BlockSpec((1, D, 128), lambda k: (0, 0, k)), full(1, D), full(1, D), full(1, 2, H), full(1, 2, H), full(1, 128)],
         compiler_params=pltpu.CompilerParams(vmem_limit_bytes=60 * 2**20),
@@ -882,48 +953,26 @@
 
 
 def body(inputs, lengths, mlm_mask, true_types, gain_in, bias_in, gain_mid, bias_mid, w_in, conv_w, w_out, decoder, cotangent, fast):
-    c = lax.axis_index("section")
     seg, D, H = inputs.shape[2], inputs.shape[3], w_in.shape[2]
-    rows = seg + 2 * HALO
     params = jnp.concatenate([gain_in, bias_in, gain_mid.reshape(1, D), bias_mid.reshape(1, D), jnp.zeros((4, D), BF)]).astype(F32)
     dec = jnp.pad(decoder, ((0, 0), (0, 128 - decoder.shape[1])))
-    (act, xe, ge, first1, hidden1, sec1, mixed1, third1, w_in1, conv1, w_out1, g_two, dgbi2, dgbm2, dgb2, counts) = run_front(
-        lengths[:, 0], inputs, cotangent, params, w_in, conv_w, w_out, dec, mlm_mask[:, 0][..., None], true_types[:, 0][..., None])
-    q = lax.axis_index("seq")
-    scal = jnp.concatenate([jnp.reshape(q * seg, (1,)), lax.dynamic_slice_in_dim(lengths[:, 0], 2 * c, 2, 0)]).astype(jnp.int32)
-    both = lambda w: lax.all_gather(w, "section", axis=0, tiled=True)
-    gi, bi, gm, bm = (both(v.astype(F32)) for v in (gain_in, bias_in, gain_mid, bias_mid))
-    grad1, dgbi1, dgbm1, g_one = call(
-        k4,
-        [((2, seg, D), BF), ((2, 8, D), F32), ((4, 8, H), F32), ((2, 900, 16, 128), BF)],
-        [((rows, H), F32), ((seg, H), F32), ((rows, H), F32), ((2, seg, H), BF), ((2, seg, H), BF), ((2 * seg, H), BF), ((2, 64, D), F32)],
-        (xe, ge, scal, first1, hidden1, sec1, mixed1, third1, w_in1[None], conv1[None], w_out1[None], gi[:1], bi[:1], gm[0], bm[0]),
-        (2,), {8: 0, 9: 0, 10: 0})
-
-    def extra(dgbi, dgbm, cnt):
-        flat = jnp.concatenate([dgbi.sum(1).reshape(-1), dgbm.sum(1).reshape(-1), cnt.sum(0)])
-        flat = jnp.pad(flat, (0, 12 * 2048 - flat.shape[0])).astype(BF).reshape(1, 12, 16, 128)
-        return jnp.concatenate([flat, flat], 0)
-
-    g_two = jnp.concatenate([g_two[:, :EXTRA0], extra(dgbi2, jnp.concatenate([dgbm2, dgb2]), counts)], 1)
-    g_one = jnp.concatenate([g_one, extra(dgbi1, dgbm1, jnp.zeros_like(counts))], 1)
-    if fast:
-        N, PU, QU = 6, 88, 64
-        total, cnt = allreduce(g_one, g_two, N, PU, QU)
-        total = total.reshape(2, UNITS, 16, 128)
-    else:
+    line = lengths[:, 0]
+    (xe, out1, first1, hidden1, sec1, mixed1, third1, first2, hidden2, w_in_b, conv1, w_out_b, pr, g_conv, third2, dsec2, dgb) = run_front(
+        line, inputs, cotangent, params, w_in, conv_w, w_out)
+    rows_of = lambda v: v.reshape(2, seg, H)
+    act, igr, total, cnt = run_back(
+        Ring(6, 88, 64, 3, 3) if fast else NoRing(6, 152, 3),
+        line, cotangent, dec, mlm_mask[:, 0][..., None], true_types[:, 0][..., None], dgb, g_conv,
+        (xe, out1, first1, hidden1, sec1, mixed1, third1, first2, hidden2, rows_of(third2), rows_of(dsec2), w_in_b, conv1, w_out_b, pr))
+    if not fast:
+        c = lax.axis_index("section")
+        g_one, g_two = total[:, 456:], jnp.concatenate([total[:, :456], g_conv[:, 44:]], 1)
         own, other = jnp.where(c == 0, g_one, g_two), jnp.where(c == 0, g_two, g_one)
         got = lax.ppermute(other, "section", [(0, 1), (1, 0)])
         total = lax.psum(own.astype(F32) + got.astype(F32), ("dp", "seq")).astype(BF)
-        cnt = lax.psum(g_two[0, EXTRA0:].astype(F32), ("section", "dp", "seq")).astype(BF)
+        cnt = lax.psum(g_two[0, :12].astype(F32), ("section", "dp", "seq")).astype(BF)
     s_conv, s_out, s_in, s_gi, s_bi, s_gm, s_bm, s_cnt = unpack(total, cnt, D, H)
-
-    def placed(one, two):
-        own, other = jnp.where(c == 0, one, two), jnp.where(c == 0, two, one)
-        got = lax.ppermute(other, "section", [(0, 1), (1, 0)])
-        return jnp.where(c == 0, jnp.concatenate([own, got]), jnp.concatenate([got, own]))[None, :, None]
-
-    return (act[None, :, None], placed(grad1, ge[:, HALO : HALO + seg]), s_gi, s_bi, s_gm, s_bm, s_in, s_conv, s_out, s_cnt[0, : decoder.shape[1]])
+    return (act[None, :, None], igr[None, :, None], s_gi, s_bi, s_gm, s_bm, s_in, s_conv, s_out, s_cnt[0, : decoder.shape[1]])
 
 
 def solution(mesh):

time: 326 us -> 263 us (0.81)
  Pallas kernels: 275 us -> 248 us
  other arithmetic: 24.7 us -> 2.04 us
  blocking collectives: 7.3 us -> 0 us
  local copies, waits for them, and re-layouts: 16.3 us -> 11.4 us
    pallas_call x3 -> x2, Pallas kernels: 266 us -> 239 us  [the longest x1 172 us: run_back(): pl.pallas_call(functools.partial(back, ring=ring), out_shape=[sh((4, seg,...]
    concatenate x6 -> x0, other arithmetic: 13.2 us -> none  [the longest x1 5.53 us: body(): jnp.concatenate([g_one, extra(dgbi1, dgbm1, jnp.zeros_like(counts))], 1)]
    all_gather x4 -> x0, blocking collectives: 7.3 us -> none  [body(): both = lambda w: lax.all_gather(w, 'section', axis=0, tiled=True)]
    slice x3 -> x0, local copies, waits for them, and re-layouts: 5.55 us -> none  [the longest x1 4.36 us: body(): g_two[:, :EXTRA0]]
    unnamed x6 -> x2, other arithmetic: 5.94 us -> 1.42 us
    reduce_sum x5 -> x0, other arithmetic: 3.61 us -> none  [the longest x2 1.84 us: extra(): dgbi.sum(1).reshape(-1)]
    unnamed x14 -> x9, local copies, waits for them, and re-layouts: 4.01 us -> 6.68 us
  transfers between devices with their start and end apart: 1 -> 0, of which waited for: 0 -> 0; matrix products, arithmetic and copies ran while one was open for 6% -> 0% of each run, Pallas kernels for 48% -> 0%
where the time goes in v3:
time: 263 us; the launch traced here: 262 us
  Pallas kernels  248 us (94%)
  local copies, waits for them, and re-layouts  11.4 us (4%)
    pallas_call x1, Pallas kernels, run_back(): pl.pallas_call(functools.partial(back, ring=ring), out_shape=[sh((4, seg,...  172 us
    pallas_call x1, Pallas kernels, run_front(): pl.pallas_call(front, out_shape=[sh(s, d) for s, d in saved] + [sh((2, 8,...  66.9 us
    pallas_call x1, Pallas kernels, unpack(): pl.pallas_call(unpack_kernel, grid=(5,), out_shape=[sh(1, 5, H, H), sh(1,...  9.23 us
    unnamed x9, local copies, waits for them, and re-layouts  6.68 us

profile of v3, /device:TPU:0, one launch (start us, length us, event | category | flops | bytes accessed | tf_op | source)
XLA Modules:
  0.0 262.3 jit_solution(6854565650263518371)
XLA Ops:
  0.6 0.7 reduce
  1.4 0.7 reduce.1
  2.1 0.7 copy.31
  2.7 0.7 copy.32
  3.4 0.8 concatenate.3
  4.2 0.6 convert_element_type.5.params
  4.8 1.1 copy.26
  5.9 0.8 pad.4.dec
  6.7 1.0 broadcast_in_dim_squeeze.9.types
  7.7 1.0 broadcast_in_dim_squeeze.8.mask
  8.7 66.9 %shard_map.204 = (bf16[2,288,1280]{2,1,0:T(8,128)(2,1)}, bf16[2,256,1280]{2,1,0:T(8,128)(2,1)}, bf16[2,256,1280]{2,1,0:T(8,128)(2,1)}, f32[2,256,640]{2,1,0:T(8,...) custom-call(s32[4]{0:T(128)} %bitcast.23, ...), custom_call_target="tpu_custom_call" | custom-call | tf_op jit(solution)/shard_map/pallas_call | solution.py:643
  75.7 172.0 %shard_map.205 = (bf16[4,256,1280]{2,1,0:T(8,128)(2,1)}, bf16[4,256,1280]{2,1,0:T(8,128)(2,1)}, bf16[2,912,16,128]{3,2,1,0:T(8,128)(2,1)}, bf16[12,16,128]{2,1,0:T(8,128)(2,1)}) custom-call(s32[4]{0:T(128)} %bitcast.24, bf16[4,1,256,1280]{3,2,1,0:T(8,128)(2,1)} %cot_all.3, bf16[1280,128]{1,0:T(8,128)(2,1)} %pad.4.dec, ...), custom_call_target="tpu_custom_call" | custom-call | tf_op jit(solution)/shard_map/pallas_call | solution.py:902
  247.7 0.0 copy-start.1
  247.7 9.2 %shard_map.206 = (f32[1,5,640,640]{3,2,1,0:T(8,128)}, f32[1,640,1280]{2,1,0:T(8,128)}, f32[1,1280,640]{2,1,0:T(8,128)}, f32[1,1280]{1,0:T(1,128)}, f32[1,1280]{1...) custom-call(bf16[2,912,16,128]{3,2,1,0:T(8,128)(2,1)} %get-tuple-element.58.conv.w_out.w_in.extra, ...), custom_call_target="tpu_custom_call" | custom-call | tf_op jit(solution)/shard_map/pallas_call | solution.py:944
  257.0 1.2 slice_bitcast_fusion
  258.1 0.0 copy-done.1
  258.1 0.0 copy-start
  258.1 1.5 copy.35
  259.6 1.2 copy-done
  260.8 1.5 copy.36
  (1 shorter events, 0.0 us)
Async XLA Ops:
  247.7 10.4 %copy-start.1 = (bf16[4,256,1280]{2,1,0:T(8,128)(2,1)S(1)}, bf16[4,256,1280]{2,1,0:T(8,128)(2,1)}, u32[]{:S(2)}) copy-start(bf16[4,256,1280]{2,1,0:T(8,128)(2,1)} %get-tuple-element.56) | copy-start | bytes 7864324
  258.1 2.7 %copy-start = (bf16[4,256,1280]{2,1,0:T(8,128)(2,1)S(1)}, bf16[4,256,1280]{2,1,0:T(8,128)(2,1)}, u32[]{:S(2)}) copy-start(bf16[4,256,1280]{2,1,0:T(8,128)(2,1)} %get-tuple-element.57) | copy-start | bytes 7864324

commit v4 on v3

v4 whole, which is shorter than its diff:
```python
import functools

import jax
import jax.numpy as jnp
from jax import lax
from jax.experimental import pallas as pl
from jax.experimental.pallas import tpu as pltpu
from jax.sharding import PartitionSpec as P


EPS = 1e-05
BF, F32 = jnp.bfloat16, jnp.float32
MESH = pl.DeviceIdType.MESH
G0 = 0.7978845608028654
G1 = 0.044715
DIL = 2
HALO = 16
OUT0, CONV0, IN0, EXTRA0, UNITS = 0, 200, 700, 900, 936
PIECES, PLANE_UNITS, Z_UNITS, SLOTS = 13, 48, 24, 8


def dot(a, b):
    return lax.dot_general(a, b, (((1,), (0,)), ((), ())), preferred_element_type=F32)


def dot_nt(a, b):
    return lax.dot_general(a, b, (((1,), (1,)), ((), ())), preferred_element_type=F32)


def dot_tn(a, b):
    return lax.dot_general(a, b, (((0,), (0,)), ((), ())), preferred_element_type=F32)


def chunks(rows, fn, size=None):
    size = size or (96 if rows % 96 == 0 else 64)

    def one(i, _):
        fn(pl.multiple_of(i * size, size), size)
        return 0

    lax.fori_loop(0, rows // size, one, 0)


def cols(j):
    return pl.ds(j * 128, 128)


def stats(load, n):
    total = load(0)
    for j in range(1, n):
        total = total + load(j)
    mean = jnp.sum(total, axis=-1, keepdims=True) * (1.0 / (128 * n))
    square = None
    for j in range(n):
        d = load(j) - mean
        square = d * d if square is None else square + d * d
    var = jnp.sum(square, axis=-1, keepdims=True) * (1.0 / (128 * n))
    return mean, lax.rsqrt(var + EPS)


def norm_gelu(load, n, gain, shift, store):
    mean, rstd = stats(load, n)
    for j in range(n):
        u = (load(j) - mean) * rstd * gain(j) + shift(j)
        t = jnp.tanh(u * (G0 + (G0 * G1) * (u * u)))
        h = 0.5 * u
        store(j, h + h * t)


def fold(v):
    rows, width = v.shape
    return jnp.sum(v.reshape(rows // 8, 8, width), axis=0)


def norm_gelu_back(load, dy, n, gain, shift, dgain, dshift, hold, store):
    mean, rstd = stats(load, n)
    s1 = s2 = None
    for j in range(n):
        g = gain(j)
        hat = (load(j) - mean) * rstd
        u = hat * g + shift(j)
        w = u * u
        t = jnp.tanh(u * (G0 + (G0 * G1) * w))
        slope = 0.5 + 0.5 * t + u * (1.0 - t * t) * (0.5 * G0 + (1.5 * G0 * G1) * w)
        du = dy(j) * slope
        if dgain is not None:
            dgain[:, cols(j)] += fold(du * hat)
            dshift[:, cols(j)] += fold(du)
        dh = du * g
        hold[0, :, cols(j)] = hat
        hold[1, :, cols(j)] = dh
        p = dh * hat
        s1 = dh if s1 is None else s1 + dh
        s2 = p if s2 is None else s2 + p
    m1 = jnp.sum(s1, axis=-1, keepdims=True) * (1.0 / (128 * n))
    m2 = jnp.sum(s2, axis=-1, keepdims=True) * (1.0 / (128 * n))
    for j in range(n):
        store(j, rstd * (hold[1, :, cols(j)] - m1 - hold[0, :, cols(j)] * m2))


def norm_gelu_both(load, dy, n, gain, shift, dgain, dshift, hold, store, store_back):
    mean, rstd = stats(load, n)
    s1 = s2 = None
    for j in range(n):
        g = gain(j)
        hat = (load(j) - mean) * rstd
        u = hat * g + shift(j)
        w = u * u
        t = jnp.tanh(u * (G0 + (G0 * G1) * w))
        half = 0.5 + 0.5 * t
        store(j, u * half)
        slope = half + u * (1.0 - t * t) * (0.5 * G0 + (1.5 * G0 * G1) * w)
        du = dy(j) * slope
        dgain[:, cols(j)] += fold(du * hat)
        dshift[:, cols(j)] += fold(du)
        dh = du * g
        hold[0, :, cols(j)] = hat
        hold[1, :, cols(j)] = dh
        p = dh * hat
        s1 = dh if s1 is None else s1 + dh
        s2 = p if s2 is None else s2 + p
    m1 = jnp.sum(s1, axis=-1, keepdims=True) * (1.0 / (128 * n))
    m2 = jnp.sum(s2, axis=-1, keepdims=True) * (1.0 / (128 * n))
    for j in range(n):
        store_back(j, rstd * (hold[1, :, cols(j)] - m1 - hold[0, :, cols(j)] * m2))


def row(ref, k):
    return lambda j: ref[pl.ds(k, 1), cols(j)]


def view(ref, *at):
    return lambda j: ref[(*at, cols(j))].astype(F32)


def put_grad(DG, c, unit, value, col0=0):
    m, n = value.shape
    per = m // 32
    value = value.astype(BF)
    for j in range(n // 128):
        block = value[:, j * 128 : (j + 1) * 128].reshape(m // 16, 16, 128)
        for h in range(2):
            DG[lax.rem(h + c, 2), pl.ds(unit + (col0 + j) * per, per)] = block[h * per : (h + 1) * per]


def put(ref, *at):
    def store(j, v):
        ref[(*at, cols(j))] = v.astype(ref.dtype)

    return store


def positions(first, i, size):
    return first + i + lax.broadcasted_iota(jnp.int32, (size, 1), 0)


class Ring:
    KINDS = ("D", "P1", "P2", "PZ1", "PZ2", "PT1", "PT2", "PT3", "G1", "G2", "Q1", "Q2", "X1", "X2", "X3", "X4", "QT1", "QT2", "QT3", "F")

    def __init__(self, N, PU, QU):
        self.N, self.PU, self.QU, self.U = N, PU, QU, PU + QU
        self.out_units, self.live = N * self.U, True

    def scratch(self):
        PU, QU, U = self.PU, self.QU, self.U
        b = lambda u, n=SLOTS: pltpu.VMEM((n, u, 16, 128), BF)
        sems = pltpu.SemaphoreType.DMA((len(self.KINDS), 2 * self.N))
        return [b(U, 4), b(PU // 2), b(PU // 4), b(PU // 4), b(PU // 8), b(QU), b(QU // 2), b(QU // 4), b(QU // 8), b(PU // 4), b(QU // 8),
                sems, sems]

    def bind(self, DG, out, RD, RP1, RP2, RZ1, RZ2, RQ1, RQ2, RX1, RX2, TQ, TX, ss, rs):
        N, PU, QU, U, ds = self.N, self.PU, self.QU, self.U, pl.ds
        c, z, q = lax.axis_index("section"), lax.axis_index("dp"), lax.axis_index("seq")
        xb, yb = lax.rem(q, 2), lax.div(q, 2)
        f, s = jnp.where(c == 0, xb, yb), jnp.where(c == 0, yb, xb)
        qx, qy = yb * 2 + 1 - xb, (1 - yb) * 2 + xb
        n1 = (c, z, jnp.where(c == 0, qx, qy))
        n2 = (c, z, jnp.where(c == 0, qy, qx))
        side = lax.div(z, 2)
        near, farc = side, 1 - side
        zp = (c, side * 2 + 1 - lax.rem(z, 2), q)
        far = (c, 3 - z, q)
        peer = (1 - c, z, q)
        inner = jnp.logical_or(z == 1, z == 2)
        outer = jnp.logical_not(inner)
        order = {k: i for i, k in enumerate(self.KINDS)}

        def cp(k, i, src, dst, dev):
            return remote(src, dst, ss.at[order[k], i], rs.at[order[k], i], dev)

        def add(dst, *terms):
            acc = terms[0][...].astype(F32)
            for t in terms[1:]:
                acc = acc + t[...].astype(F32)
            dst[...] = acc.astype(BF)

        def phys(i):
            return jnp.where(i < 6, i + 3, jnp.where(i < 9, i - 6, i))

        def part(i, start=0, size=U):
            return DG.at[0, ds(phys(i) * U + start, size)]

        H, Q4, E8 = PU // 2, PU // 4, PU // 8
        h, h2, h4 = QU // 2, QU // 4, QU // 8
        pq = lambda a, b: ((2 * a + b) * Q4, Q4)
        pch = lambda k: ((2 * f + s) * Q4 + k * E8, E8)
        tch = lambda k: ds(k * E8, E8)
        qn = lambda k: (PU + k * h, h)
        qhalf = lambda k, a: (PU + k * h + a * h2, h2)
        qquart = lambda k, a, b: (PU + k * h + (2 * a + b) * h4, h4)
        k8 = lambda i: lax.rem(i, SLOTS)
        rd = lambda i: RD.at[lax.rem(i, 4)]
        same = lambda k, at, dev: (lambda i: cp(k, i, part(i, *at), part(i, *at), dev))
        C = dict(
            D=lambda i: cp("D", i, DG.at[1, ds(phys(i) * U, U)], rd(i), peer),
            P1=lambda i: cp("P1", i, part(i, (1 - f) * H, H), RP1.at[k8(i)], n1),
            P2=lambda i: cp("P2", i, part(i, *pq(f, 1 - s)), RP2.at[k8(i)], n2),
            PZ1=lambda i: cp("PZ1", i, part(i, *pq(f, s)), RZ1.at[k8(i)], zp),
            PZ2=lambda i: cp("PZ2", i, part(i, *pch(farc)), RZ2.at[k8(i)], far),
            PT1=lambda i: cp("PT1", i, TQ.at[k8(i), tch(near)], TQ.at[k8(i), tch(near)], far),
            PT2=lambda i: cp("PT2", i, TQ.at[k8(i), tch(near)], TQ.at[k8(i), tch(near)], zp),
            PT3=lambda i: cp("PT3", i, TQ.at[k8(i), tch(farc)], TQ.at[k8(i), tch(farc)], zp),
            G1=same("G1", pq(f, s), n2),
            G2=same("G2", (f * H, H), n1),
            Q1=lambda i: cp("Q1", i, part(i, PU, QU), RQ1.at[k8(i)], zp),
            Q2=lambda i: cp("Q2", i, part(i, *qn(farc)), RQ2.at[k8(i)], far),
            X1=lambda i: cp("X1", i, part(i, *qhalf(near, 1 - f)), RX1.at[k8(i)], n1),
            X2=lambda i: cp("X2", i, part(i, *qquart(near, f, 1 - s)), RX2.at[k8(i)], n2),
            X3=lambda i: cp("X3", i, part(i, *qquart(near, f, s)), TX.at[k8(i)], n2),
            X4=same("X4", qhalf(near, f), n1),
            QT1=same("QT1", qn(near), far),
            QT2=same("QT2", qn(near), zp),
            QT3=same("QT3", qn(farc), zp),
        )

        def final(i, start):
            to = out.at[c, ds(phys(i) * U - jnp.where(i < N, 0, N * U), U)]
            there, here = cp("F", i, part(i), to, peer), pltpu.make_async_copy(part(i), to, ss.at[order["F"], i])
            both_ways(jnp.where(i < N, 1, 0) == c, here.start if start else here.wait, there.start if start else there.wait_send)

        def on_inner(fn):
            pl.when(inner)(fn)

        def on_outer(fn):
            pl.when(outer)(fn)

        def s0(i):
            C["D"](i).start()

        def s1(i):
            C["D"](i).wait()
            add(part(i), part(i), rd(i))
            C["P1"](i).start()
            on_outer(lambda: C["Q1"](i).start())

        def s2(i):
            @on_inner
            def _():
                C["Q1"](i).wait_recv()
                add(part(i, *qn(farc)), part(i, *qn(farc)), RQ1.at[k8(i), ds(farc * h, h)])
                C["Q2"](i).start()

            C["P1"](i).wait()
            add(part(i, f * H, H), part(i, f * H, H), RP1.at[k8(i)])
            C["P2"](i).start()
            on_outer(lambda: C["Q1"](i).wait_send())

        def s3(i):
            C["P2"](i).wait()
            add(part(i, *pq(f, s)), part(i, *pq(f, s)), RP2.at[k8(i)])
            on_outer(lambda: C["PZ1"](i).start())

            @on_inner
            def _():
                C["Q2"](i).wait()
                add(part(i, *qn(near)), part(i, *qn(near)), RQ1.at[k8(i), ds(near * h, h)], RQ2.at[k8(i)])
                C["X1"](i).start()

        def s4(i):
            @on_inner
            def _():
                C["PZ1"](i).wait_recv()
                add(part(i, *pch(farc)), part(i, *pch(farc)), RZ1.at[k8(i), tch(farc)])
                C["PZ2"](i).start()
                C["X1"](i).wait()
                add(part(i, *qhalf(near, f)), part(i, *qhalf(near, f)), RX1.at[k8(i)])
                C["X2"](i).start()

            on_outer(lambda: C["PZ1"](i).wait_send())

        def s5(i):
            @on_inner
            def _():
                C["PZ2"](i).wait()
                add(TQ.at[k8(i), tch(near)], part(i, *pch(near)), RZ1.at[k8(i), tch(near)], RZ2.at[k8(i)])
                C["PT1"](i).start()
                C["PT2"](i).start()
                C["X2"](i).wait()
                add(part(i, *qquart(near, f, s)), part(i, *qquart(near, f, s)), RX2.at[k8(i)])
                C["X3"](i).start()

        def s6(i):
            @on_inner
            def _():
                C["PT1"](i).wait()
                C["PT3"](i).start()
                C["X3"](i).wait()
                part(i, *qquart(near, f, 1 - s))[...] = TX[k8(i)]
                C["X4"](i).start()

        def s7(i):
            @on_outer
            def _():
                C["PT2"](i).wait_recv()
                C["PT3"](i).wait_recv()

            @on_inner
            def _():
                C["PT2"](i).wait_send()
                C["PT3"](i).wait_send()

            part(i, *pq(f, s))[...] = TQ[k8(i)]
            C["G1"](i).start()

            @on_inner
            def _():
                C["X4"](i).wait()
                C["QT1"](i).start()
                C["QT2"](i).start()

        def s8(i):
            C["G1"](i).wait()
            C["G2"](i).start()

            @on_inner
            def _():
                C["QT1"](i).wait()
                C["QT3"](i).start()

        def s9(i):
            C["G2"](i).wait()

            @on_outer
            def _():
                C["QT2"](i).wait_recv()
                C["QT3"](i).wait_recv()

            @on_inner
            def _():
                C["QT2"](i).wait_send()
                C["QT3"](i).wait_send()

            final(i, True)

        def s10(i):
            final(i, False)

        stages = (s0, s1, s2, s3, s4, s5, s6, s7, s8, s9, s10)

        def step(t):
            for k, stage in enumerate(stages):
                i = t - k
                pl.when(jnp.logical_and(i >= 0, i < 2 * N))(functools.partial(stage, i))

        def finish():
            def one(j, _):
                i = jnp.where(c == 1, j, j + N)
                cp("F", i, part(i), out.at[c, ds(0, U)], peer).wait_recv()
                return 0

            lax.fori_loop(0, N, one, 0)

        def barrier():
            b = pltpu.get_barrier_semaphore()
            for d in plane(c, z, q) + [zp]:
                pl.semaphore_signal(b, inc=1, device_id=d, device_id_type=MESH)

            @on_inner
            def _():
                pl.semaphore_signal(b, inc=1, device_id=far, device_id_type=MESH)
                pl.semaphore_wait(b, 9)

            on_outer(lambda: pl.semaphore_wait(b, 8))

        self.step, self.finish, self.barrier, self.iters = step, finish, barrier, 2 * N + len(stages) - 1


class NoRing:
    def __init__(self, N, U):
        self.N, self.U, self.live, self.out_units = N, U, False, 2 * N * U

    def scratch(self):
        return []

    def bind(self, *refs):
        pass

    def barrier(self):
        greet(plane(lax.axis_index("section"), lax.axis_index("dp"), lax.axis_index("seq")))

    def step(self, t):
        pass


def plane(c, z, q):
    out = []
    for i in range(1, 8):
        n = lax.rem(c * 4 + q + i, 8)
        out.append((lax.div(n, 4), z, lax.rem(n, 4)))
    return out


def greet(ids):
    barrier = pltpu.get_barrier_semaphore()
    for d in ids:
        pl.semaphore_signal(barrier, inc=1, device_id=d, device_id_type=MESH)
    pl.semaphore_wait(barrier, len(ids))


def remote(src, dst, ss, rs, dev):
    return pltpu.make_async_remote_copy(src_ref=src, dst_ref=dst, send_sem=ss, recv_sem=rs, device_id=dev, device_id_type=MESH)


def both_ways(cond, here, there):
    @pl.when(cond)
    def _():
        here()

    @pl.when(jnp.logical_not(cond))
    def _():
        there()


class Spread:
    def __init__(self, c, z, q, ss, rs, ls):
        self.c, self.z, self.q, self.ss, self.rs, self.ls = c, z, q, ss, rs, ls

    def go(self, a, src, dst, m, start):
        c, z, q = self.c, self.z, self.q
        for h in range(2):
            s, d, j = src.at[m, :, h], dst(q), 2 * m + h
            far = remote(s, d, self.ss.at[a, j], self.rs.at[a, q], (jnp.int32(h), z, 2 * c + m))
            near = pltpu.make_async_copy(s, d, self.ls.at[a])
            both_ways(jnp.logical_and(h == c, 2 * c + m == q), near.start if start else near.wait, far.start if start else far.wait_send)

    def arrive(self, a, src, dst):
        c, z, q = self.c, self.z, self.q
        fc = lax.div(q, 2)
        for p in range(4):
            @pl.when(jnp.logical_not(jnp.logical_and(c == fc, p == q)))
            def _():
                remote(src.at[0, :, 0], dst(p), self.ss.at[a, 0], self.rs.at[a, p], (fc, z, jnp.int32(p))).wait_recv()

    def back(self, a, src, dst, p, start):
        c, z, q = self.c, self.z, self.q
        tc, slot = lax.div(q, 2), lax.rem(q, 2)
        s, d = src.at[pl.ds(2 * p, 2)], dst.at[slot, :, c]
        far = remote(s, d, self.ss.at[a, p], self.rs.at[a, 2 * slot + c], (tc, z, jnp.int32(p)))
        near = pltpu.make_async_copy(s, d, self.ls.at[a])
        both_ways(jnp.logical_and(tc == c, p == q), near.start if start else near.wait, far.start if start else far.wait_send)

    def back_arrive(self, a, src, dst, m):
        c, z, q = self.c, self.z, self.q
        for h in range(2):
            @pl.when(jnp.logical_not(jnp.logical_and(h == c, 2 * c + m == q)))
            def _():
                remote(src.at[pl.ds(0, 2)], dst.at[m, :, h], self.ss.at[a, 0], self.rs.at[a, 2 * m + h], (jnp.int32(h), z, 2 * c + m)).wait_recv()


def edges(ref, m, seg, ss, rs, z, q, c):
    before = remote(ref.at[m, pl.ds(HALO, HALO)], ref.at[m, pl.ds(HALO + seg, HALO)], ss.at[0, m], rs.at[0, m], (c, z, q - 1))
    after = remote(ref.at[m, pl.ds(seg, HALO)], ref.at[m, pl.ds(0, HALO)], ss.at[1, m], rs.at[1, m], (c, z, q + 1))
    return ((q > 0, q < 3, before), (q < 3, q > 0, after))


def whole(lengths, inputs, cot_all, params, w_in, conv_w, w_out, dec, code, act, igr, total, cnt,
          WI, WC, WO, PR, xe, cot, out1, first1, hidden1, sec1, mixed1, third1, first2, hidden2, sec2, dth2, sp, dthr, thirdr, dpad,
          third2, dsec2, og, ge, hd, me, hold, dgbi, dgbm, counts, DG,
          ws, wr, wl, xs, xr, xl, ss, rs, ls, gs, gr, ps, pr, pw, *ring_refs, ring):
    c, z, q = lax.axis_index("section"), lax.axis_index("dp"), lax.axis_index("seq")
    peer = (1 - c, z, q)
    seg, D = cot.shape[1:]
    H = mixed1.shape[2]
    nd, nh = D // 128, H // 128
    rows = seg + 2 * HALO
    base = q * seg
    he, dme = hd.at[pl.ds(0, rows)], hd.at[pl.ds(rows, rows)]
    ring.bind(DG, total, *ring_refs)
    own = [pltpu.make_async_copy(inputs.at[2 * c + m, 0], xe.at[m, pl.ds(HALO, seg)], xl.at[m]) for m in range(2)]
    own += [pltpu.make_async_copy(cot_all.at[2 * c + m, 0], cot.at[m], xl.at[2 + m]) for m in range(2)]
    mats = [(params, PR.at[c]), (w_in.at[0], WI.at[c])] + [(conv_w.at[0, k], WC.at[c, k]) for k in range(5)] + [(w_out.at[0], WO.at[c])]
    loads = [pltpu.make_async_copy(s, d, wl.at[i]) for i, (s, d) in enumerate(mats)]
    for cp in own[:2] + loads + own[2:]:
        cp.start()
    ring.barrier()
    sends = [remote(s, d, ws.at[i], wr.at[i], peer) for i, (s, d) in enumerate(mats)]
    halos = []
    for m in range(2):
        x = inputs.at[2 * c + m, 0]
        halos.append((q > 0, q < 3, remote(x.at[pl.ds(0, HALO)], xe.at[m, pl.ds(HALO + seg, HALO)], xs.at[0, m], xr.at[0, m], (c, z, q - 1))))
        halos.append((q < 3, q > 0, remote(x.at[pl.ds(seg - HALO, HALO)], xe.at[m, pl.ds(0, HALO)], xs.at[1, m], xr.at[1, m], (c, z, q + 1))))
    for cond, _, cp in halos:
        pl.when(cond)(cp.start)
    for cp in sends:
        cp.start()

    @pl.when(q == 0)
    def _():
        xe[:, pl.ds(0, HALO)] = jnp.zeros((2, HALO, D), BF)
        ge[:, pl.ds(0, HALO)] = jnp.zeros((2, HALO, D), BF)

    @pl.when(q == 3)
    def _():
        xe[:, pl.ds(HALO + seg, HALO)] = jnp.zeros((2, HALO, D), BF)
        ge[:, pl.ds(HALO + seg, HALO)] = jnp.zeros((2, HALO, D), BF)

    def have(i):
        loads[i].wait()
        sends[i].wait_recv()

    for ref in (dgbi, dgbm, counts):
        ref[...] = jnp.zeros_like(ref)
    zero = jnp.zeros((2, 64, H), BF)
    for ref in (sp, dpad):
        ref[pl.ds(0, 2)] = zero
        ref[pl.ds(10, 2)] = zero
    sec1[:, pl.ds(0, 8)] = jnp.zeros((2, 8, H), F32)
    sec1[:, pl.ds(rows + 8, 8)] = jnp.zeros((2, 8, H), F32)
    spread = Spread(c, z, q, ss, rs, ls)
    sp_at = lambda p: sp.at[pl.ds(2 + 2 * p, 2)]
    dthr_at = lambda p: dthr.at[pl.ds(2 * p, 2)]
    gi, bi = lambda l: row(PR.at[l], 0), lambda l: row(PR.at[l], 1)
    gm = lambda l, k: (lambda j: PR[l, pl.ds(2, 1), cols(k * nh + j)])
    bm = lambda l, k: (lambda j: PR[l, pl.ds(3, 1), cols(k * nh + j)])

    have(0)
    for m in range(2):
        own[m].wait()
    for _, cond, cp in halos:
        pl.when(cond)(cp.wait_recv)

    def first_norm(m, _):
        def a(i, size):
            r = pl.ds(i, size)
            norm_gelu(view(xe, m, r), nd, gi(0), bi(0), put(first1, m, r))

        chunks(rows, a)
        return 0

    lax.fori_loop(0, 2, first_norm, 0)
    have(1)

    def forward(m, _):
        length = lengths[2 * c + m]
        he[...] = dot(first1[m], WI[0])
        hidden1[m] = he[pl.ds(HALO, seg)]

        def b(i, size):
            pos = positions(base - HALO, i, size)
            keep = jnp.logical_and(pos >= 0, pos < length)

            def store(j, v):
                sec1[m, pl.ds(i + 8, size), cols(j)] = jnp.where(keep, v, 0.0).astype(BF).astype(F32)

            norm_gelu(view(he, pl.ds(i, size)), nh, gm(0, 0), bm(0, 0), store)

        chunks(rows, b)

        @pl.when(m == 0)
        def _():
            for k in range(5):
                have(2 + k)

        acc = None
        for k in range(5):
            term = dot(sec1[m, pl.ds(8 + DIL * (k - 2), rows)].astype(BF), WC[0, k])
            acc = term if acc is None else acc + term
        mixed1[m] = acc

        def e(i, size):
            norm_gelu(view(mixed1, m, pl.ds(i + HALO, size)), nh, gm(0, 1), bm(0, 1), put(third1, m, pl.ds(i, size)))

        chunks(seg, e)

        @pl.when(m == 0)
        def _():
            have(7)

        he[pl.ds(0, seg)] = dot(third1[m], WO[0, :, :H])
        me[...] = dot(third1[m], WO[0, :, H:])

        def d(i, size):
            r = pl.ds(i, size)
            for j in range(nd):
                br = he[r, cols(j)] if j < nh else me[r, cols(j - nh)]
                out1[m, r, cols(j)] = (xe[m, pl.ds(i + HALO, size), cols(j)].astype(F32) + br).astype(BF)
            norm_gelu(view(out1, m, r), nd, gi(1), bi(1), put(first2, m, r))

        chunks(seg, d)
        hidden2[m] = dot(first2[m], WI[1])

        def f(jj, _):
            i = pl.multiple_of(jj * 64, 64)
            pos = positions(base, i, 64)

            def store(j, v):
                sec2[m, lax.div(jj, 2), lax.rem(jj, 2), :, cols(j)] = jnp.where(pos < length, v, 0.0).astype(BF)

            norm_gelu(view(hidden2, m, pl.ds(i, 64)), nh, gm(1, 0), bm(1, 0), store)
            return 0

        lax.fori_loop(0, seg // 64, f, 0)
        spread.go(0, sec2, sp_at, m, True)
        return 0

    lax.fori_loop(0, 2, forward, 0)
    for m in range(2):
        own[2 + m].wait()

    def third_grad(m, _):
        dth2[m] = dot_nt(cot[m], WO[1]).astype(BF).reshape(2, 2, 64, H)
        spread.go(1, dth2, dthr_at, m, True)
        return 0

    lax.fori_loop(0, 2, third_grad, 0)

    def place(i, src, dst, layer):
        to = dst.at[pl.ds(2 * c, 2)]
        here, there = pltpu.make_async_copy(src, to, pw.at[i]), remote(src, to, ps.at[i], pr.at[i // 2], peer)
        both_ways(c == layer, here.start, there.start)
        return lambda: both_ways(c == layer, here.wait, there.wait_send)

    placed = [place(0, out1, act, 0)]
    for m in range(2):
        spread.go(0, sec2, sp_at, m, False)
    spread.arrive(0, sec2, sp_at)

    def conv(r, _):
        acc = None
        for k in range(5):
            term = dot(sp[pl.ds(4 * r + k, 4)].reshape(256, H), WC[1, k])
            acc = term if acc is None else acc + term
        hd[pl.ds(256 * r, 256)] = acc
        return 0

    lax.fori_loop(0, 2, conv, 0)
    for m in range(2):
        spread.go(1, dth2, dthr_at, m, False)
    spread.arrive(1, dth2, dthr_at)

    def mid(i, _):
        every = pl.ds(0, 64)
        norm_gelu_both(view(hd, pl.ds(pl.multiple_of(64 * i, 64), 64)), view(dthr, i, every), nh, gm(1, 1), bm(1, 1), dgbm.at[2], dgbm.at[3], hold,
                       put(thirdr, i, every), put(dpad, i + 2, every))
        return 0

    lax.fori_loop(0, 8, mid, 0)
    for p in range(4):
        spread.back(2, thirdr, third2, p, True)
    dm2 = dpad[pl.ds(2, 8)].reshape(512, H)

    def conv_grads(k, _):
        put_grad(DG, c, CONV0 + k * 100, dot_tn(sp[pl.ds(k, 8)].reshape(512, H), dm2))
        return 0

    lax.fori_loop(0, 5, conv_grads, 0)
    ring.step(0)

    def conv_back(r, _):
        acc = None
        for k in range(5):
            term = dot_nt(dpad[pl.ds(4 * r + 4 - k, 4)].reshape(256, H), WC[1, k])
            acc = term if acc is None else acc + term
        dthr[pl.ds(4 * r, 4)] = acc.astype(BF).reshape(4, 64, H)
        return 0

    lax.fori_loop(0, 2, conv_back, 0)
    for p in range(4):
        spread.back(3, dthr, dsec2, p, True)
    ring.step(1)
    for p in range(4):
        spread.back(2, thirdr, third2, p, False)
    for m in range(2):
        spread.back_arrive(2, thirdr, third2, m)
    labels = lax.broadcasted_iota(jnp.int32, (1, 128), 1)

    def two_out(m, _):
        t = third2[m].reshape(seg, H)
        he[pl.ds(0, seg)] = dot(t, WO[1, :, :H])
        me[...] = dot(t, WO[1, :, H:])

        def a(i, size):
            r = pl.ds(i, size)
            for j in range(nd):
                br = he[r, cols(j)] if j < nh else me[r, cols(j - nh)]
                og[m, r, cols(j)] = (out1[m, r, cols(j)].astype(F32) + br).astype(BF)

        chunks(seg, a)
        logits = jnp.where(labels < 30, dot(og[m], dec[...]), -1e30)
        ex = jnp.exp(logits - jnp.max(logits, axis=-1, keepdims=True))
        probs = ex / jnp.sum(ex, axis=-1, keepdims=True)
        kept = positions(base, 0, seg) < lengths[2 * c + m]
        counts[...] += fold(jnp.where(jnp.logical_and(code[2 * c + m] == labels, kept), probs, 0.0))
        return 0

    lax.fori_loop(0, 2, two_out, 0)
    placed.append(place(1, og, act, 1))
    ring.step(2)
    for p in range(4):
        spread.back(3, dthr, dsec2, p, False)
    for m in range(2):
        spread.back_arrive(3, dthr, dsec2, m)
    dh = lambda m: dpad.at[pl.ds(4 * m, 4)]

    def two(m, _):
        def b(i, _):
            pos = positions(base, i * 64, 64)
            u, h = lax.div(i, 2), lax.rem(i, 2)
            ds = lambda j: jnp.where(pos < lengths[2 * c + m], dsec2[m, u, h, :, cols(j)].astype(F32), 0.0)
            norm_gelu_back(view(hidden2, m, pl.ds(pl.multiple_of(i * 64, 64), 64)), ds, nh, gm(1, 0), bm(1, 0), dgbm.at[0], dgbm.at[1], hold,
                           put(dpad, 4 * m + i, pl.ds(0, 64)))
            return 0

        lax.fori_loop(0, seg // 64, b, 0)
        dhm = dh(m)[...].reshape(seg, H)
        he[pl.ds(0, seg)] = dot_nt(dhm, WI[1, :H])
        me[...] = dot_nt(dhm, WI[1, H:])

        def e(i, size):
            r = pl.ds(i, size)
            df = lambda j: he[r, cols(j)] if j < nh else me[r, cols(j - nh)]

            def store(j, v):
                ge[m, pl.ds(i + HALO, size), cols(j)] = (cot[m, r, cols(j)].astype(F32) + v).astype(BF)

            norm_gelu_back(view(out1, m, r), df, nd, gi(1), bi(1), dgbi.at[0], dgbi.at[1], hold, store)

        chunks(seg, e)
        for cond, _, cp in edges(ge, m, seg, gs, gr, z, q, c):
            pl.when(cond)(cp.start)
        ring.step(3 + m)
        return 0

    lax.fori_loop(0, 2, two, 0)
    placed.append(place(2, ge.at[:, pl.ds(HALO, seg)], igr, 1))
    flat = lambda v: v.reshape(2 * seg, v.shape[-1])
    t2 = flat(third2[...])
    for j in range(2):
        put_grad(DG, c, OUT0, dot_tn(t2, flat(cot[:, :, pl.ds(j * H, H)])), nh * j)
    ring.step(5)
    put_grad(DG, c, IN0, dot_tn(flat(first2[...]), dpad[pl.ds(0, 8)].reshape(2 * seg, H)))

    def extra(first_unit, with_counts):
        flat_rows = [dgbi[k, :, cols(j)] for k in range(2) for j in range(nd)]
        flat_rows += [dgbm[k, :, cols(j)] for k in range(4) for j in range(nh)]
        small = [jnp.sum(v, axis=0, keepdims=True) for v in flat_rows]
        if with_counts:
            small.append(jnp.sum(counts[...], axis=0, keepdims=True))
        size = UNITS - EXTRA0
        small.append(jnp.zeros((48 - len(small), 128), F32))
        block = jnp.concatenate(small, axis=0).astype(BF).reshape(3, 16, 128)
        for h in range(2):
            DG[h, pl.ds(first_unit, 3)] = block
            DG[h, pl.ds(first_unit + 3, size - 3)] = jnp.zeros((size - 3, 16, 128), BF)

    extra(EXTRA0, True)
    ring.step(6)
    for ref in (dgbi, dgbm):
        ref[...] = jnp.zeros_like(ref)
    for m in range(2):
        for s_cond, r_cond, cp in edges(ge, m, seg, gs, gr, z, q, c):
            pl.when(s_cond)(cp.wait_send)
            pl.when(r_cond)(cp.wait_recv)
    for done in placed[:2]:
        done()
    dm = lambda m: dsec2.at[m]

    def one(m, _):
        he[...] = dot_nt(ge[m], WO[0])

        def a(i, _):
            r = pl.ds(pl.multiple_of(i * 64 + HALO, 16), 64)
            u, h = lax.div(i, 2), lax.rem(i, 2)

            def store(j, v):
                v = v.astype(BF)
                dme[r, cols(j)] = v.astype(F32)
                dsec2[m, u, h, :, cols(j)] = v

            norm_gelu_back(view(mixed1, m, r), view(he, r), nh, gm(0, 1), bm(0, 1), dgbm.at[2], dgbm.at[3], hold, store)
            return 0

        lax.fori_loop(0, seg // 64, a, 0)
        for edge in (0, rows - HALO):
            r = pl.ds(edge, HALO)
            pos = positions(base - HALO, edge, HALO)
            within = jnp.logical_and(pos >= 0, pos < 4 * seg)

            def store(j, v):
                dme[r, cols(j)] = jnp.where(within, v, 0.0).astype(BF).astype(F32)

            norm_gelu_back(view(mixed1, m, r), view(he, r), nh, gm(0, 1), bm(0, 1), None, None, hold.at[:, pl.ds(0, HALO)], store)
        ring.step(7 + 3 * m)
        acc = None
        for k in range(5):
            term = dot_nt(dme[pl.ds(HALO - DIL * (k - 2), seg)].astype(BF), WC[0, k])
            acc = term if acc is None else acc + term
        he[pl.ds(0, seg)] = acc

        def b(i, _):
            r = pl.ds(pl.multiple_of(i * 64, 64), 64)
            pos = positions(base, i * 64, 64)
            ds = lambda j: jnp.where(pos < lengths[2 * c + m], he[r, cols(j)], 0.0)
            norm_gelu_back(view(hidden1, m, r), ds, nh, gm(0, 0), bm(0, 0), dgbm.at[0], dgbm.at[1], hold, put(dpad, 4 * m + i, pl.ds(0, 64)))
            return 0

        lax.fori_loop(0, seg // 64, b, 0)
        ring.step(8 + 3 * m)
        dhm = dh(m)[...].reshape(seg, H)
        he[pl.ds(0, seg)] = dot_nt(dhm, WI[0, :H])
        me[...] = dot_nt(dhm, WI[0, H:])

        def e(i, size):
            r, x = pl.ds(i, size), pl.ds(i + HALO, size)
            df = lambda j: he[r, cols(j)] if j < nh else me[r, cols(j - nh)]

            def store(j, v):
                og[m, r, cols(j)] = (ge[m, x, cols(j)].astype(F32) + v).astype(BF)

            norm_gelu_back(view(xe, m, x), df, nd, gi(0), bi(0), dgbi.at[0], dgbi.at[1], hold, store)

        chunks(seg, e)
        ring.step(9 + 3 * m)
        return 0

    lax.fori_loop(0, 2, one, 0)
    placed.append(place(3, og, igr, 0))
    low = UNITS
    t1 = flat(third1[...])
    for j in range(2):
        put_grad(DG, c, low + OUT0, dot_tn(t1, flat(ge[:, pl.ds(HALO, seg), pl.ds(j * H, H)])), nh * j)
    ring.step(13)
    d1 = flat(dsec2[...])
    for k in range(5):
        for m in range(2):
            third2[m] = sec1[m, pl.ds(8 + HALO + DIL * (k - 2), seg)].astype(BF).reshape(2, 2, 64, H)
        put_grad(DG, c, low + CONV0 + k * 100, dot_tn(flat(third2[...]), d1))
        if k in (1, 3):
            ring.step(14 + k // 2)
    put_grad(DG, c, low + IN0, dot_tn(flat(first1[:, pl.ds(HALO, seg)]), dpad[pl.ds(0, 8)].reshape(2 * seg, H)))
    extra(low + EXTRA0, False)

    def rest(t, _):
        ring.step(t)
        return 0

    if ring.live:
        lax.fori_loop(16, ring.iters, rest, 0)
        ring.finish()
        cnt[...] = DG[0, pl.ds(EXTRA0, 3)]
    else:
        everything = pltpu.make_async_copy(DG, total, pw.at[0])
        everything.start()
        everything.wait()
        cnt[...] = jnp.zeros_like(cnt)
    for done in placed[2:]:
        done()
    for i, dst in ((0, act), (1, igr)):
        remote(og, dst.at[pl.ds(2 * (1 - c), 2)], ps.at[0], pr.at[i], peer).wait_recv()
    for cp in sends:
        cp.wait_send()
    for cond, _, cp in halos:
        pl.when(cond)(cp.wait_send)


def run(ring, lengths, inputs, cot, params, w_in, conv_w, w_out, dec, code):
    seg, D, H = inputs.shape[2], inputs.shape[3], w_in.shape[2]
    rows = seg + 2 * HALO
    any_, vm, sm = (pl.BlockSpec(memory_space=s) for s in (pl.ANY, pltpu.VMEM, pltpu.SMEM))
    sh = jax.ShapeDtypeStruct
    dma = lambda *s: pltpu.SemaphoreType.DMA(s)
    part = (2, 2, 2, 64, H)
    scratch = [((2, D, H), BF), ((2, 5, H, H), BF), ((2, H, D), BF), ((2, 8, D), F32), ((2, rows, D), BF), ((2, seg, D), BF),
               ((2, seg, D), BF), ((2, rows, D), BF), ((2, seg, H), F32), ((2, rows + 16, H), F32), ((2, rows, H), F32), ((2, seg, H), BF),
               ((2, seg, D), BF), ((2, seg, H), F32), (part, BF), (part, BF), ((12, 64, H), BF), ((8, 64, H), BF), ((8, 64, H), BF),
               ((12, 64, H), BF), (part, BF), (part, BF), ((2, seg, D), BF), ((2, rows, D), BF), ((2 * rows, H), F32), ((seg, H), F32),
               ((2, 64, D), F32), ((2, 8, D), F32), ((4, 8, H), F32), ((8, 128), F32), ((2, 2 * UNITS, 16, 128), BF)]
    return pl.pallas_call(
        functools.partial(whole, ring=ring),
        out_shape=[sh((4, seg, D), BF), sh((4, seg, D), BF), sh((2, ring.out_units, 16, 128), BF), sh((3, 16, 128), BF)],
        in_specs=[sm] + [any_] * 6 + [vm, vm],
        out_specs=[any_, any_, any_, vm],
        scratch_shapes=[pltpu.VMEM(s, d) for s, d in scratch]
        + [dma(8), dma(8), dma(8), dma(2, 2), dma(2, 2), dma(4), dma(4, 4), dma(4, 4), dma(4), dma(2, 2), dma(2, 2), dma(4), dma(2), dma(4)]
        + ring.scratch(),
        compiler_params=pltpu.CompilerParams(collective_id=1, has_side_effects=True, vmem_limit_bytes=63 * 2**20 + 2**19),
    )(lengths, inputs, cot, params, w_in, conv_w, w_out, dec, code)


def unpack_kernel(conv, w_out, w_in, extra, cnt, s_conv, s_out, s_in, gi, bi, gm, bm, counts):
    H = s_conv.shape[-1]
    for j in range(5):
        for h in range(2):
            s_conv[0, 0, pl.ds(h * 320, 320), cols(j)] = conv[h, pl.ds(j * 20, 20)].reshape(320, 128).astype(F32)
    for j in range(2):
        for h in range(2):
            s_out[0, pl.ds(h * 320, 320), cols(j)] = w_out[h, pl.ds(j * 20, 20)].reshape(320, 128).astype(F32)
    for h in range(2):
        s_in[0, pl.ds(h * 640, 640)] = w_in[h].reshape(640, 128).astype(F32)

    @pl.when(pl.program_id(0) == 0)
    def _():
        small = extra[0, pl.ds(0, 3)].reshape(48, 128).astype(F32)
        for j in range(10):
            gi[:, cols(j)] = small[j : j + 1]
            bi[:, cols(j)] = small[10 + j : 11 + j]
        for k in range(2):
            for j in range(5):
                gm[0, pl.ds(k, 1), cols(j)] = small[20 + 10 * k + j : 21 + 10 * k + j]
                bm[0, pl.ds(k, 1), cols(j)] = small[25 + 10 * k + j : 26 + 10 * k + j]
        counts[...] = cnt[...].reshape(48, 128)[40:41].astype(F32)


def unpack(total, cnt, D, H):
    def spec(units, first, moves=1):
        return pl.BlockSpec(tuple(pl.Element(n) for n in (2, units, 16, 128)), lambda k: (0, first + units * k * moves, 0, 0))

    def full(*s):
        return pl.BlockSpec(s, lambda k: (0,) * len(s))

    sh = lambda *s: jax.ShapeDtypeStruct(s, F32)
    return pl.pallas_call(
        unpack_kernel,
        grid=(5,),
        out_shape=[sh(1, 5, H, H), sh(1, H, D), sh(1, D, H), sh(1, D), sh(1, D), sh(1, 2, H), sh(1, 2, H), sh(1, 128)],
        in_specs=[spec(100, CONV0), spec(40, OUT0), spec(40, IN0), spec(36, EXTRA0, 0), full(3, 16, 128)],
        out_specs=[pl.BlockSpec((1, 1, H, H), lambda k: (0, k, 0, 0)), pl.BlockSpec((1, H, 256), lambda k: (0, 0, k)),
                   pl.BlockSpec((1, D, 128), lambda k: (0, 0, k)), full(1, D), full(1, D), full(1, 2, H), full(1, 2, H), full(1, 128)],
        compiler_params=pltpu.CompilerParams(vmem_limit_bytes=60 * 2**20),
    )(total, total, total, total, cnt)


def body(inputs, lengths, mlm_mask, true_types, gain_in, bias_in, gain_mid, bias_mid, w_in, conv_w, w_out, decoder, cotangent, fast):
    D, H = inputs.shape[3], w_in.shape[2]
    params = jnp.concatenate([gain_in, bias_in, gain_mid.reshape(1, D), bias_mid.reshape(1, D), jnp.zeros((4, D), BF)]).astype(F32)
    dec = jnp.pad(decoder, ((0, 0), (0, 128 - decoder.shape[1])))
    code = jnp.where(mlm_mask[:, 0] == 1, true_types[:, 0], -1)[..., None]
    ring = Ring(PIECES, PLANE_UNITS, Z_UNITS) if fast else NoRing(PIECES, PLANE_UNITS + Z_UNITS)
    act, igr, total, cnt = run(ring, lengths[:, 0], inputs, cotangent, params, w_in, conv_w, w_out, dec, code)
    if not fast:
        c = lax.axis_index("section")
        halves = jnp.where(c == 0, total, total[::-1])
        g_two, g_one = halves[:, :UNITS], halves[:, UNITS:]
        own, other = jnp.where(c == 0, g_one, g_two), jnp.where(c == 0, g_two, g_one)
        got = lax.ppermute(other, "section", [(0, 1), (1, 0)])
        total = lax.psum(own.astype(F32) + got.astype(F32), ("dp", "seq")).astype(BF)
        cnt = lax.psum(g_two[0, EXTRA0 : EXTRA0 + 3].astype(F32), ("section", "dp", "seq")).astype(BF)
    s_conv, s_out, s_in, s_gi, s_bi, s_gm, s_bm, s_cnt = unpack(total, cnt, D, H)
    return (act[None, :, None], igr[None, :, None], s_gi, s_bi, s_gm, s_bm, s_in, s_conv, s_out, s_cnt[0, : decoder.shape[1]])


def solution(mesh):
    fast = mesh.shape["dp"] == 4 and mesh.shape["seq"] == 4
    return jax.shard_map(
        functools.partial(body, fast=fast),
        mesh=mesh,
        in_specs=(P(None, "dp", "seq", None), P(None, "dp"), P(None, "dp", "seq"), P(None, "dp", "seq"), P("section", None),
                  P("section", None), P("section", None, None), P("section", None, None), P("section", None, None),
                  P("section", None, None, None), P("section", None, None), P(), P(None, "dp", "seq", None)),
        out_specs=(P("section", None, "dp", "seq", None), P("section", None, "dp", "seq", None), P("section", None), P("section", None),
                   P("section", None, None), P("section", None, None), P("section", None, None), P("section", None, None, None),
                   P("section", None, None), P()),
        check_vma=False,
    )
```

time: 263 us -> 233 us (0.89)
  Pallas kernels: 248 us -> 220 us
    pallas_call x2 -> x1, Pallas kernels: 239 us -> 210 us  [run(): pl.pallas_call(functools.partial(whole, ring=ring), out_shape=[sh((4, seg...]
where the time goes in v4:
time: 233 us; the launch traced here: 232 us
  Pallas kernels  220 us (94%)
  local copies, waits for them, and re-layouts  10.4 us (4%)
    pallas_call x1, Pallas kernels, run(): pl.pallas_call(functools.partial(whole, ring=ring), out_shape=[sh((4, seg...  210 us
    pallas_call x1, Pallas kernels, unpack(): pl.pallas_call(unpack_kernel, grid=(5,), out_shape=[sh(1, 5, H, H), sh(1,...  9.3 us
    unnamed x9, local copies, waits for them, and re-layouts  6.68 us

profile of v4, /device:TPU:0, one launch (start us, length us, event | category | flops | bytes accessed | tf_op | source)
XLA Modules:
  0.0 232.1 jit_solution(2344442955686933875)
XLA Ops:
  0.6 0.7 fusion
  1.4 0.7 copy.32
  2.1 0.7 copy.33
  2.8 0.8 concatenate.3
  3.5 0.6 convert_element_type.5.params
  4.1 1.1 copy.28
  5.2 0.8 pad.4.dec
  6.0 1.0 select_n.16.code
  7.0 210.4 %shard_map.204 = (bf16[4,256,1280]{2,1,0:T(8,128)(2,1)}, bf16[4,256,1280]{2,1,0:T(8,128)(2,1)}, bf16[2,936,16,128]{3,2,1,0:T(8,128)(2,1)}, bf16[3,16,128]{2,1,0:T(8,128)(2,1)}) custom-call(s32[4]{0:T(128)} %bitcast.19, bf16[4,1,256,1280]{3,2,1,0:T(8,128)(2,1)} %inputs.1, bf16[4,1,256,1280]{3,2,1,0:T(8,128)(2,1)} %cot_all.1, ...), custom_call_target="tpu_custom_call" | custom-call | tf_op jit(solution)/shard_map/pallas_call | solution.py:888
  217.4 0.0 copy-start.1
  217.5 9.3 %shard_map.205 = (f32[1,5,640,640]{3,2,1,0:T(8,128)}, f32[1,640,1280]{2,1,0:T(8,128)}, f32[1,1280,640]{2,1,0:T(8,128)}, f32[1,1280]{1,0:T(1,128)}, f32[1,1280]{1...) custom-call(bf16[2,936,16,128]{3,2,1,0:T(8,128)(2,1)} %get-tuple-element.24.conv.w_out.w_in.extra, ...), custom_call_target="tpu_custom_call" | custom-call | tf_op jit(solution)/shard_map/pallas_call | solution.py:932
  226.8 1.2 slice_bitcast_fusion
  227.9 0.0 copy-done.1
  227.9 0.0 copy-start
  227.9 1.5 copy.36
  229.4 1.2 copy-done
  230.6 1.5 copy.37
  (1 shorter events, 0.0 us)
Async XLA Ops:
  217.4 10.5 %copy-start.1 = (bf16[4,256,1280]{2,1,0:T(8,128)(2,1)S(1)}, bf16[4,256,1280]{2,1,0:T(8,128)(2,1)}, u32[]{:S(2)}) copy-start(bf16[4,256,1280]{2,1,0:T(8,128)(2,1)} %get-tuple-element.22) | copy-start | bytes 7864324
  227.9 2.7 %copy-start = (bf16[4,256,1280]{2,1,0:T(8,128)(2,1)S(1)}, bf16[4,256,1280]{2,1,0:T(8,128)(2,1)}, u32[]{:S(2)}) copy-start(bf16[4,256,1280]{2,1,0:T(8,128)(2,1)} %get-tuple-element.23) | copy-start | bytes 7864324

commit v5 on v4

--- a/solution.py
+++ b/solution.py
@@ -16,7 +16,7 @@
 DIL = 2
 HALO = 16
 OUT0, CONV0, IN0, EXTRA0, UNITS = 0, 200, 700, 900, 936
-PIECES, PLANE_UNITS, Z_UNITS, SLOTS = 13, 48, 24, 8
+PIECES, PLANE_UNITS, Z_UNITS, SLOTS = 9, 80, 24, 7
 
 
 def dot(a, b):
@@ -163,9 +163,9 @@
 
     def scratch(self):
         PU, QU, U = self.PU, self.QU, self.U
-        b = lambda u, n=SLOTS: pltpu.VMEM((n, u, 16, 128), BF)
+        b = lambda u, n=SLOTS - 1: pltpu.VMEM((n, u, 16, 128), BF)
         sems = pltpu.SemaphoreType.DMA((len(self.KINDS), 2 * self.N))
-        return [b(U, 4), b(PU // 2), b(PU // 4), b(PU // 4), b(PU // 8), b(QU), b(QU // 2), b(QU // 4), b(QU // 8), b(PU // 4), b(QU // 8),
+        return [b(U, 4), b(PU // 2), b(PU // 4), b(PU // 4, SLOTS), b(PU // 8), b(QU, SLOTS), b(QU // 2, SLOTS), b(QU // 4), b(QU // 8), b(PU // 4), b(QU // 8),
                 sems, sems]
 
     def bind(self, DG, out, RD, RP1, RP2, RZ1, RZ2, RQ1, RQ2, RX1, RX2, TQ, TX, ss, rs):
@@ -195,7 +195,7 @@
             dst[...] = acc.astype(BF)
 
         def phys(i):
-            return jnp.where(i < 6, i + 3, jnp.where(i < 9, i - 6, i))
+            return jnp.where(i < 4, i + 2, jnp.where(i < 6, i - 4, i))
 
         def part(i, start=0, size=U):
             return DG.at[0, ds(phys(i) * U + start, size)]
@@ -209,24 +209,25 @@
         qhalf = lambda k, a: (PU + k * h + a * h2, h2)
         qquart = lambda k, a, b: (PU + k * h + (2 * a + b) * h4, h4)
         k8 = lambda i: lax.rem(i, SLOTS)
+        k7 = lambda i: lax.rem(i, SLOTS - 1)
         rd = lambda i: RD.at[lax.rem(i, 4)]
         same = lambda k, at, dev: (lambda i: cp(k, i, part(i, *at), part(i, *at), dev))
         C = dict(
             D=lambda i: cp("D", i, DG.at[1, ds(phys(i) * U, U)], rd(i), peer),
-            P1=lambda i: cp("P1", i, part(i, (1 - f) * H, H), RP1.at[k8(i)], n1),
-            P2=lambda i: cp("P2", i, part(i, *pq(f, 1 - s)), RP2.at[k8(i)], n2),
+            P1=lambda i: cp("P1", i, part(i, (1 - f) * H, H), RP1.at[k7(i)], n1),
+            P2=lambda i: cp("P2", i, part(i, *pq(f, 1 - s)), RP2.at[k7(i)], n2),
             PZ1=lambda i: cp("PZ1", i, part(i, *pq(f, s)), RZ1.at[k8(i)], zp),
-            PZ2=lambda i: cp("PZ2", i, part(i, *pch(farc)), RZ2.at[k8(i)], far),
-            PT1=lambda i: cp("PT1", i, TQ.at[k8(i), tch(near)], TQ.at[k8(i), tch(near)], far),
-            PT2=lambda i: cp("PT2", i, TQ.at[k8(i), tch(near)], TQ.at[k8(i), tch(near)], zp),
-            PT3=lambda i: cp("PT3", i, TQ.at[k8(i), tch(farc)], TQ.at[k8(i), tch(farc)], zp),
+            PZ2=lambda i: cp("PZ2", i, part(i, *pch(farc)), RZ2.at[k7(i)], far),
+            PT1=lambda i: cp("PT1", i, TQ.at[k7(i), tch(near)], TQ.at[k7(i), tch(near)], far),
+            PT2=lambda i: cp("PT2", i, TQ.at[k7(i), tch(near)], TQ.at[k7(i), tch(near)], zp),
+            PT3=lambda i: cp("PT3", i, TQ.at[k7(i), tch(farc)], TQ.at[k7(i), tch(farc)], zp),
             G1=same("G1", pq(f, s), n2),
             G2=same("G2", (f * H, H), n1),
             Q1=lambda i: cp("Q1", i, part(i, PU, QU), RQ1.at[k8(i)], zp),
             Q2=lambda i: cp("Q2", i, part(i, *qn(farc)), RQ2.at[k8(i)], far),
-            X1=lambda i: cp("X1", i, part(i, *qhalf(near, 1 - f)), RX1.at[k8(i)], n1),
-            X2=lambda i: cp("X2", i, part(i, *qquart(near, f, 1 - s)), RX2.at[k8(i)], n2),
-            X3=lambda i: cp("X3", i, part(i, *qquart(near, f, s)), TX.at[k8(i)], n2),
+            X1=lambda i: cp("X1", i, part(i, *qhalf(near, 1 - f)), RX1.at[k7(i)], n1),
+            X2=lambda i: cp("X2", i, part(i, *qquart(near, f, 1 - s)), RX2.at[k7(i)], n2),
+            X3=lambda i: cp("X3", i, part(i, *qquart(near, f, s)), TX.at[k7(i)], n2),
             X4=same("X4", qhalf(near, f), n1),
             QT1=same("QT1", qn(near), far),
             QT2=same("QT2", qn(near), zp),
@@ -261,13 +262,13 @@
                 C["Q2"](i).start()
 
             C["P1"](i).wait()
-            add(part(i, f * H, H), part(i, f * H, H), RP1.at[k8(i)])
+            add(part(i, f * H, H), part(i, f * H, H), RP1.at[k7(i)])
             C["P2"](i).start()
             on_outer(lambda: C["Q1"](i).wait_send())
 
         def s3(i):
             C["P2"](i).wait()
-            add(part(i, *pq(f, s)), part(i, *pq(f, s)), RP2.at[k8(i)])
+            add(part(i, *pq(f, s)), part(i, *pq(f, s)), RP2.at[k7(i)])
             on_outer(lambda: C["PZ1"](i).start())
 
             @on_inner
@@ -283,7 +284,7 @@
                 add(part(i, *pch(farc)), part(i, *pch(farc)), RZ1.at[k8(i), tch(farc)])
                 C["PZ2"](i).start()
                 C["X1"](i).wait()
-                add(part(i, *qhalf(near, f)), part(i, *qhalf(near, f)), RX1.at[k8(i)])
+                add(part(i, *qhalf(near, f)), part(i, *qhalf(near, f)), RX1.at[k7(i)])
                 C["X2"](i).start()
 
             on_outer(lambda: C["PZ1"](i).wait_send())
@@ -292,11 +293,11 @@
             @on_inner
             def _():
                 C["PZ2"](i).wait()
-                add(TQ.at[k8(i), tch(near)], part(i, *pch(near)), RZ1.at[k8(i), tch(near)], RZ2.at[k8(i)])
+                add(TQ.at[k7(i), tch(near)], part(i, *pch(near)), RZ1.at[k8(i), tch(near)], RZ2.at[k7(i)])
                 C["PT1"](i).start()
                 C["PT2"](i).start()
                 C["X2"](i).wait()
-                add(part(i, *qquart(near, f, s)), part(i, *qquart(near, f, s)), RX2.at[k8(i)])
+                add(part(i, *qquart(near, f, s)), part(i, *qquart(near, f, s)), RX2.at[k7(i)])
                 C["X3"](i).start()
 
         def s6(i):
@@ -305,7 +306,7 @@
                 C["PT1"](i).wait()
                 C["PT3"](i).start()
                 C["X3"](i).wait()
-                part(i, *qquart(near, f, 1 - s))[...] = TX[k8(i)]
+                part(i, *qquart(near, f, 1 - s))[...] = TX[k7(i)]
                 C["X4"](i).start()
 
         def s7(i):
@@ -319,7 +320,7 @@
                 C["PT2"](i).wait_send()
                 C["PT3"](i).wait_send()
 
-            part(i, *pq(f, s))[...] = TQ[k8(i)]
+            part(i, *pq(f, s))[...] = TQ[k7(i)]
             C["G1"](i).start()
 
             @on_inner
@@ -454,7 +455,7 @@
     def back(self, a, src, dst, p, start):
         c, z, q = self.c, self.z, self.q
         tc, slot = lax.div(q, 2), lax.rem(q, 2)
-        s, d = src.at[pl.ds(2 * p, 2)], dst.at[slot, :, c]
+        s, d = src, dst.at[slot, :, c]
         far = remote(s, d, self.ss.at[a, p], self.rs.at[a, 2 * slot + c], (tc, z, jnp.int32(p)))
         near = pltpu.make_async_copy(s, d, self.ls.at[a])
         both_ways(jnp.logical_and(tc == c, p == q), near.start if start else near.wait, far.start if start else far.wait_send)
@@ -473,9 +474,9 @@
     return ((q > 0, q < 3, before), (q < 3, q > 0, after))
 
 
-def whole(lengths, inputs, cot_all, params, w_in, conv_w, w_out, dec, code, act, igr, total, cnt,
-          WI, WC, WO, PR, xe, cot, out1, first1, hidden1, sec1, mixed1, third1, first2, hidden2, sec2, dth2, sp, dthr, thirdr, dpad,
-          third2, dsec2, og, ge, hd, me, hold, dgbi, dgbm, counts, DG,
+def whole(lengths, inputs, cot_all, w_in, conv_w, w_out, gain_in, bias_in, gain_mid, bias_mid, dec, mask, types, act, igr, total, cnt,
+          WI, WC, WO, PR, xe, cot, out1, first1, hidden1, sec1, mixed1, third1, first2, hidden2, sec2, dth2, sp, dthr, dpad,
+          third2, dsec2, og, ge, hd, hold, dgbi, dgbm, counts, DG,
           ws, wr, wl, xs, xr, xl, ss, rs, ls, gs, gr, ps, pr, pw, *ring_refs, ring):
     c, z, q = lax.axis_index("section"), lax.axis_index("dp"), lax.axis_index("seq")
     peer = (1 - c, z, q)
@@ -484,14 +485,20 @@
     nd, nh = D // 128, H // 128
     rows = seg + 2 * HALO
     base = q * seg
-    he, dme = hd.at[pl.ds(0, rows)], hd.at[pl.ds(rows, rows)]
+    he, dme, me = hd.at[pl.ds(0, rows)], hd.at[pl.ds(rows, rows)], hd.at[pl.ds(rows, seg)]
     ring.bind(DG, total, *ring_refs)
     own = [pltpu.make_async_copy(inputs.at[2 * c + m, 0], xe.at[m, pl.ds(HALO, seg)], xl.at[m]) for m in range(2)]
     own += [pltpu.make_async_copy(cot_all.at[2 * c + m, 0], cot.at[m], xl.at[2 + m]) for m in range(2)]
-    mats = [(params, PR.at[c]), (w_in.at[0], WI.at[c])] + [(conv_w.at[0, k], WC.at[c, k]) for k in range(5)] + [(w_out.at[0], WO.at[c])]
-    loads = [pltpu.make_async_copy(s, d, wl.at[i]) for i, (s, d) in enumerate(mats)]
+    mats = [(PR.at[c], PR.at[c]), (w_in.at[0], WI.at[c])] + [(conv_w.at[0, k], WC.at[c, k]) for k in range(5)] + [(w_out.at[0], WO.at[c])]
+    loads = [pltpu.make_async_copy(s, d, wl.at[i]) for i, (s, d) in enumerate(mats) if i > 0]
     for cp in own[:2] + loads + own[2:]:
         cp.start()
+    PR[c, pl.ds(4, 4)] = jnp.zeros((4, D), F32)
+    PR[c, pl.ds(0, 1)] = gain_in[...].astype(F32)
+    PR[c, pl.ds(1, 1)] = bias_in[...].astype(F32)
+    for k in range(2):
+        PR[c, pl.ds(2, 1), pl.ds(k * H, H)] = gain_mid[0, pl.ds(k, 1)].astype(F32)
+        PR[c, pl.ds(3, 1), pl.ds(k * H, H)] = bias_mid[0, pl.ds(k, 1)].astype(F32)
     ring.barrier()
     sends = [remote(s, d, ws.at[i], wr.at[i], peer) for i, (s, d) in enumerate(mats)]
     halos = []
@@ -501,8 +508,17 @@
         halos.append((q < 3, q > 0, remote(x.at[pl.ds(seg - HALO, HALO)], xe.at[m, pl.ds(0, HALO)], xs.at[1, m], xr.at[1, m], (c, z, q + 1))))
     for cond, _, cp in halos:
         pl.when(cond)(cp.start)
-    for cp in sends:
-        cp.start()
+    sends[0].start()
+
+    @pl.when(c == 0)
+    def _():
+        for cp in sends[1:]:
+            cp.start()
+
+    @pl.when(c == 1)
+    def _():
+        for cp in sends[7:] + sends[1:7]:
+            cp.start()
 
     @pl.when(q == 0)
     def _():
@@ -514,9 +530,8 @@
         xe[:, pl.ds(HALO + seg, HALO)] = jnp.zeros((2, HALO, D), BF)
         ge[:, pl.ds(HALO + seg, HALO)] = jnp.zeros((2, HALO, D), BF)
 
-    def have(i):
-        loads[i].wait()
-        sends[i].wait_recv()
+    def have(i, layer):
+        both_ways(c == layer, loads[i - 1].wait, sends[i].wait_recv)
 
     for ref in (dgbi, dgbm, counts):
         ref[...] = jnp.zeros_like(ref)
@@ -533,7 +548,7 @@
     gm = lambda l, k: (lambda j: PR[l, pl.ds(2, 1), cols(k * nh + j)])
     bm = lambda l, k: (lambda j: PR[l, pl.ds(3, 1), cols(k * nh + j)])
 
-    have(0)
+    sends[0].wait_recv()
     for m in range(2):
         own[m].wait()
     for _, cond, cp in halos:
@@ -548,16 +563,25 @@
         return 0
 
     lax.fori_loop(0, 2, first_norm, 0)
-    have(1)
-
-    def forward(m, _):
-        length = lengths[2 * c + m]
+    for m in range(2):
+        own[2 + m].wait()
+    have(7, 1)
+
+    def third_grad(m, _):
+        dth2[m] = dot_nt(cot[m], WO[1]).astype(BF).reshape(2, 2, 64, H)
+        spread.go(1, dth2, dthr_at, m, True)
+        return 0
+
+    lax.fori_loop(0, 2, third_grad, 0)
+    have(1, 0)
+
+    def second_norm(m, _):
         he[...] = dot(first1[m], WI[0])
         hidden1[m] = he[pl.ds(HALO, seg)]
 
         def b(i, size):
             pos = positions(base - HALO, i, size)
-            keep = jnp.logical_and(pos >= 0, pos < length)
+            keep = jnp.logical_and(pos >= 0, pos < lengths[2 * c + m])
 
             def store(j, v):
                 sec1[m, pl.ds(i + 8, size), cols(j)] = jnp.where(keep, v, 0.0).astype(BF).astype(F32)
@@ -565,12 +589,13 @@
             norm_gelu(view(he, pl.ds(i, size)), nh, gm(0, 0), bm(0, 0), store)
 
         chunks(rows, b)
-
-        @pl.when(m == 0)
-        def _():
-            for k in range(5):
-                have(2 + k)
-
+        return 0
+
+    lax.fori_loop(0, 2, second_norm, 0)
+    for k in range(5):
+        have(2 + k, 0)
+
+    def forward(m, _):
         acc = None
         for k in range(5):
             term = dot(sec1[m, pl.ds(8 + DIL * (k - 2), rows)].astype(BF), WC[0, k])
@@ -584,7 +609,7 @@
 
         @pl.when(m == 0)
         def _():
-            have(7)
+            have(7, 0)
 
         he[pl.ds(0, seg)] = dot(third1[m], WO[0, :, :H])
         me[...] = dot(third1[m], WO[0, :, H:])
@@ -597,6 +622,11 @@
             norm_gelu(view(out1, m, r), nd, gi(1), bi(1), put(first2, m, r))
 
         chunks(seg, d)
+
+        @pl.when(m == 0)
+        def _():
+            have(1, 1)
+
         hidden2[m] = dot(first2[m], WI[1])
 
         def f(jj, _):
@@ -604,7 +634,7 @@
             pos = positions(base, i, 64)
 
             def store(j, v):
-                sec2[m, lax.div(jj, 2), lax.rem(jj, 2), :, cols(j)] = jnp.where(pos < length, v, 0.0).astype(BF)
+                sec2[m, lax.div(jj, 2), lax.rem(jj, 2), :, cols(j)] = jnp.where(pos < lengths[2 * c + m], v, 0.0).astype(BF)
 
             norm_gelu(view(hidden2, m, pl.ds(i, 64)), nh, gm(1, 0), bm(1, 0), store)
             return 0
@@ -614,15 +644,8 @@
         return 0
 
     lax.fori_loop(0, 2, forward, 0)
-    for m in range(2):
-        own[2 + m].wait()
-
-    def third_grad(m, _):
-        dth2[m] = dot_nt(cot[m], WO[1]).astype(BF).reshape(2, 2, 64, H)
-        spread.go(1, dth2, dthr_at, m, True)
-        return 0
-
-    lax.fori_loop(0, 2, third_grad, 0)
+    for k in range(5):
+        have(2 + k, 1)
 
     def place(i, src, dst, layer):
         to = dst.at[pl.ds(2 * c, 2)]
@@ -651,20 +674,24 @@
     def mid(i, _):
         every = pl.ds(0, 64)
         norm_gelu_both(view(hd, pl.ds(pl.multiple_of(64 * i, 64), 64)), view(dthr, i, every), nh, gm(1, 1), bm(1, 1), dgbm.at[2], dgbm.at[3], hold,
-                       put(thirdr, i, every), put(dpad, i + 2, every))
+                       put(dth2, lax.div(i, 4), lax.rem(lax.div(i, 2), 2), lax.rem(i, 2), every), put(dpad, i + 2, every))
         return 0
 
     lax.fori_loop(0, 8, mid, 0)
     for p in range(4):
-        spread.back(2, thirdr, third2, p, True)
+        spread.back(2, dth2.at[p // 2, p % 2], third2, p, True)
     dm2 = dpad[pl.ds(2, 8)].reshape(512, H)
 
     def conv_grads(k, _):
         put_grad(DG, c, CONV0 + k * 100, dot_tn(sp[pl.ds(k, 8)].reshape(512, H), dm2))
+
+        @pl.when(k % 2 == 1)
+        def _():
+            ring.step(lax.div(k, 2))
+
         return 0
 
     lax.fori_loop(0, 5, conv_grads, 0)
-    ring.step(0)
 
     def conv_back(r, _):
         acc = None
@@ -676,38 +703,19 @@
 
     lax.fori_loop(0, 2, conv_back, 0)
     for p in range(4):
-        spread.back(3, dthr, dsec2, p, True)
-    ring.step(1)
-    for p in range(4):
-        spread.back(2, thirdr, third2, p, False)
-    for m in range(2):
-        spread.back_arrive(2, thirdr, third2, m)
-    labels = lax.broadcasted_iota(jnp.int32, (1, 128), 1)
-
-    def two_out(m, _):
-        t = third2[m].reshape(seg, H)
-        he[pl.ds(0, seg)] = dot(t, WO[1, :, :H])
-        me[...] = dot(t, WO[1, :, H:])
-
-        def a(i, size):
-            r = pl.ds(i, size)
-            for j in range(nd):
-                br = he[r, cols(j)] if j < nh else me[r, cols(j - nh)]
-                og[m, r, cols(j)] = (out1[m, r, cols(j)].astype(F32) + br).astype(BF)
-
-        chunks(seg, a)
-        logits = jnp.where(labels < 30, dot(og[m], dec[...]), -1e30)
-        ex = jnp.exp(logits - jnp.max(logits, axis=-1, keepdims=True))
-        probs = ex / jnp.sum(ex, axis=-1, keepdims=True)
-        kept = positions(base, 0, seg) < lengths[2 * c + m]
-        counts[...] += fold(jnp.where(jnp.logical_and(code[2 * c + m] == labels, kept), probs, 0.0))
-        return 0
-
-    lax.fori_loop(0, 2, two_out, 0)
-    placed.append(place(1, og, act, 1))
+        spread.back(3, dthr.at[pl.ds(2 * p, 2)], dsec2, p, True)
     ring.step(2)
     for p in range(4):
-        spread.back(3, dthr, dsec2, p, False)
+        spread.back(2, dth2.at[p // 2, p % 2], third2, p, False)
+    for m in range(2):
+        spread.back_arrive(2, dthr, third2, m)
+    flat = lambda v: v.reshape(2 * seg, v.shape[-1])
+    t2 = flat(third2[...])
+    for j in range(2):
+        put_grad(DG, c, OUT0, dot_tn(t2, flat(cot[:, :, pl.ds(j * H, H)])), nh * j)
+    ring.step(3)
+    for p in range(4):
+        spread.back(3, dthr.at[pl.ds(2 * p, 2)], dsec2, p, False)
     for m in range(2):
         spread.back_arrive(3, dthr, dsec2, m)
     dh = lambda m: dpad.at[pl.ds(4 * m, 4)]
@@ -738,16 +746,11 @@
         chunks(seg, e)
         for cond, _, cp in edges(ge, m, seg, gs, gr, z, q, c):
             pl.when(cond)(cp.start)
-        ring.step(3 + m)
+        ring.step(4 + m)
         return 0
 
     lax.fori_loop(0, 2, two, 0)
     placed.append(place(2, ge.at[:, pl.ds(HALO, seg)], igr, 1))
-    flat = lambda v: v.reshape(2 * seg, v.shape[-1])
-    t2 = flat(third2[...])
-    for j in range(2):
-        put_grad(DG, c, OUT0, dot_tn(t2, flat(cot[:, :, pl.ds(j * H, H)])), nh * j)
-    ring.step(5)
     put_grad(DG, c, IN0, dot_tn(flat(first2[...]), dpad[pl.ds(0, 8)].reshape(2 * seg, H)))
 
     def extra(first_unit, with_counts):
@@ -755,7 +758,7 @@
         flat_rows += [dgbm[k, :, cols(j)] for k in range(4) for j in range(nh)]
         small = [jnp.sum(v, axis=0, keepdims=True) for v in flat_rows]
         if with_counts:
-            small.append(jnp.sum(counts[...], axis=0, keepdims=True))
+            small.append(jnp.pad(jnp.sum(counts[...], axis=0, keepdims=True), ((0, 0), (0, 128 - classes))))
         size = UNITS - EXTRA0
         small.append(jnp.zeros((48 - len(small), 128), F32))
         block = jnp.concatenate(small, axis=0).astype(BF).reshape(3, 16, 128)
@@ -763,7 +766,7 @@
             DG[h, pl.ds(first_unit, 3)] = block
             DG[h, pl.ds(first_unit + 3, size - 3)] = jnp.zeros((size - 3, 16, 128), BF)
 
-    extra(EXTRA0, True)
+    extra(EXTRA0, False)
     ring.step(6)
     for ref in (dgbi, dgbm):
         ref[...] = jnp.zeros_like(ref)
@@ -771,8 +774,6 @@
         for s_cond, r_cond, cp in edges(ge, m, seg, gs, gr, z, q, c):
             pl.when(s_cond)(cp.wait_send)
             pl.when(r_cond)(cp.wait_recv)
-    for done in placed[:2]:
-        done()
     dm = lambda m: dsec2.at[m]
 
     def one(m, _):
@@ -800,7 +801,6 @@
                 dme[r, cols(j)] = jnp.where(within, v, 0.0).astype(BF).astype(F32)
 
             norm_gelu_back(view(mixed1, m, r), view(he, r), nh, gm(0, 1), bm(0, 1), None, None, hold.at[:, pl.ds(0, HALO)], store)
-        ring.step(7 + 3 * m)
         acc = None
         for k in range(5):
             term = dot_nt(dme[pl.ds(HALO - DIL * (k - 2), seg)].astype(BF), WC[0, k])
@@ -815,56 +815,93 @@
             return 0
 
         lax.fori_loop(0, seg // 64, b, 0)
-        ring.step(8 + 3 * m)
-        dhm = dh(m)[...].reshape(seg, H)
-        he[pl.ds(0, seg)] = dot_nt(dhm, WI[0, :H])
-        me[...] = dot_nt(dhm, WI[0, H:])
-
-        def e(i, size):
-            r, x = pl.ds(i, size), pl.ds(i + HALO, size)
-            df = lambda j: he[r, cols(j)] if j < nh else me[r, cols(j - nh)]
-
-            def store(j, v):
-                og[m, r, cols(j)] = (ge[m, x, cols(j)].astype(F32) + v).astype(BF)
-
-            norm_gelu_back(view(xe, m, x), df, nd, gi(0), bi(0), dgbi.at[0], dgbi.at[1], hold, store)
-
-        chunks(seg, e)
-        ring.step(9 + 3 * m)
+        ring.step(7 + m)
         return 0
 
     lax.fori_loop(0, 2, one, 0)
-    placed.append(place(3, og, igr, 0))
     low = UNITS
     t1 = flat(third1[...])
     for j in range(2):
         put_grad(DG, c, low + OUT0, dot_tn(t1, flat(ge[:, pl.ds(HALO, seg), pl.ds(j * H, H)])), nh * j)
-    ring.step(13)
+    ring.step(9)
     d1 = flat(dsec2[...])
     for k in range(5):
         for m in range(2):
-            third2[m] = sec1[m, pl.ds(8 + HALO + DIL * (k - 2), seg)].astype(BF).reshape(2, 2, 64, H)
-        put_grad(DG, c, low + CONV0 + k * 100, dot_tn(flat(third2[...]), d1))
+            sec2[m] = sec1[m, pl.ds(8 + HALO + DIL * (k - 2), seg)].astype(BF).reshape(2, 2, 64, H)
+        put_grad(DG, c, low + CONV0 + k * 100, dot_tn(flat(sec2[...]), d1))
         if k in (1, 3):
-            ring.step(14 + k // 2)
+            ring.step(10 + k // 2)
     put_grad(DG, c, low + IN0, dot_tn(flat(first1[:, pl.ds(HALO, seg)]), dpad[pl.ds(0, 8)].reshape(2 * seg, H)))
-    extra(low + EXTRA0, False)
+    ring.step(12)
+    classes = dec.shape[0]
+    labels = lax.broadcasted_iota(jnp.int32, (1, classes), 1).astype(F32)
+
+    def two_out(m, _):
+        t = third2[m].reshape(seg, H)
+        he[pl.ds(0, seg)] = dot(t, WO[1, :, :H])
+        me[...] = dot(t, WO[1, :, H:])
+
+        def a(i, size):
+            r = pl.ds(i, size)
+            for j in range(nd):
+                br = he[r, cols(j)] if j < nh else me[r, cols(j - nh)]
+                og[m, r, cols(j)] = (out1[m, r, cols(j)].astype(F32) + br).astype(BF)
+
+        chunks(seg, a)
+        logits = dot_nt(og[m], dec[...])
+        ex = jnp.exp(logits - jnp.max(logits, axis=-1, keepdims=True))
+        probs = ex / jnp.sum(ex, axis=-1, keepdims=True)
+        pos = base + lax.broadcasted_iota(jnp.int32, (1, seg), 1)
+        live = jnp.logical_and(mask[2 * c + m] == 1, pos < lengths[2 * c + m])
+        code = jnp.where(live, types[2 * c + m], -1).astype(F32)
+        code = jnp.broadcast_to(code, (128, seg)).T[:, :classes]
+        counts[...] += fold(jnp.where(code == labels, probs, 0.0))
+        ring.step(13 + m)
+        return 0
+
+    lax.fori_loop(0, 2, two_out, 0)
+    placed.append(place(1, og, act, 1))
+    placed[-1]()
+
+    def one_in(m, _):
+        dhm = dh(m)[...].reshape(seg, H)
+        he[pl.ds(0, seg)] = dot_nt(dhm, WI[0, :H])
+        me[...] = dot_nt(dhm, WI[0, H:])
+        ring.step(15 + m)
+
+        def e(i, _):
+            r, x = pl.ds(pl.multiple_of(i * 64, 64), 64), pl.ds(pl.multiple_of(i * 64 + HALO, 16), 64)
+            df = lambda j: he[r, cols(j)] if j < nh else me[r, cols(j - nh)]
+
+            def store(j, v):
+                og[m, r, cols(j)] = (ge[m, x, cols(j)].astype(F32) + v).astype(BF)
+
+            norm_gelu_back(view(xe, m, x), df, nd, gi(0), bi(0), dgbi.at[0], dgbi.at[1], hold, store)
+
+            return 0
+
+        lax.fori_loop(0, seg // 64, e, 0)
+        return 0
+
+    lax.fori_loop(0, 2, one_in, 0)
+    placed.append(place(3, og, igr, 0))
+    extra(low + EXTRA0, True)
 
     def rest(t, _):
         ring.step(t)
         return 0
 
     if ring.live:
-        lax.fori_loop(16, ring.iters, rest, 0)
+        lax.fori_loop(17, ring.iters, rest, 0)
         ring.finish()
-        cnt[...] = DG[0, pl.ds(EXTRA0, 3)]
+        cnt[...] = DG[0, pl.ds(UNITS + EXTRA0, 3)]
     else:
         everything = pltpu.make_async_copy(DG, total, pw.at[0])
         everything.start()
         everything.wait()
         cnt[...] = jnp.zeros_like(cnt)
-    for done in placed[2:]:
-        done()
+    for i in (0, 1, 3):
+        placed[i]()
     for i, dst in ((0, act), (1, igr)):
         remote(og, dst.at[pl.ds(2 * (1 - c), 2)], ps.at[0], pr.at[i], peer).wait_recv()
     for cp in sends:
@@ -873,7 +910,7 @@
         pl.when(cond)(cp.wait_send)
 
 
-def run(ring, lengths, inputs, cot, params, w_in, conv_w, w_out, dec, code):
+def run(ring, lengths, inputs, cot, w_in, conv_w, w_out, gain_in, bias_in, gain_mid, bias_mid, dec, mask, types):
     seg, D, H = inputs.shape[2], inputs.shape[3], w_in.shape[2]
     rows = seg + 2 * HALO
     any_, vm, sm = (pl.BlockSpec(memory_space=s) for s in (pl.ANY, pltpu.VMEM, pltpu.SMEM))
@@ -882,19 +919,19 @@
     part = (2, 2, 2, 64, H)
     scratch = [((2, D, H), BF), ((2, 5, H, H), BF), ((2, H, D), BF), ((2, 8, D), F32), ((2, rows, D), BF), ((2, seg, D), BF),
                ((2, seg, D), BF), ((2, rows, D), BF), ((2, seg, H), F32), ((2, rows + 16, H), F32), ((2, rows, H), F32), ((2, seg, H), BF),
-               ((2, seg, D), BF), ((2, seg, H), F32), (part, BF), (part, BF), ((12, 64, H), BF), ((8, 64, H), BF), ((8, 64, H), BF),
-               ((12, 64, H), BF), (part, BF), (part, BF), ((2, seg, D), BF), ((2, rows, D), BF), ((2 * rows, H), F32), ((seg, H), F32),
-               ((2, 64, D), F32), ((2, 8, D), F32), ((4, 8, H), F32), ((8, 128), F32), ((2, 2 * UNITS, 16, 128), BF)]
+               ((2, seg, D), BF), ((2, seg, H), F32), (part, BF), (part, BF), ((12, 64, H), BF), ((8, 64, H), BF),
+               ((12, 64, H), BF), (part, BF), (part, BF), ((2, seg, D), BF), ((2, rows, D), BF), ((2 * rows, H), F32),
+               ((2, 64, D), F32), ((2, 8, D), F32), ((4, 8, H), F32), ((8, dec.shape[0]), F32), ((2, 2 * UNITS, 16, 128), BF)]
     return pl.pallas_call(
         functools.partial(whole, ring=ring),
         out_shape=[sh((4, seg, D), BF), sh((4, seg, D), BF), sh((2, ring.out_units, 16, 128), BF), sh((3, 16, 128), BF)],
-        in_specs=[sm] + [any_] * 6 + [vm, vm],
+        in_specs=[sm] + [any_] * 5 + [vm] * 7,
         out_specs=[any_, any_, any_, vm],
         scratch_shapes=[pltpu.VMEM(s, d) for s, d in scratch]
         + [dma(8), dma(8), dma(8), dma(2, 2), dma(2, 2), dma(4), dma(4, 4), dma(4, 4), dma(4), dma(2, 2), dma(2, 2), dma(4), dma(2), dma(4)]
         + ring.scratch(),
         compiler_params=pltpu.CompilerParams(collective_id=1, has_side_effects=True, vmem_limit_bytes=63 * 2**20 + 2**19),
-    )(lengths, inputs, cot, params, w_in, conv_w, w_out, dec, code)
+    )(lengths, inputs, cot, w_in, conv_w, w_out, gain_in, bias_in, gain_mid, bias_mid, dec, mask, types)
 
 
 def unpack_kernel(conv, w_out, w_in, extra, cnt, s_conv, s_out, s_in, gi, bi, gm, bm, counts):
@@ -918,10 +955,10 @@
             for j in range(5):
                 gm[0, pl.ds(k, 1), cols(j)] = small[20 + 10 * k + j : 21 + 10 * k + j]
                 bm[0, pl.ds(k, 1), cols(j)] = small[25 + 10 * k + j : 26 + 10 * k + j]
-        counts[...] = cnt[...].reshape(48, 128)[40:41].astype(F32)
-
-
-def unpack(total, cnt, D, H):
+        counts[...] = cnt[...].reshape(48, 128)[40, : counts.shape[0]].astype(F32)
+
+
+def unpack(total, cnt, D, H, classes):
     def spec(units, first, moves=1):
         return pl.BlockSpec(tuple(pl.Element(n) for n in (2, units, 16, 128)), lambda k: (0, first + units * k * moves, 0, 0))
 
@@ -932,21 +969,19 @@
     return pl.pallas_call(
         unpack_kernel,
         grid=(5,),
-        out_shape=[sh(1, 5, H, H), sh(1, H, D), sh(1, D, H), sh(1, D), sh(1, D), sh(1, 2, H), sh(1, 2, H), sh(1, 128)],
+        out_shape=[sh(1, 5, H, H), sh(1, H, D), sh(1, D, H), sh(1, D), sh(1, D), sh(1, 2, H), sh(1, 2, H), sh(classes)],
         in_specs=[spec(100, CONV0), spec(40, OUT0), spec(40, IN0), spec(36, EXTRA0, 0), full(3, 16, 128)],
         out_specs=[pl.BlockSpec((1, 1, H, H), lambda k: (0, k, 0, 0)), pl.BlockSpec((1, H, 256), lambda k: (0, 0, k)),
-                   pl.BlockSpec((1, D, 128), lambda k: (0, 0, k)), full(1, D), full(1, D), full(1, 2, H), full(1, 2, H), full(1, 128)],
+                   pl.BlockSpec((1, D, 128), lambda k: (0, 0, k)), full(1, D), full(1, D), full(1, 2, H), full(1, 2, H), full(classes)],
         compiler_params=pltpu.CompilerParams(vmem_limit_bytes=60 * 2**20),
     )(total, total, total, total, cnt)
 
 
 def body(inputs, lengths, mlm_mask, true_types, gain_in, bias_in, gain_mid, bias_mid, w_in, conv_w, w_out, decoder, cotangent, fast):
     D, H = inputs.shape[3], w_in.shape[2]
-    params = jnp.concatenate([gain_in, bias_in, gain_mid.reshape(1, D), bias_mid.reshape(1, D), jnp.zeros((4, D), BF)]).astype(F32)
-    dec = jnp.pad(decoder, ((0, 0), (0, 128 - decoder.shape[1])))
-    code = jnp.where(mlm_mask[:, 0] == 1, true_types[:, 0], -1)[..., None]
     ring = Ring(PIECES, PLANE_UNITS, Z_UNITS) if fast else NoRing(PIECES, PLANE_UNITS + Z_UNITS)
-    act, igr, total, cnt = run(ring, lengths[:, 0], inputs, cotangent, params, w_in, conv_w, w_out, dec, code)
+    act, igr, total, cnt = run(
+        ring, lengths[:, 0], inputs, cotangent, w_in, conv_w, w_out, gain_in, bias_in, gain_mid, bias_mid, decoder.T, mlm_mask, true_types)
     if not fast:
         c = lax.axis_index("section")
         halves = jnp.where(c == 0, total, total[::-1])
@@ -954,9 +989,9 @@
         own, other = jnp.where(c == 0, g_one, g_two), jnp.where(c == 0, g_two, g_one)
         got = lax.ppermute(other, "section", [(0, 1), (1, 0)])
         total = lax.psum(own.astype(F32) + got.astype(F32), ("dp", "seq")).astype(BF)
-        cnt = lax.psum(g_two[0, EXTRA0 : EXTRA0 + 3].astype(F32), ("section", "dp", "seq")).astype(BF)
-    s_conv, s_out, s_in, s_gi, s_bi, s_gm, s_bm, s_cnt = unpack(total, cnt, D, H)
-    return (act[None, :, None], igr[None, :, None], s_gi, s_bi, s_gm, s_bm, s_in, s_conv, s_out, s_cnt[0, : decoder.shape[1]])
+        cnt = lax.psum(g_one[0, EXTRA0 : EXTRA0 + 3].astype(F32), ("section", "dp", "seq")).astype(BF)
+    s_conv, s_out, s_in, s_gi, s_bi, s_gm, s_bm, s_cnt = unpack(total, cnt, D, H, decoder.shape[1])
+    return (act[None, :, None], igr[None, :, None], s_gi, s_bi, s_gm, s_bm, s_in, s_conv, s_out, s_cnt)
 
 
 def solution(mesh):

time: 233 us -> 216 us (0.927)
  Pallas kernels: 220 us -> 210 us
  local copies, waits for them, and re-layouts: 10.4 us -> 4.17 us
    pallas_call x1, Pallas kernels: 210 us -> 201 us  [run(): pl.pallas_call(functools.partial(whole, ring=ring), out_shape=[sh((4, seg...]
    unnamed x9 -> x6, local copies, waits for them, and re-layouts: 6.68 us -> 4.17 us
where the time goes in v5:
time: 216 us; the launch traced here: 215 us
  Pallas kernels  210 us (97%)
  local copies, waits for them, and re-layouts  4.17 us (2%)
    pallas_call x1, Pallas kernels, run(): pl.pallas_call(functools.partial(whole, ring=ring), out_shape=[sh((4, seg...  201 us
    pallas_call x1, Pallas kernels, unpack(): pl.pallas_call(unpack_kernel, grid=(5,), out_shape=[sh(1, 5, H, H), sh(1,...  9.3 us

profile of v5, /device:TPU:0, one launch (start us, length us, event | category | flops | bytes accessed | tf_op | source)
XLA Modules:
  0.0 215.3 jit_solution(6357349193822278256)
XLA Ops:
  0.6 201.2 %shard_map.204 = (bf16[4,256,1280]{2,1,0:T(8,128)(2,1)}, bf16[4,256,1280]{2,1,0:T(8,128)(2,1)}, bf16[2,936,16,128]{3,2,1,0:T(8,128)(2,1)}, bf16[3,16,128]{2,1,0:T(8,128)(2,1)}) custom-call(s32[4]{0:T(128)} %bitcast.11, bf16[4,1,256,1280]{3,2,1,0:T(8,128)(2,1)} %inputs.1, bf16[4,1,256,1280]{3,2,1,0:T(8,128)(2,1)} %cot_all.1, bf16[1,1280,640]{2,1,0:T(8,128)(2,1)} %w_in.1, ...), custom_call_target="tpu_custom_call" | custom-call | tf_op jit(solution)/shard_map/pallas_call | solution.py:925
  201.8 0.0 copy-start.1
  201.8 9.3 %shard_map.205 = (f32[1,5,640,640]{3,2,1,0:T(8,128)}, f32[1,640,1280]{2,1,0:T(8,128)}, f32[1,1280,640]{2,1,0:T(8,128)}, f32[1,1280]{1,0:T(1,128)}, f32[1,1280]{1...) custom-call(bf16[2,936,16,128]{3,2,1,0:T(8,128)(2,1)} %get-tuple-element.24.conv.w_out.w_in.extra, ...), custom_call_target="tpu_custom_call" | custom-call | tf_op jit(solution)/shard_map/pallas_call | solution.py:969
  211.1 0.0 copy-done.1
  211.1 0.0 copy-start
  211.1 1.5 copy.27
  212.6 1.2 copy-done
  213.8 1.5 copy.28
Async XLA Ops:
  201.8 9.3 %copy-start.1 = (bf16[4,256,1280]{2,1,0:T(8,128)(2,1)S(1)}, bf16[4,256,1280]{2,1,0:T(8,128)(2,1)}, u32[]{:S(2)}) copy-start(bf16[4,256,1280]{2,1,0:T(8,128)(2,1)} %get-tuple-element.22) | copy-start | bytes 7864324
  211.1 2.7 %copy-start = (bf16[4,256,1280]{2,1,0:T(8,128)(2,1)S(1)}, bf16[4,256,1280]{2,1,0:T(8,128)(2,1)}, u32[]{:S(2)}) copy-start(bf16[4,256,1280]{2,1,0:T(8,128)(2,1)} %get-tuple-element.23) | copy-start | bytes 7864324

commit v6 on v5

--- a/solution.py
+++ b/solution.py
@@ -31,14 +31,14 @@
     return lax.dot_general(a, b, (((0,), (0,)), ((), ())), preferred_element_type=F32)
 
 
-def chunks(rows, fn, size=None):
+def chunks(rows, fn, size=None, unroll=1):
     size = size or (96 if rows % 96 == 0 else 64)
 
     def one(i, _):
         fn(pl.multiple_of(i * size, size), size)
         return 0
 
-    lax.fori_loop(0, rows // size, one, 0)
+    lax.fori_loop(0, rows // size, one, 0, unroll=unroll)
 
 
 def cols(j):
@@ -559,7 +559,7 @@
             r = pl.ds(i, size)
             norm_gelu(view(xe, m, r), nd, gi(0), bi(0), put(first1, m, r))
 
-        chunks(rows, a)
+        chunks(rows, a, unroll=3)
         return 0
 
     lax.fori_loop(0, 2, first_norm, 0)
@@ -588,7 +588,7 @@
 
             norm_gelu(view(he, pl.ds(i, size)), nh, gm(0, 0), bm(0, 0), store)
 
-        chunks(rows, b)
+        chunks(rows, b, unroll=3)
         return 0
 
     lax.fori_loop(0, 2, second_norm, 0)
@@ -605,7 +605,7 @@
         def e(i, size):
             norm_gelu(view(mixed1, m, pl.ds(i + HALO, size)), nh, gm(0, 1), bm(0, 1), put(third1, m, pl.ds(i, size)))
 
-        chunks(seg, e)
+        chunks(seg, e, unroll=4)
 
         @pl.when(m == 0)
         def _():
@@ -621,7 +621,7 @@
                 out1[m, r, cols(j)] = (xe[m, pl.ds(i + HALO, size), cols(j)].astype(F32) + br).astype(BF)
             norm_gelu(view(out1, m, r), nd, gi(1), bi(1), put(first2, m, r))
 
-        chunks(seg, d)
+        chunks(seg, d, unroll=4)
 
         @pl.when(m == 0)
         def _():
@@ -639,7 +639,7 @@
             norm_gelu(view(hidden2, m, pl.ds(i, 64)), nh, gm(1, 0), bm(1, 0), store)
             return 0
 
-        lax.fori_loop(0, seg // 64, f, 0)
+        lax.fori_loop(0, seg // 64, f, 0, unroll=4)
         spread.go(0, sec2, sp_at, m, True)
         return 0
 
@@ -677,7 +677,7 @@
                        put(dth2, lax.div(i, 4), lax.rem(lax.div(i, 2), 2), lax.rem(i, 2), every), put(dpad, i + 2, every))
         return 0
 
-    lax.fori_loop(0, 8, mid, 0)
+    lax.fori_loop(0, 8, mid, 0, unroll=4)
     for p in range(4):
         spread.back(2, dth2.at[p // 2, p % 2], third2, p, True)
     dm2 = dpad[pl.ds(2, 8)].reshape(512, H)
@@ -729,7 +729,7 @@
                            put(dpad, 4 * m + i, pl.ds(0, 64)))
             return 0
 
-        lax.fori_loop(0, seg // 64, b, 0)
+        lax.fori_loop(0, seg // 64, b, 0, unroll=2)
         dhm = dh(m)[...].reshape(seg, H)
         he[pl.ds(0, seg)] = dot_nt(dhm, WI[1, :H])
         me[...] = dot_nt(dhm, WI[1, H:])
@@ -743,7 +743,7 @@
 
             norm_gelu_back(view(out1, m, r), df, nd, gi(1), bi(1), dgbi.at[0], dgbi.at[1], hold, store)
 
-        chunks(seg, e)
+        chunks(seg, e, unroll=2)
         for cond, _, cp in edges(ge, m, seg, gs, gr, z, q, c):
             pl.when(cond)(cp.start)
         ring.step(4 + m)
@@ -791,7 +791,7 @@
             norm_gelu_back(view(mixed1, m, r), view(he, r), nh, gm(0, 1), bm(0, 1), dgbm.at[2], dgbm.at[3], hold, store)
             return 0
 
-        lax.fori_loop(0, seg // 64, a, 0)
+        lax.fori_loop(0, seg // 64, a, 0, unroll=2)
         for edge in (0, rows - HALO):
             r = pl.ds(edge, HALO)
             pos = positions(base - HALO, edge, HALO)
@@ -814,7 +814,7 @@
             norm_gelu_back(view(hidden1, m, r), ds, nh, gm(0, 0), bm(0, 0), dgbm.at[0], dgbm.at[1], hold, put(dpad, 4 * m + i, pl.ds(0, 64)))
             return 0
 
-        lax.fori_loop(0, seg // 64, b, 0)
+        lax.fori_loop(0, seg // 64, b, 0, unroll=2)
         ring.step(7 + m)
         return 0
 
@@ -934,8 +934,9 @@
     )(lengths, inputs, cot, w_in, conv_w, w_out, gain_in, bias_in, gain_mid, bias_mid, dec, mask, types)
 
 
-def unpack_kernel(conv, w_out, w_in, extra, cnt, s_conv, s_out, s_in, gi, bi, gm, bm, counts):
-    H = s_conv.shape[-1]
+def unpack_kernel(conv, w_out, w_in, extra, cnt, act, igr, s_conv, s_out, s_in, gi, bi, gm, bm, counts, act_o, igr_o):
+    act_o[...] = act[...]
+    igr_o[...] = igr[...]
     for j in range(5):
         for h in range(2):
             s_conv[0, 0, pl.ds(h * 320, 320), cols(j)] = conv[h, pl.ds(j * 20, 20)].reshape(320, 128).astype(F32)
@@ -958,23 +959,25 @@
         counts[...] = cnt[...].reshape(48, 128)[40, : counts.shape[0]].astype(F32)
 
 
-def unpack(total, cnt, D, H, classes):
+def unpack(total, cnt, act, igr, D, H, classes):
     def spec(units, first, moves=1):
         return pl.BlockSpec(tuple(pl.Element(n) for n in (2, units, 16, 128)), lambda k: (0, first + units * k * moves, 0, 0))
 
     def full(*s):
         return pl.BlockSpec(s, lambda k: (0,) * len(s))
 
+    block = pl.BlockSpec((1, *act.shape[1:]), lambda k: (jnp.minimum(k, act.shape[0] - 1), 0, 0))
     sh = lambda *s: jax.ShapeDtypeStruct(s, F32)
     return pl.pallas_call(
         unpack_kernel,
         grid=(5,),
-        out_shape=[sh(1, 5, H, H), sh(1, H, D), sh(1, D, H), sh(1, D), sh(1, D), sh(1, 2, H), sh(1, 2, H), sh(classes)],
-        in_specs=[spec(100, CONV0), spec(40, OUT0), spec(40, IN0), spec(36, EXTRA0, 0), full(3, 16, 128)],
+        out_shape=[sh(1, 5, H, H), sh(1, H, D), sh(1, D, H), sh(1, D), sh(1, D), sh(1, 2, H), sh(1, 2, H), sh(classes),
+                   jax.ShapeDtypeStruct(act.shape, BF), jax.ShapeDtypeStruct(igr.shape, BF)],
+        in_specs=[spec(100, CONV0), spec(40, OUT0), spec(40, IN0), spec(36, EXTRA0, 0), full(3, 16, 128), block, block],
         out_specs=[pl.BlockSpec((1, 1, H, H), lambda k: (0, k, 0, 0)), pl.BlockSpec((1, H, 256), lambda k: (0, 0, k)),
-                   pl.BlockSpec((1, D, 128), lambda k: (0, 0, k)), full(1, D), full(1, D), full(1, 2, H), full(1, 2, H), full(classes)],
+                   pl.BlockSpec((1, D, 128), lambda k: (0, 0, k)), full(1, D), full(1, D), full(1, 2, H), full(1, 2, H), full(classes), block, block],
         compiler_params=pltpu.CompilerParams(vmem_limit_bytes=60 * 2**20),
-    )(total, total, total, total, cnt)
+    )(total, total, total, total, cnt, act, igr)
 
 
 def body(inputs, lengths, mlm_mask, true_types, gain_in, bias_in, gain_mid, bias_mid, w_in, conv_w, w_out, decoder, cotangent, fast):
@@ -990,7 +993,7 @@
         got = lax.ppermute(other, "section", [(0, 1), (1, 0)])
         total = lax.psum(own.astype(F32) + got.astype(F32), ("dp", "seq")).astype(BF)
         cnt = lax.psum(g_one[0, EXTRA0 : EXTRA0 + 3].astype(F32), ("section", "dp", "seq")).astype(BF)
-    s_conv, s_out, s_in, s_gi, s_bi, s_gm, s_bm, s_cnt = unpack(total, cnt, D, H, decoder.shape[1])
+    s_conv, s_out, s_in, s_gi, s_bi, s_gm, s_bm, s_cnt, act, igr = unpack(total, cnt, act, igr, D, H, decoder.shape[1])
     return (act[None, :, None], igr[None, :, None], s_gi, s_bi, s_gm, s_bm, s_in, s_conv, s_out, s_cnt)
 
 

time: 216 us -> 205 us (0.949)
  Pallas kernels: 210 us -> 204 us
  local copies, waits for them, and re-layouts: 4.17 us -> 0 us
    pallas_call x1, Pallas kernels: 201 us -> 192 us  [run(): pl.pallas_call(functools.partial(whole, ring=ring), out_shape=[sh((4, seg...]
    unnamed x6 -> x0, local copies, waits for them, and re-layouts: 4.17 us -> none
    pallas_call x1, Pallas kernels: 9.3 us -> 12.1 us  [unpack(): pl.pallas_call(unpack_kernel, grid=(5,), out_shape=[sh(1, 5, H, H), sh(1,...]
where the time goes in v6:
time: 205 us
  Pallas kernels  204 us (100%)
    pallas_call x1, Pallas kernels, run(): pl.pallas_call(functools.partial(whole, ring=ring), out_shape=[sh((4, seg...  192 us
    pallas_call x1, Pallas kernels, unpack(): pl.pallas_call(unpack_kernel, grid=(5,), out_shape=[sh(1, 5, H, H), sh(1,...  12.1 us

profile of v6, /device:TPU:0, one launch (start us, length us, event | category | flops | bytes accessed | tf_op | source)
XLA Modules:
  0.0 204.8 jit_solution(17807759806818614919)
XLA Ops:
  0.6 191.8 %shard_map.204 = (bf16[4,256,1280]{2,1,0:T(8,128)(2,1)}, bf16[4,256,1280]{2,1,0:T(8,128)(2,1)}, bf16[2,936,16,128]{3,2,1,0:T(8,128)(2,1)}, bf16[3,16,128]{2,1,0:T(8,128)(2,1)}) custom-call(s32[4]{0:T(128)} %bitcast.9, bf16[4,1,256,1280]{3,2,1,0:T(8,128)(2,1)} %inputs.1, bf16[4,1,256,1280]{3,2,1,0:T(8,128)(2,1)} %cot_all.1, bf16[1,1280,640]{2,1,0:T(8,128)(2,1)} %w_in.1, ...), custom_call_target="tpu_custom_call" | custom-call | tf_op jit(solution)/shard_map/pallas_call | solution.py:925
  192.5 12.1 %shard_map.205 = (f32[1,5,640,640]{3,2,1,0:T(8,128)}, f32[1,640,1280]{2,1,0:T(8,128)}, f32[1,1280,640]{2,1,0:T(8,128)}, f32[1,1280]{1,0:T(1,128)}, f32[1,1280]{1...) custom-call(bf16[2,936,16,128]{3,2,1,0:T(8,128)(2,1)} %get-tuple-ele, ...), custom_call_target="tpu_custom_call" | custom-call | tf_op jit(solution)/shard_map/pallas_call | solution.py:971

commit v7 on v6

--- a/solution.py
+++ b/solution.py
@@ -682,16 +682,10 @@
         spread.back(2, dth2.at[p // 2, p % 2], third2, p, True)
     dm2 = dpad[pl.ds(2, 8)].reshape(512, H)
 
-    def conv_grads(k, _):
+    for k in range(5):
         put_grad(DG, c, CONV0 + k * 100, dot_tn(sp[pl.ds(k, 8)].reshape(512, H), dm2))
-
-        @pl.when(k % 2 == 1)
-        def _():
-            ring.step(lax.div(k, 2))
-
-        return 0
-
-    lax.fori_loop(0, 5, conv_grads, 0)
+        if k in (1, 3):
+            ring.step(k // 2)
 
     def conv_back(r, _):
         acc = None

time: 205 us -> 205 us (level)
  no operation moved by 1% of the time
where the time goes in v7:
time: 205 us; the launch traced here: 204 us
  Pallas kernels  204 us (100%)
    pallas_call x1, Pallas kernels, run(): pl.pallas_call(functools.partial(whole, ring=ring), out_shape=[sh((4, seg...  191 us
    pallas_call x1, Pallas kernels, unpack(): pl.pallas_call(unpack_kernel, grid=(5,), out_shape=[sh(1, 5, H, H), sh(1,...  12.1 us

profile of v7, /device:TPU:0, one launch (start us, length us, event | category | flops | bytes accessed | tf_op | source)
XLA Modules:
  0.0 204.4 jit_solution(15444133083500008768)
XLA Ops:
  0.6 191.5 %shard_map.204 = (bf16[4,256,1280]{2,1,0:T(8,128)(2,1)}, bf16[4,256,1280]{2,1,0:T(8,128)(2,1)}, bf16[2,936,16,128]{3,2,1,0:T(8,128)(2,1)}, bf16[3,16,128]{2,1,0:T(8,128)(2,1)}) custom-call(s32[4]{0:T(128)} %bitcast.9, bf16[4,1,256,1280]{3,2,1,0:T(8,128)(2,1)} %inputs.1, bf16[4,1,256,1280]{3,2,1,0:T(8,128)(2,1)} %cot_all.1, bf16[1,1280,640]{2,1,0:T(8,128)(2,1)} %w_in.1, ...), custom_call_target="tpu_custom_call" | custom-call | tf_op jit(solution)/shard_map/pallas_call | solution.py:919
  192.1 12.1 %shard_map.205 = (f32[1,5,640,640]{3,2,1,0:T(8,128)}, f32[1,640,1280]{2,1,0:T(8,128)}, f32[1,1280,640]{2,1,0:T(8,128)}, f32[1,1280]{1,0:T(1,128)}, f32[1,1280]{1...) custom-call(bf16[2,936,16,128]{3,2,1,0:T(8,128)(2,1)} %get-tuple-ele, ...), custom_call_target="tpu_custom_call" | custom-call | tf_op jit(solution)/shard_map/pallas_call | solution.py:965
